TPU v7x, 32 devices: a whole 2x2x4 slice. The times are simulated.
32 devices in a mesh: af: 4 (over z), gy: 4 (over x, core), gz: 2 (over y).
Axes of the slice: x: 2, y: 2, z: 4, core: 2. Of those that a mesh axis runs over, the one named last changes fastest.
Arguments:
- slab: bfloat16 [512, 16384], P('af', ('gy', 'gz')), may hold values from -4000 to 4000
- block_owner: int32 [4, 2, 4], P('gy', 'gz'), may hold values from 0 to 3, each once within a row
- basis_init: float32 [512, 128], replicated, may hold values from -0.25 to 0.25
Outputs:
- triangle: float32 [512, 512], replicated
- basis: float32 [512, 128], replicated
- core: bfloat16 [128, 16384], P(None, ('gy', 'gz', 'af'))
Inputs may be any that keep to these rules, and one draw needn't show every extreme that they name: For every gy and gz index, block_owner[gy, gz, :] is a permutation of the 4 af indices.
All inputs are finite; a program needn't handle non-finite values.
Results may differ from a plain program's by a relative error of at most 0.0049.
Values may be sent and summed in bfloat16 or wider, within the bound.
No kernel may reach another device: no remote copies, remote signals or barrier semaphores. Data moves between devices by JAX's collectives and lax.ppermute only.
A program may use at most 64 MiB of HBM per device.

v0:
```python
import functools

import jax
import jax.numpy as jnp
from jax import lax
from jax.experimental import pallas as pl
from jax.experimental.pallas import tpu as pltpu
from jax.sharding import PartitionSpec as P

ITERS = 2
GROUP = 16
HIGH = lax.Precision.HIGHEST


def split3(x):
    hi = x.astype(jnp.bfloat16)
    rest = x - hi.astype(jnp.float32)
    mid = rest.astype(jnp.bfloat16)
    low = (rest - mid.astype(jnp.float32)).astype(jnp.bfloat16)
    return hi, mid, low


def dot_nn(a, b):
    return lax.dot_general(a, b, (((1,), (0,)), ((), ())), precision=HIGH, preferred_element_type=jnp.float32)


def dot_nt(a, b):
    return lax.dot_general(a, b, (((1,), (1,)), ((), ())), precision=HIGH, preferred_element_type=jnp.float32)


def dot_tn(a, b):
    return lax.dot_general(a, b, (((0,), (0,)), ((), ())), precision=HIGH, preferred_element_type=jnp.float32)


def eliminate(state, start, n):
    rows = pl.ds(pl.multiple_of(start, GROUP), GROUP)
    left = state[rows, :n]
    right = state[rows, n:]
    shape = (GROUP, n)
    row = lax.broadcasted_iota(jnp.int32, shape, 0)
    lane = lax.broadcasted_iota(jnp.int32, shape, 1)
    cols = [
        jnp.take_along_axis(left, jnp.full(shape, 0, jnp.int32) + (start + k), axis=1, mode="promise_in_bounds")
        for k in range(GROUP)
    ]
    pivots = jnp.ones(shape, jnp.float32)
    for i in range(GROUP):
        pivot = jnp.broadcast_to(cols[i][i : i + 1, :], shape)
        pivots = jnp.where(row == i, pivot, pivots)
        if i == GROUP - 1:
            break
        inverse = 1.0 / pivot
        below = jnp.where(row > i, cols[i], 0.0)
        for k in range(i + 1, GROUP):
            cols[k] = cols[k] - (below * cols[k][i : i + 1, :]) * inverse
        factor = below * inverse
        left = left - factor * left[i : i + 1, :]
        right = right - factor * right[i : i + 1, :]
    scale = lax.rsqrt(pivots)
    left = left * scale
    right = right * scale
    state[rows, :n] = left
    state[rows, n:] = right
    hi, mid, low = split3(jnp.where(lane >= start + GROUP, left, 0.0))
    first = jnp.concatenate([hi, hi, mid, mid, hi, low], axis=0)
    wide = jnp.concatenate([left, right], axis=1)
    hi, mid, low = split3(wide)
    second = jnp.concatenate([hi, mid, hi, mid, low, hi], axis=0)
    delta = lax.dot_general(first, second, (((0,), (0,)), ((), ())), preferred_element_type=jnp.float32)
    state[...] = state[...] - delta


def factor_kernel(gram_ref, basis_ref, cols_ref, tri_ref, out_ref, core_ref, work, one, two):
    size = gram_ref.shape[0]
    n = basis_ref.shape[1]
    phases = size // n
    eye = (
        lax.broadcasted_iota(jnp.int32, (n, n), 0) == lax.broadcasted_iota(jnp.int32, (n, n), 1)
    ).astype(jnp.float32)
    upper = lax.broadcasted_iota(jnp.int32, (n, n), 0) <= lax.broadcasted_iota(jnp.int32, (n, n), 1)
    work[...] = gram_ref[...]
    tri_ref[...] = jnp.zeros_like(tri_ref)
    basis = basis_ref[...]
    for phase in range(max(phases, 2 * ITERS)):
        if phase < phases:
            at = slice(phase * n, (phase + 1) * n)
            rest = slice((phase + 1) * n, size)
            one[:, :n] = work[at, at]
            one[:, n:] = eye
        if phase < 2 * ITERS:
            if phase % 2 == 0:
                wide = dot_nn(gram_ref[...], basis)
                two[:, :n] = dot_tn(basis, wide)
            else:
                two[:, :n] = dot_tn(wide, wide)
            two[:, n:] = eye

        def step(group, carry):
            if phase < phases:
                eliminate(one, group * GROUP, n)
            if phase < 2 * ITERS:
                eliminate(two, group * GROUP, n)
            return carry

        lax.fori_loop(0, n // GROUP, step, 0)
        if phase < phases:
            tri_ref[at, at] = jnp.where(upper, one[:, :n], 0.0).T
            if phase < phases - 1:
                panel = dot_nn(one[:, n:], work[at, rest])
                tri_ref[rest, at] = panel.T
                work[rest, rest] = work[rest, rest] - dot_tn(panel, panel)
        if phase < 2 * ITERS:
            wide = dot_nt(wide, two[:, n:])
            if phase % 2 == 1:
                basis = wide
    out_ref[...] = basis
    narrow = basis.astype(jnp.bfloat16)
    core_ref[...] = lax.dot_general(
        narrow, cols_ref[...], (((0,), (0,)), ((), ())), preferred_element_type=jnp.float32
    ).astype(jnp.bfloat16)


def factor(gram, basis, columns):
    size = gram.shape[0]
    n = basis.shape[1]
    return pl.pallas_call(
        factor_kernel,
        out_shape=(
            jax.ShapeDtypeStruct((size, size), jnp.float32),
            jax.ShapeDtypeStruct((size, n), jnp.float32),
            jax.ShapeDtypeStruct((n, columns.shape[1]), jnp.bfloat16),
        ),
        scratch_shapes=[
            pltpu.VMEM((size, size), jnp.float32),
            pltpu.VMEM((n, 2 * n), jnp.float32),
            pltpu.VMEM((n, 2 * n), jnp.float32),
        ],
        compiler_params=pltpu.CompilerParams(vmem_limit_bytes=32 * 1024 * 1024),
        name="factor",
    )(gram, basis, columns)


def reduce_all(value):
    steps = []
    for axis in ("gy", "gz", "af"):
        distance = 1
        while distance < lax.axis_size(axis):
            steps.append((axis, distance))
            distance *= 2
    rows = value.shape[0]
    cuts = []
    for axis, distance in steps:
        bit = (lax.axis_index(axis) // distance) % 2
        half = value.shape[0] // 2
        kept = lax.dynamic_slice_in_dim(value, bit * half, half, 0)
        sent = lax.dynamic_slice_in_dim(value, (1 - bit) * half, half, 0)
        pairs = [(i, i ^ distance) for i in range(lax.axis_size(axis))]
        value = kept + lax.ppermute(sent, axis, pairs)
        cuts.append((axis, pairs, bit))
    for axis, pairs, bit in reversed(cuts):
        got = lax.ppermute(value, axis, pairs)
        value = jnp.where(
            bit == 0, jnp.concatenate([value, got], 0), jnp.concatenate([got, value], 0)
        )
    return value


def on_device(slab, block_owner, basis_init):
    fibers = lax.axis_size("af")
    local_rows = slab.shape[0]
    block_cols = slab.shape[1] // fibers
    owners = block_owner.reshape(fibers)
    labels = jnp.arange(fibers, dtype=jnp.int32)
    onehot = (owners[:, None] == labels[None, :]).astype(jnp.int32)
    source = jnp.sum(onehot * labels[:, None], axis=0)
    pieces = slab.reshape(local_rows, fibers, block_cols)
    arranged = jnp.take(pieces, source, axis=1)
    received = lax.all_to_all(arranged, "af", split_axis=1, concat_axis=0, tiled=True)
    columns = received.reshape(local_rows * fibers, block_cols)
    devices_all = fibers * lax.axis_size("gy") * lax.axis_size("gz")
    divisor = block_cols * devices_all
    gram_local = (
        lax.dot_general(
            columns, columns, (((1,), (1,)), ((), ())), preferred_element_type=jnp.float32
        )
        / divisor
    )
    summed = reduce_all(gram_local)
    return factor(summed, basis_init, columns)


def solution(mesh):
    placed = (P("af", ("gy", "gz")), P("gy", "gz", None), P())
    return jax.shard_map(
        on_device,
        mesh=mesh,
        in_specs=placed,
        out_specs=(P(), P(), P(None, ("gy", "gz", "af"))),
        check_vma=False,
    )
```

profile of v0, /device:TPU:0, one launch (start us, length us, event | category | flops | bytes accessed | tf_op | source)
XLA Modules:
  0.0 101.4 jit_solution(1158813990236246235)
XLA Ops:
  0.6 0.0 copy-start.1
  0.6 0.6 copy-done.1
  1.3 0.1 select_reduce_fusion
  1.4 1.3 %copy.8 = bf16[128,2048]{0,1:T(8,128)(2,1)S(1)} copy(bf16[128,2048]{1,0:T(8,128)(2,1)} %param.3) | data formatting | bytes 1048576 | tf_op args[0]
  2.7 0.2 copy.9
  2.9 0.6 gather_fusion
  3.5 0.9 select_bitcast_fusion
  4.4 6.3 %all-to-all-start = ((bf16[128,4,512]{2,0,1:T(8,128)(2,1)}), bf16[128,4,512]{2,0,1:T(8,128)(2,1)S(1)}, u32[]{:S(2)}, u32[]{:S(2)}) async-start(bf16[128,4,512]{2,0,1:T(8,128)(2,1)} %select_bitcast_fusion), calls=%async_computation | async-start | bytes 1048576 | tf_op jit(solution)/shard_map/all_to_all | solution.py:178
  10.8 14.5 %all-to-all-done = bf16[128,4,512]{2,0,1:T(8,128)(2,1)S(1)} async-done(((bf16[128,4,512]{2,0,1:T(8,128)(2,1)}), bf16[128,4,512]{2,0,1:T(8,128)(2,1)S(1)}, u32[]{:S(2)}, u32[]{:S(2)}) %all-to-all-start) | async-done | bytes 524320 | tf_op jit(solution)/shard_map/all_to_all | solution.py:178
  25.2 0.5 convolution_multiply_fusion
  25.8 0.1 collective-permute-start
  25.9 1.9 %collective-permute-done = f32[256,512]{1,0:T(8,128)S(1)} collective-permute-done((f32[256,512]{1,0:T(8,128)S(1)}, f32[256,512]{1,0:T(8,128)S(1)}, u32[]{:S(2)}, u32[]{:S(2)}) %collective-permute-start) | collective-permute-done | bytes 524320 | tf_op jit(solution)/shard_map/ppermute | solution.py:158
  27.8 0.1 dynamic-slice_add_fusion
  27.9 1.6 %collective-permute-start.1 = (f32[128,512]{1,0:T(8,128)S(1)}, f32[128,512]{1,0:T(8,128)S(1)}, u32[]{:S(2)}, u32[]{:S(2)}) collective-permute-start(f32[128,512]{1,0:T(8,128)S(1)} %constant_dynamic-slice_fusion.3), channel_id=1, source_target_pairs={{0,4},{2,6},{4,0},{6,2},{1,5},{3,7},{5,1},{7,3},{8,12},{10,14},{12... | collective-permute-start | bytes 786440 | tf_op jit(solution)/shard_map/ppermute | solution.py:158
  29.4 6.9 %collective-permute-done.1 = f32[128,512]{1,0:T(8,128)S(1)} collective-permute-done((f32[128,512]{1,0:T(8,128)S(1)}, f32[128,512]{1,0:T(8,128)S(1)}, u32[]{:S(2)}, u32[]{:S(2)}) %collective-permute-start.1) | collective-permute-done | bytes 262176 | tf_op jit(solution)/shard_map/ppermute | solution.py:158
  36.4 1.6 %collective-permute-start.2 = (f32[64,512]{1,0:T(8,128)S(1)}, f32[64,512]{1,0:T(8,128)S(1)}, u32[]{:S(2)}, u32[]{:S(2)}) collective-permute-start(f32[64,512]{1,0:T(8,128)S(1)} %constant_dynamic-slice_fusion.2), channel_id=1, source_target_pairs={{0,1},{1,0},{2,3},{3,2},{4,5},{5,4},{6,7},{7,6},{8,9},{9,8},{10,11... | collective-permute-start | bytes 393224 | tf_op jit(solution)/shard_map/ppermute | solution.py:158
  37.9 3.4 %collective-permute-done.2 = f32[64,512]{1,0:T(8,128)S(1)} collective-permute-done((f32[64,512]{1,0:T(8,128)S(1)}, f32[64,512]{1,0:T(8,128)S(1)}, u32[]{:S(2)}, u32[]{:S(2)}) %collective-permute-start.2) | collective-permute-done | bytes 131104 | tf_op jit(solution)/shard_map/ppermute | solution.py:158
  41.4 0.1 collective-permute-start.3
  41.6 4.2 %collective-permute-done.3 = f32[32,512]{1,0:T(8,128)S(1)} collective-permute-done((f32[32,512]{1,0:T(8,128)S(1)}, f32[32,512]{1,0:T(8,128)S(1)}, u32[]{:S(2)}, u32[]{:S(2)}) %collective-permute-start.3) | collective-permute-done | bytes 65568 | tf_op jit(solution)/shard_map/ppermute | solution.py:158
  45.8 0.1 collective-permute-start.4
  45.9 5.3 %collective-permute-done.4 = f32[16,512]{1,0:T(8,128)S(1)} collective-permute-done((f32[16,512]{1,0:T(8,128)S(1)}, f32[16,512]{1,0:T(8,128)S(1)}, u32[]{:S(2)}, u32[]{:S(2)}) %collective-permute-start.4) | collective-permute-done | bytes 32800 | tf_op jit(solution)/shard_map/ppermute | solution.py:158
  51.2 0.0 collective-permute-start.5
  51.2 4.8 %collective-permute-done.5 = f32[16,512]{1,0:T(8,128)S(1)} collective-permute-done((f32[16,512]{1,0:T(8,128)S(1)}, f32[16,512]{1,0:T(8,128)S(1)}, u32[]{:S(2)}, u32[]{:S(2)}) %collective-permute-start.5) | collective-permute-done | bytes 32800 | tf_op jit(solution)/shard_map/ppermute | solution.py:161
  56.0 0.1 collective-permute-start.6
  56.1 4.2 %collective-permute-done.6 = f32[32,512]{1,0:T(8,128)S(1)} collective-permute-done((f32[32,512]{1,0:T(8,128)S(1)}, f32[32,512]{1,0:T(8,128)S(1)}, u32[]{:S(2)}, u32[]{:S(2)}) %collective-permute-start.6) | collective-permute-done | bytes 65568 | tf_op jit(solution)/shard_map/ppermute | solution.py:161
  60.3 1.6 %collective-permute-start.7 = (f32[64,512]{1,0:T(8,128)S(1)}, f32[64,512]{1,0:T(8,128)S(1)}, u32[]{:S(2)}, u32[]{:S(2)}) collective-permute-start(f32[64,512]{1,0:T(8,128)S(1)} %maximum_select_fusion.3), channel_id=1, source_target_pairs={{0,1},{1,0},{2,3},{3,2},{4,5},{5,4},{6,7},{7,6},{8,9},{9,8},{10,11... | collective-permute-start | bytes 393224 | tf_op jit(solution)/shard_map/ppermute | solution.py:161
  61.9 3.4 %collective-permute-done.7 = f32[64,512]{1,0:T(8,128)S(1)} collective-permute-done((f32[64,512]{1,0:T(8,128)S(1)}, f32[64,512]{1,0:T(8,128)S(1)}, u32[]{:S(2)}, u32[]{:S(2)}) %collective-permute-start.7) | collective-permute-done | bytes 131104 | tf_op jit(solution)/shard_map/ppermute | solution.py:161
  65.4 1.6 %collective-permute-start.8 = (f32[128,512]{1,0:T(8,128)S(1)}, f32[128,512]{1,0:T(8,128)S(1)}, u32[]{:S(2)}, u32[]{:S(2)}) collective-permute-start(f32[128,512]{1,0:T(8,128)S(1)} %maximum_select_fusion.2), channel_id=1, source_target_pairs={{0,4},{2,6},{4,0},{6,2},{1,5},{3,7},{5,1},{7,3},{8,12},{10,14},{12... | collective-permute-start | bytes 786440 | tf_op jit(solution)/shard_map/ppermute | solution.py:161
  67.0 4.9 %collective-permute-done.8 = f32[128,512]{1,0:T(8,128)S(1)} collective-permute-done((f32[128,512]{1,0:T(8,128)S(1)}, f32[128,512]{1,0:T(8,128)S(1)}, u32[]{:S(2)}, u32[]{:S(2)}) %collective-permute-start.8) | collective-permute-done | bytes 262176 | tf_op jit(solution)/shard_map/ppermute | solution.py:161
  71.9 0.1 collective-permute-start.9
  72.0 0.0 copy-start
  72.0 1.9 %collective-permute-done.9 = f32[256,512]{1,0:T(8,128)S(1)} collective-permute-done((f32[256,512]{1,0:T(8,128)S(1)}, f32[256,512]{1,0:T(8,128)S(1)}, u32[]{:S(2)}, u32[]{:S(2)}) %collective-permute-start.9) | collective-permute-done | bytes 524320 | tf_op jit(solution)/shard_map/ppermute | solution.py:161
  73.9 0.1 maximum_select_fusion.gram_ref
  74.0 0.0 copy-done
  74.0 27.4 %factor.1 = (f32[512,512]{1,0:T(8,128)}, f32[512,128]{1,0:T(8,128)}, bf16[128,512]{1,0:T(8,128)(2,1)}) custom-call(f32[512,512]{1,0:T(8,128)S(1)} %maximum_select_fusion.gram_ref, f32[512,128]{1,0:T(8,128)S(1)} %copy-done, bf16[512,512]{1,0:T(8,128)(2,1)S(1)} %bitcast.16), custom_call_target="tpu_custom_call" | custom-call | tf_op jit(solution)/shard_map/factor/pallas_call | solution.py:126
  (16 shorter events, 0.3 us)
Async XLA Ops:
  0.6 0.7 copy-start.1
  4.4 20.8 %all-to-all-start = ((bf16[128,4,512]{2,0,1:T(8,128)(2,1)}), bf16[128,4,512]{2,0,1:T(8,128)(2,1)S(1)}, u32[]{:S(2)}, u32[]{:S(2)}) async-start(bf16[128,4,512]{2,0,1:T(8,128)(2,1)} %select_bitcast_fusion), calls=%async_computation | async-start | bytes 1048576 | tf_op jit(solution)/shard_map/all_to_all | solution.py:178
  25.8 2.0 %collective-permute-start = (f32[256,512]{1,0:T(8,128)S(1)}, f32[256,512]{1,0:T(8,128)S(1)}, u32[]{:S(2)}, u32[]{:S(2)}) collective-permute-start(f32[256,512]{1,0:T(8,128)S(1)} %constant_dynamic-slice_fusion.4), channel_id=1, source_target_pairs={{0,2},{2,0},{4,6},{6,4},{1,3},{3,1},{5,7},{7,5},{8,10},{10,8},{12,... | collective-permute-start | bytes 1572872 | tf_op jit(solution)/shard_map/ppermute | solution.py:158
  27.9 8.4 %collective-permute-start.1 = (f32[128,512]{1,0:T(8,128)S(1)}, f32[128,512]{1,0:T(8,128)S(1)}, u32[]{:S(2)}, u32[]{:S(2)}) collective-permute-start(f32[128,512]{1,0:T(8,128)S(1)} %constant_dynamic-slice_fusion.3), channel_id=1, source_target_pairs={{0,4},{2,6},{4,0},{6,2},{1,5},{3,7},{5,1},{7,3},{8,12},{10,14},{12... | collective-permute-start | bytes 786440 | tf_op jit(solution)/shard_map/ppermute | solution.py:158
  36.4 5.0 %collective-permute-start.2 = (f32[64,512]{1,0:T(8,128)S(1)}, f32[64,512]{1,0:T(8,128)S(1)}, u32[]{:S(2)}, u32[]{:S(2)}) collective-permute-start(f32[64,512]{1,0:T(8,128)S(1)} %constant_dynamic-slice_fusion.2), channel_id=1, source_target_pairs={{0,1},{1,0},{2,3},{3,2},{4,5},{5,4},{6,7},{7,6},{8,9},{9,8},{10,11... | collective-permute-start | bytes 393224 | tf_op jit(solution)/shard_map/ppermute | solution.py:158
  41.4 4.3 %collective-permute-start.3 = (f32[32,512]{1,0:T(8,128)S(1)}, f32[32,512]{1,0:T(8,128)S(1)}, u32[]{:S(2)}, u32[]{:S(2)}) collective-permute-start(f32[32,512]{1,0:T(8,128)S(1)} %constant_dynamic-slice_fusion.1), channel_id=1, source_target_pairs={{0,8},{8,0},{16,24},{24,16},{1,9},{9,1},{17,25},{25,17},{2,10},{10... | collective-permute-start | bytes 196616 | tf_op jit(solution)/shard_map/ppermute | solution.py:158
  45.8 5.4 %collective-permute-start.4 = (f32[16,512]{1,0:T(8,128)S(1)}, f32[16,512]{1,0:T(8,128)S(1)}, u32[]{:S(2)}, u32[]{:S(2)}) collective-permute-start(f32[16,512]{1,0:T(8,128)S(1)} %constant_dynamic-slice_fusion), channel_id=1, source_target_pairs={{0,16},{8,24},{16,0},{24,8},{1,17},{9,25},{17,1},{25,9},{2,18},{10... | collective-permute-start | bytes 98312 | tf_op jit(solution)/shard_map/ppermute | solution.py:158
  51.2 4.8 %collective-permute-start.5 = (f32[16,512]{1,0:T(8,128)S(1)}, f32[16,512]{1,0:T(8,128)S(1)}, u32[]{:S(2)}, u32[]{:S(2)}) collective-permute-start(f32[16,512]{1,0:T(8,128)S(1)} %dynamic-slice_add_fusion.4), channel_id=1, source_target_pairs={{0,16},{8,24},{16,0},{24,8},{1,17},{9,25},{17,1},{25,9},{2,18},{10... | collective-permute-start | bytes 98312 | tf_op jit(solution)/shard_map/ppermute | solution.py:161
  56.0 4.3 %collective-permute-start.6 = (f32[32,512]{1,0:T(8,128)S(1)}, f32[32,512]{1,0:T(8,128)S(1)}, u32[]{:S(2)}, u32[]{:S(2)}) collective-permute-start(f32[32,512]{1,0:T(8,128)S(1)} %maximum_select_fusion.4), channel_id=1, source_target_pairs={{0,8},{8,0},{16,24},{24,16},{1,9},{9,1},{17,25},{25,17},{2,10},{10... | collective-permute-start | bytes 196616 | tf_op jit(solution)/shard_map/ppermute | solution.py:161
  60.3 5.0 %collective-permute-start.7 = (f32[64,512]{1,0:T(8,128)S(1)}, f32[64,512]{1,0:T(8,128)S(1)}, u32[]{:S(2)}, u32[]{:S(2)}) collective-permute-start(f32[64,512]{1,0:T(8,128)S(1)} %maximum_select_fusion.3), channel_id=1, source_target_pairs={{0,1},{1,0},{2,3},{3,2},{4,5},{5,4},{6,7},{7,6},{8,9},{9,8},{10,11... | collective-permute-start | bytes 393224 | tf_op jit(solution)/shard_map/ppermute | solution.py:161
  65.4 6.4 %collective-permute-start.8 = (f32[128,512]{1,0:T(8,128)S(1)}, f32[128,512]{1,0:T(8,128)S(1)}, u32[]{:S(2)}, u32[]{:S(2)}) collective-permute-start(f32[128,512]{1,0:T(8,128)S(1)} %maximum_select_fusion.2), channel_id=1, source_target_pairs={{0,4},{2,6},{4,0},{6,2},{1,5},{3,7},{5,1},{7,3},{8,12},{10,14},{12... | collective-permute-start | bytes 786440 | tf_op jit(solution)/shard_map/ppermute | solution.py:161
  71.9 2.0 %collective-permute-start.9 = (f32[256,512]{1,0:T(8,128)S(1)}, f32[256,512]{1,0:T(8,128)S(1)}, u32[]{:S(2)}, u32[]{:S(2)}) collective-permute-start(f32[256,512]{1,0:T(8,128)S(1)} %maximum_select_fusion.1), channel_id=1, source_target_pairs={{0,2},{2,0},{4,6},{6,4},{1,3},{3,1},{5,7},{7,5},{8,10},{10,8},{12,... | collective-permute-start | bytes 1572872 | tf_op jit(solution)/shard_map/ppermute | solution.py:161
  72.0 2.0 %copy-start = (f32[512,128]{1,0:T(8,128)S(1)}, f32[512,128]{1,0:T(8,128)}, u32[]{:S(2)}) copy-start(f32[512,128]{1,0:T(8,128)} %basis_ref.1) | copy-start | bytes 786436
where the time goes:
time: 102 us; the launch traced here: 101 us
  waiting for transfers between devices  55.4 us (54%)
  Pallas kernels  27.4 us (27%)
  starting transfers between devices  13 us (13%)
  local copies, waits for them, and re-layouts  2.88 us (3%)
  other arithmetic  1.37 us (1%)
    pallas_call x1, Pallas kernels, factor(): pl.pallas_call(factor_kernel, out_shape=(jax.ShapeDtypeStruct((size, size...  27.4 us
    ppermute x5, waiting for transfers between devices, reduce_all(): value = kept + lax.ppermute(sent, axis, pairs)  21.6 us
    ppermute x5, waiting for transfers between devices, reduce_all(): got = lax.ppermute(value, axis, pairs)  19.3 us
    all_to_all x1, waiting for transfers between devices, on_device(): lax.all_to_all(arranged, 'af', split_axis=1, concat_axis=0, tiled=True)  14.5 us
    all_to_all x1, starting transfers between devices, on_device(): lax.all_to_all(arranged, 'af', split_axis=1, concat_axis=0, tiled=True)  6.32 us
    ppermute x5, starting transfers between devices, reduce_all(): value = kept + lax.ppermute(sent, axis, pairs)  3.36 us
    ppermute x5, starting transfers between devices, reduce_all(): got = lax.ppermute(value, axis, pairs)  3.29 us
  transfers between devices with their start and end apart: 11, of which 11 were waited for; matrix products, arithmetic and copies ran while one was open for 0% of the time, Pallas kernels for 0%

commit v1 on v0

--- a/solution.py
+++ b/solution.py
@@ -2,6 +2,7 @@
 
 import jax
 import jax.numpy as jnp
+import numpy as np
 from jax import lax
 from jax.experimental import pallas as pl
 from jax.experimental.pallas import tpu as pltpu
@@ -70,9 +71,50 @@
     state[...] = state[...] - delta
 
 
-def factor_kernel(gram_ref, basis_ref, cols_ref, tri_ref, out_ref, core_ref, work, one, two):
-    size = gram_ref.shape[0]
+def upper_blocks(size, n):
+    count = size // n
+    return [(i, j) for i in range(count) for j in range(i, count)]
+
+
+def gram_kernel(divisor, n, place_ref, *refs):
+    pieces, (columns_ref, gram_ref) = refs[:-2], refs[-2:]
+    rows = pieces[0].shape[0]
+    for distance, piece in enumerate(pieces):
+        start = pl.multiple_of(lax.bitwise_xor(place_ref[0], distance) * rows, rows)
+        columns_ref[pl.ds(start, rows), :] = piece[...]
+    for b, (i, j) in enumerate(upper_blocks(columns_ref.shape[0], n)):
+        gram_ref[b * n : (b + 1) * n, :] = lax.dot_general(
+            columns_ref[i * n : (i + 1) * n, :],
+            columns_ref[j * n : (j + 1) * n, :],
+            (((1,), (1,)), ((), ())),
+            preferred_element_type=jnp.float32,
+        ) * (1.0 / divisor)
+
+
+def local_gram(place, pieces, divisor, n):
+    rows, width = pieces[0].shape
+    size = rows * len(pieces)
+    vmem = pl.BlockSpec(memory_space=pltpu.VMEM)
+    return pl.pallas_call(
+        functools.partial(gram_kernel, divisor, n),
+        out_shape=(
+            jax.ShapeDtypeStruct((size, width), pieces[0].dtype),
+            jax.ShapeDtypeStruct((len(upper_blocks(size, n)) * n, n), jnp.float32),
+        ),
+        in_specs=[pl.BlockSpec(memory_space=pltpu.SMEM)] + [vmem] * len(pieces),
+        out_specs=(vmem, vmem),
+        name="local_gram",
+    )(place.reshape(1), *pieces)
+
+
+def factor_kernel(blocks_ref, basis_ref, cols_ref, tri_ref, out_ref, core_ref, gram_ref, work, one, two):
+    size = tri_ref.shape[0]
     n = basis_ref.shape[1]
+    for b, (i, j) in enumerate(upper_blocks(size, n)):
+        block = blocks_ref[b * n : (b + 1) * n, :]
+        gram_ref[i * n : (i + 1) * n, j * n : (j + 1) * n] = block
+        if i != j:
+            gram_ref[j * n : (j + 1) * n, i * n : (i + 1) * n] = block.T
     phases = size // n
     eye = (
         lax.broadcasted_iota(jnp.int32, (n, n), 0) == lax.broadcasted_iota(jnp.int32, (n, n), 1)
@@ -120,9 +162,8 @@
     ).astype(jnp.bfloat16)
 
 
-def factor(gram, basis, columns):
-    size = gram.shape[0]
-    n = basis.shape[1]
+def factor(blocks, basis, columns):
+    size, n = basis.shape
     return pl.pallas_call(
         factor_kernel,
         out_shape=(
@@ -132,61 +173,88 @@
         ),
         scratch_shapes=[
             pltpu.VMEM((size, size), jnp.float32),
+            pltpu.VMEM((size, size), jnp.float32),
             pltpu.VMEM((n, 2 * n), jnp.float32),
             pltpu.VMEM((n, 2 * n), jnp.float32),
         ],
         compiler_params=pltpu.CompilerParams(vmem_limit_bytes=32 * 1024 * 1024),
         name="factor",
-    )(gram, basis, columns)
+    )(blocks, basis, columns)
+
+
+class Group:
+    def __init__(self, bits):
+        self.axes = tuple(dict.fromkeys(axis for axis, _ in bits))
+        self.bits = bits
+        self.size = 2 ** len(bits)
+        self.me = 0
+        for b, (axis, distance) in enumerate(bits):
+            self.me = self.me + (((lax.axis_index(axis) // distance) % 2) << b)
+
+    def swap(self, value, change):
+        sizes = [lax.axis_size(axis) for axis in self.axes]
+        pairs = []
+        for source, place in enumerate(np.ndindex(*sizes)):
+            place = list(place)
+            for b, (axis, distance) in enumerate(self.bits):
+                if (change >> b) & 1:
+                    place[self.axes.index(axis)] ^= distance
+            pairs.append((source, int(np.ravel_multi_index(place, sizes))))
+        return lax.ppermute(value, self.axes, pairs)
+
+    def scatter_sum(self, value):
+        part = value.shape[0] // self.size
+        got = [
+            self.swap(lax.dynamic_slice_in_dim(value, (self.me ^ d) * part, part, 0), d)
+            for d in range(1, self.size)
+        ]
+        return sum(got, lax.dynamic_slice_in_dim(value, self.me * part, part, 0))
+
+    def gather(self, value):
+        got = [value] + [self.swap(value, d) for d in range(1, self.size)]
+        whole = jnp.zeros((self.size, *value.shape), value.dtype)
+        for d in range(self.size):
+            whole = lax.dynamic_update_slice_in_dim(whole, got[d][None], self.me ^ d, 0)
+        return whole.reshape(self.size * value.shape[0], *value.shape[1:])
+
+
+def axis_bits(axis):
+    size = lax.axis_size(axis)
+    assert size & (size - 1) == 0, axis
+    return [(axis, 1 << b) for b in range(size.bit_length() - 1)]
 
 
 def reduce_all(value):
-    steps = []
-    for axis in ("gy", "gz", "af"):
-        distance = 1
-        while distance < lax.axis_size(axis):
-            steps.append((axis, distance))
-            distance *= 2
-    rows = value.shape[0]
-    cuts = []
-    for axis, distance in steps:
-        bit = (lax.axis_index(axis) // distance) % 2
-        half = value.shape[0] // 2
-        kept = lax.dynamic_slice_in_dim(value, bit * half, half, 0)
-        sent = lax.dynamic_slice_in_dim(value, (1 - bit) * half, half, 0)
-        pairs = [(i, i ^ distance) for i in range(lax.axis_size(axis))]
-        value = kept + lax.ppermute(sent, axis, pairs)
-        cuts.append((axis, pairs, bit))
-    for axis, pairs, bit in reversed(cuts):
-        got = lax.ppermute(value, axis, pairs)
-        value = jnp.where(
-            bit == 0, jnp.concatenate([value, got], 0), jnp.concatenate([got, value], 0)
-        )
+    first, *rest = axis_bits("gy") + axis_bits("gz")
+    groups = [Group([first])] + [Group(rest[b : b + 2]) for b in range(0, len(rest), 2)]
+    for group in groups:
+        value = group.scatter_sum(value)
+    for bit in axis_bits("af"):
+        value = value + Group([bit]).swap(value, 1)
+    for group in reversed(groups):
+        value = group.gather(value)
     return value
 
 
 def on_device(slab, block_owner, basis_init):
     fibers = lax.axis_size("af")
-    local_rows = slab.shape[0]
     block_cols = slab.shape[1] // fibers
     owners = block_owner.reshape(fibers)
     labels = jnp.arange(fibers, dtype=jnp.int32)
     onehot = (owners[:, None] == labels[None, :]).astype(jnp.int32)
     source = jnp.sum(onehot * labels[:, None], axis=0)
-    pieces = slab.reshape(local_rows, fibers, block_cols)
-    arranged = jnp.take(pieces, source, axis=1)
-    received = lax.all_to_all(arranged, "af", split_axis=1, concat_axis=0, tiled=True)
-    columns = received.reshape(local_rows * fibers, block_cols)
+    along = Group(axis_bits("af"))
+
+    def block_of(distance):
+        start = source[along.me ^ distance] * block_cols
+        return lax.dynamic_slice_in_dim(slab, start, block_cols, 1)
+
+    pieces = [block_of(0)]
+    for distance in range(1, fibers):
+        pieces.append(along.swap(block_of(distance), distance))
     devices_all = fibers * lax.axis_size("gy") * lax.axis_size("gz")
-    divisor = block_cols * devices_all
-    gram_local = (
-        lax.dot_general(
-            columns, columns, (((1,), (1,)), ((), ())), preferred_element_type=jnp.float32
-        )
-        / divisor
-    )
-    summed = reduce_all(gram_local)
-    return factor(summed, basis_init, columns)
+    columns, blocks = local_gram(along.me, pieces, block_cols * devices_all, basis_init.shape[1])
+    return factor(reduce_all(blocks), basis_init, columns)
 
 
 def solution(mesh):

time: 102 us -> 84.4 us (0.83)
  waiting for transfers between devices: 55.4 us -> 31.6 us
  between operations: 0.94 us -> 3.51 us
  Pallas kernels: 27.4 us -> 29.9 us
  local copies, waits for them, and re-layouts: 2.88 us -> 5 us
  other arithmetic: 1.37 us -> 0.17 us
    all_to_all x1 -> x0, waiting for transfers between devices: 14.5 us -> none  [on_device(): lax.all_to_all(arranged, 'af', split_axis=1, concat_axis=0, tiled=True)]
    ppermute x10 -> x13, waiting for transfers between devices: 40.9 us -> 31.6 us  [swap(): return lax.ppermute(value, self.axes, pairs)]
    ppermute x10 -> x13, starting transfers between devices: 6.64 us -> 14 us  [swap(): return lax.ppermute(value, self.axes, pairs)]
    all_to_all x1 -> x0, starting transfers between devices: 6.32 us -> none  [on_device(): lax.all_to_all(arranged, 'af', split_axis=1, concat_axis=0, tiled=True)]
    dynamic_slice x5 -> x4, local copies, waits for them, and re-layouts: 0.12 us -> 3.53 us  [the longest x1 1.81 us: block_of(): return lax.dynamic_slice_in_dim(slab, start, block_cols, 1)]
    pallas_call x0 -> x1, Pallas kernels: none -> 2.47 us  [local_gram(): pl.pallas_call(functools.partial(gram_kernel, divisor, n), out_shape=(jax...]
    select_n x7 -> x0, other arithmetic: 1.12 us -> none  [the longest x2 0.91 us: on_device(): arranged = jnp.take(pieces, source, axis=1)]
  transfers between devices with their start and end apart: 11 -> 13, of which waited for: 11 -> 13; matrix products, arithmetic and copies ran while one was open for 0% -> 0% of each run, Pallas kernels for 0% -> 0%
where the time goes in v1:
time: 84.4 us; the launch traced here: 84.1 us
  waiting for transfers between devices  31.6 us (37%)
  Pallas kernels  29.9 us (35%)
  starting transfers between devices  14 us (17%)
  local copies, waits for them, and re-layouts  5 us (6%)
  between operations  3.51 us (4%)
    ppermute x13, waiting for transfers between devices, swap(): return lax.ppermute(value, self.axes, pairs)  31.6 us
    pallas_call x1, Pallas kernels, factor(): pl.pallas_call(factor_kernel, out_shape=(jax.ShapeDtypeStruct((size, size...  27.4 us
    ppermute x13, starting transfers between devices, swap(): return lax.ppermute(value, self.axes, pairs)  14 us
    pallas_call x1, Pallas kernels, local_gram(): pl.pallas_call(functools.partial(gram_kernel, divisor, n), out_shape=(jax...  2.47 us
    dynamic_slice x1, local copies, waits for them, and re-layouts, block_of(): return lax.dynamic_slice_in_dim(slab, start, block_cols, 1)  1.81 us
  transfers between devices with their start and end apart: 13, of which 13 were waited for; matrix products, arithmetic and copies ran while one was open for 0% of the time, Pallas kernels for 0%

profile of v1, /device:TPU:0, one launch (start us, length us, event | category | flops | bytes accessed | tf_op | source)
XLA Modules:
  0.0 84.1 jit_solution(7624723975827378165)
XLA Ops:
  0.7 0.0 copy-start.6
  0.7 0.6 copy-done.6
  1.3 0.1 select_reduce_fusion
  1.4 0.6 fusion
  4.6 1.8 %constant_dynamic-slice_fusion.4 = (bf16[128,512]{1,0:T(8,128)(2,1)S(1)}, bf16[128,512]{1,0:T(8,128)(2,1)S(1)}, bf16[128,512]{1,0:T(8,128)(2,1)}, bf16[128,512]{1,0:T(8,128)(2,1)S(1)}) fusion(bf16[128,2048]{1,0:T(8,128)(2,1)} %param.3, s32[]{:T(128)S(6)} %select_n.103, s32[]{:T(128)S(6)} %select_n.99, s32[]{:T(128)S(6)} %select_n.97, s32[]{:T(128)S(6)} %select_n.101), kind=kLoop, calls=%fused_computation.12 | loop fusion | bytes 1048592 | tf_op jit(solution)/shard_map/dynamic_slice | solution.py:250
  6.5 5.0 %collective-permute-start.2 = (bf16[128,512]{1,0:T(8,128)(2,1)S(1)}, bf16[128,512]{1,0:T(8,128)(2,1)S(1)}, u32[]{:S(2)}, u32[]{:S(2)}) collective-permute-start(bf16[128,512]{1,0:T(8,128)(2,1)S(1)} %get-tuple-element.9), channel_id=1, source_target_pairs={{0,24},{8,16},{16,8},{24,0},{1,25},{9,17},{17,9},{25,1},{2,26},{10... | collective-permute-start | bytes 393224 | tf_op jit(solution)/shard_map/ppermute | solution.py:203
  11.5 0.0 collective-permute-start
  11.5 0.6 collective-permute-start.1
  12.1 3.8 %collective-permute-done.2.refs_3_ = bf16[128,512]{1,0:T(8,128)(2,1)S(1)} collective-permute-done((bf16[128,512]{1,0:T(8,128)(2,1)S(1)}, bf16[128,512]{1,0:T(8,128)(2,1)S(1)}, u32[]{:S(2)}, u32[]{:S(2)}) %collective-permute-start.2) | collective-permute-done | bytes 131104 | tf_op jit(solution)/shard_map/ppermute | solution.py:203
  15.9 0.0 copy-start.3
  15.9 3.0 %collective-permute-done.refs_1_ = bf16[128,512]{1,0:T(8,128)(2,1)S(1)} collective-permute-done((bf16[128,512]{1,0:T(8,128)(2,1)S(1)}, bf16[128,512]{1,0:T(8,128)(2,1)S(1)}, u32[]{:S(2)}, u32[]{:S(2)}) %collective-permute-start) | collective-permute-done | bytes 131104 | tf_op jit(solution)/shard_map/ppermute | solution.py:203
  18.9 0.0 copy-start.4
  18.9 3.7 %collective-permute-done.1.refs_2_ = bf16[128,512]{1,0:T(8,128)(2,1)S(1)} collective-permute-done((bf16[128,512]{1,0:T(8,128)(2,1)S(1)}, bf16[128,512]{1,0:T(8,128)(2,1)S(1)}, u32[]{:S(2)}, u32[]{:S(2)}) %collective-permute-start.1) | collective-permute-done | bytes 131104 | tf_op jit(solution)/shard_map/ppermute | solution.py:203
  22.6 0.0 copy-start.5
  22.6 0.0 copy-done.3
  22.6 0.0 copy-done.4
  22.6 0.6 copy-done.5
  23.2 2.5 %local_gram.1 = (bf16[512,512]{1,0:T(8,128)(2,1)}, f32[1280,128]{1,0:T(8,128)}) custom-call(s32[1]{0:T(128)} %bitcast.place_ref, bf16[128,512]{1,0:T(8,128)(2,1)} %get-tuple-element.11.refs_0_, bf16[128,512]{1,0:T(8,128)(2,1)} %copy-done.4, bf16[128,512]{1,0:T(8,128)(2,1)} %copy-done.5, bf16[128,512]{1,0:T(8,128)(2,1)} %copy-done.3), custom_call_target="tpu_custom_call" | custom-call | tf_op jit(solution)/shard_map/local_gram/pallas_call | solution.py:98
  25.7 0.0 copy-start.2
  25.7 1.1 %constant_dynamic-slice_fusion.3 = f32[640,128]{1,0:T(8,128)S(1)} fusion(f32[1280,128]{1,0:T(8,128)} %get-tuple-element.5, s32[]{:T(128)S(6)} %select_n.106), kind=kLoop, calls=%fused_computation.11 | loop fusion | bytes 655364 | tf_op jit(solution)/shard_map/dynamic_slice | solution.py:208
  26.8 0.1 collective-permute-start.3
  26.9 1.5 %collective-permute-done.3 = f32[640,128]{1,0:T(8,128)S(1)} collective-permute-done((f32[640,128]{1,0:T(8,128)S(1)}, f32[640,128]{1,0:T(8,128)S(1)}, u32[]{:S(2)}, u32[]{:S(2)}) %collective-permute-start.3) | collective-permute-done | bytes 327712 | tf_op jit(solution)/shard_map/ppermute | solution.py:203
  28.5 0.0 copy-done.2
  28.5 1.6 %collective-permute-start.4 = (f32[160,128]{1,0:T(8,128)S(1)}, f32[160,128]{1,0:T(8,128)S(1)}, u32[]{:S(2)}, u32[]{:S(2)}) collective-permute-start(f32[160,128]{1,0:T(8,128)S(1)} %get-tuple-element.13), channel_id=1, source_target_pairs={{0,4},{1,5},{2,6},{3,7},{4,0},{5,1},{6,2},{7,3},{8,12},{9,13},{10,... | collective-permute-start | bytes 245768 | tf_op jit(solution)/shard_map/ppermute | solution.py:203
  30.1 1.5 %collective-permute-start.6 = (f32[160,128]{1,0:T(8,128)S(1)}, f32[160,128]{1,0:T(8,128)S(1)}, u32[]{:S(2)}, u32[]{:S(2)}) collective-permute-start(f32[160,128]{1,0:T(8,128)S(1)} %get-tuple-element.14), channel_id=1, source_target_pairs={{0,5},{1,4},{2,7},{3,6},{4,1},{5,0},{6,3},{7,2},{8,13},{9,12},{10,... | collective-permute-start | bytes 245768 | tf_op jit(solution)/shard_map/ppermute | solution.py:203
  31.6 0.5 collective-permute-start.5
  32.1 1.0 %collective-permute-done.4 = f32[160,128]{1,0:T(8,128)S(1)} collective-permute-done((f32[160,128]{1,0:T(8,128)S(1)}, f32[160,128]{1,0:T(8,128)S(1)}, u32[]{:S(2)}, u32[]{:S(2)}) %collective-permute-start.4) | collective-permute-done | bytes 81952 | tf_op jit(solution)/shard_map/ppermute | solution.py:203
  33.1 2.8 %collective-permute-done.6 = f32[160,128]{1,0:T(8,128)S(1)} collective-permute-done((f32[160,128]{1,0:T(8,128)S(1)}, f32[160,128]{1,0:T(8,128)S(1)}, u32[]{:S(2)}, u32[]{:S(2)}) %collective-permute-start.6) | collective-permute-done | bytes 81952 | tf_op jit(solution)/shard_map/ppermute | solution.py:203
  35.9 1.2 %collective-permute-done.5 = f32[160,128]{1,0:T(8,128)S(1)} collective-permute-done((f32[160,128]{1,0:T(8,128)S(1)}, f32[160,128]{1,0:T(8,128)S(1)}, u32[]{:S(2)}, u32[]{:S(2)}) %collective-permute-start.5) | collective-permute-done | bytes 81952 | tf_op jit(solution)/shard_map/ppermute | solution.py:203
  37.1 0.1 collective-permute-start.7
  37.2 4.4 %collective-permute-done.7 = f32[160,128]{1,0:T(8,128)S(1)} collective-permute-done((f32[160,128]{1,0:T(8,128)S(1)}, f32[160,128]{1,0:T(8,128)S(1)}, u32[]{:S(2)}, u32[]{:S(2)}) %collective-permute-start.7) | collective-permute-done | bytes 81952 | tf_op jit(solution)/shard_map/ppermute | solution.py:203
  41.7 1.1 %collective-permute-start.8 = (f32[160,128]{1,0:T(8,128)S(1)}, f32[160,128]{1,0:T(8,128)S(1)}, u32[]{:S(2)}, u32[]{:S(2)}) collective-permute-start(f32[160,128]{1,0:T(8,128)S(1)} %add.130), channel_id=1, source_target_pairs={{0,16},{8,24},{16,0},{24,8},{1,17},{9,25},{17,1},{25,9},{2,18},{10... | collective-permute-start | bytes 245768 | tf_op jit(solution)/shard_map/ppermute | solution.py:203
  42.7 4.8 %collective-permute-done.8 = f32[160,128]{1,0:T(8,128)S(1)} collective-permute-done((f32[160,128]{1,0:T(8,128)S(1)}, f32[160,128]{1,0:T(8,128)S(1)}, u32[]{:S(2)}, u32[]{:S(2)}) %collective-permute-start.8) | collective-permute-done | bytes 81952 | tf_op jit(solution)/shard_map/ppermute | solution.py:203
  47.6 1.5 %collective-permute-start.9 = (f32[160,128]{1,0:T(8,128)S(1)}, f32[160,128]{1,0:T(8,128)S(1)}, u32[]{:S(2)}, u32[]{:S(2)}) collective-permute-start(f32[160,128]{1,0:T(8,128)S(1)} %get-tuple-element.8), channel_id=1, source_target_pairs={{0,4},{1,5},{2,6},{3,7},{4,0},{5,1},{6,2},{7,3},{8,12},{9,13},{10,... | collective-permute-start | bytes 245768 | tf_op jit(solution)/shard_map/ppermute | solution.py:203
  49.0 0.6 collective-permute-start.10
  49.6 1.5 %collective-permute-start.11 = (f32[160,128]{1,0:T(8,128)S(1)}, f32[160,128]{1,0:T(8,128)S(1)}, u32[]{:S(2)}, u32[]{:S(2)}) collective-permute-start(f32[160,128]{1,0:T(8,128)S(1)} %get-tuple-element.8), channel_id=1, source_target_pairs={{0,5},{1,4},{2,7},{3,6},{4,1},{5,0},{6,3},{7,2},{8,13},{9,12},{10,... | collective-permute-start | bytes 245768 | tf_op jit(solution)/shard_map/ppermute | solution.py:203
  51.1 1.0 %collective-permute-done.9 = f32[160,128]{1,0:T(8,128)S(1)} collective-permute-done((f32[160,128]{1,0:T(8,128)S(1)}, f32[160,128]{1,0:T(8,128)S(1)}, u32[]{:S(2)}, u32[]{:S(2)}) %collective-permute-start.9) | collective-permute-done | bytes 81952 | tf_op jit(solution)/shard_map/ppermute | solution.py:203
  52.1 1.4 %collective-permute-done.10 = f32[160,128]{1,0:T(8,128)S(1)} collective-permute-done((f32[160,128]{1,0:T(8,128)S(1)}, f32[160,128]{1,0:T(8,128)S(1)}, u32[]{:S(2)}, u32[]{:S(2)}) %collective-permute-start.10) | collective-permute-done | bytes 81952 | tf_op jit(solution)/shard_map/ppermute | solution.py:203
  53.5 1.5 %collective-permute-done.11 = f32[160,128]{1,0:T(8,128)S(1)} collective-permute-done((f32[160,128]{1,0:T(8,128)S(1)}, f32[160,128]{1,0:T(8,128)S(1)}, u32[]{:S(2)}, u32[]{:S(2)}) %collective-permute-start.11) | collective-permute-done | bytes 81952 | tf_op jit(solution)/shard_map/ppermute | solution.py:203
  55.0 0.1 collective-permute-start.12
  55.1 0.0 copy-start
  55.2 0.0 copy-start.1
  55.2 1.5 %collective-permute-done.12 = f32[640,128]{1,0:T(8,128)S(1)} collective-permute-done((f32[640,128]{1,0:T(8,128)S(1)}, f32[640,128]{1,0:T(8,128)S(1)}, u32[]{:S(2)}, u32[]{:S(2)}) %collective-permute-start.12) | collective-permute-done | bytes 327712 | tf_op jit(solution)/shard_map/ppermute | solution.py:203
  56.7 0.0 copy-done
  56.7 0.0 copy-done.1
  56.7 27.4 %factor.1 = (f32[512,512]{1,0:T(8,128)}, f32[512,128]{1,0:T(8,128)}, bf16[128,512]{1,0:T(8,128)(2,1)}) custom-call(f32[1280,128]{1,0:T(8,128)S(1)} %bitcast.21, f32[512,128]{1,0:T(8,128)S(1)} %copy-done.1, bf16[512,512]{1,0:T(8,128)(2,1)S(1)} %copy-done), custom_call_target="tpu_custom_call" | custom-call | tf_op jit(solution)/shard_map/factor/pallas_call | solution.py:167
  (12 shorter events, 0.3 us)
Async XLA Ops:
  0.7 0.7 copy-start.6
  6.5 9.4 %collective-permute-start.2 = (bf16[128,512]{1,0:T(8,128)(2,1)S(1)}, bf16[128,512]{1,0:T(8,128)(2,1)S(1)}, u32[]{:S(2)}, u32[]{:S(2)}) collective-permute-start(bf16[128,512]{1,0:T(8,128)(2,1)S(1)} %get-tuple-element.9), channel_id=1, source_target_pairs={{0,24},{8,16},{16,8},{24,0},{1,25},{9,17},{17,9},{25,1},{2,26},{10... | collective-permute-start | bytes 393224 | tf_op jit(solution)/shard_map/ppermute | solution.py:203
  11.5 7.4 %collective-permute-start = (bf16[128,512]{1,0:T(8,128)(2,1)S(1)}, bf16[128,512]{1,0:T(8,128)(2,1)S(1)}, u32[]{:S(2)}, u32[]{:S(2)}) collective-permute-start(bf16[128,512]{1,0:T(8,128)(2,1)S(1)} %get-tuple-element.10), channel_id=1, source_target_pairs={{0,8},{8,0},{16,24},{24,16},{1,9},{9,1},{17,25},{25,17},{2,10},{10... | collective-permute-start | bytes 393224 | tf_op jit(solution)/shard_map/ppermute | solution.py:203
  11.5 11.1 %collective-permute-start.1 = (bf16[128,512]{1,0:T(8,128)(2,1)S(1)}, bf16[128,512]{1,0:T(8,128)(2,1)S(1)}, u32[]{:S(2)}, u32[]{:S(2)}) collective-permute-start(bf16[128,512]{1,0:T(8,128)(2,1)S(1)} %get-tuple-element.12), channel_id=1, source_target_pairs={{0,16},{8,24},{16,0},{24,8},{1,17},{9,25},{17,1},{25,9},{2,18},{10... | collective-permute-start | bytes 393224 | tf_op jit(solution)/shard_map/ppermute | solution.py:203
  15.9 6.7 %copy-start.3 = (bf16[128,512]{1,0:T(8,128)(2,1)}, bf16[128,512]{1,0:T(8,128)(2,1)S(1)}, u32[]{:S(2)}) copy-start(bf16[128,512]{1,0:T(8,128)(2,1)S(1)} %collective-permute-done.2.refs_3_) | copy-start | bytes 393220
  18.9 3.7 %copy-start.4 = (bf16[128,512]{1,0:T(8,128)(2,1)}, bf16[128,512]{1,0:T(8,128)(2,1)S(1)}, u32[]{:S(2)}) copy-start(bf16[128,512]{1,0:T(8,128)(2,1)S(1)} %collective-permute-done.refs_1_) | copy-start | bytes 393220
  22.6 0.7 copy-start.5
  25.7 2.8 %copy-start.2 = (f32[1280,128]{1,0:T(8,128)S(1)}, f32[1280,128]{1,0:T(8,128)}, u32[]{:S(2)}) copy-start(f32[1280,128]{1,0:T(8,128)} %get-tuple-element.5) | copy-start | bytes 1966084
  26.8 1.7 %collective-permute-start.3 = (f32[640,128]{1,0:T(8,128)S(1)}, f32[640,128]{1,0:T(8,128)S(1)}, u32[]{:S(2)}, u32[]{:S(2)}) collective-permute-start(f32[640,128]{1,0:T(8,128)S(1)} %constant_dynamic-slice_fusion.3), channel_id=1, source_target_pairs={{0,2},{2,0},{4,6},{6,4},{1,3},{3,1},{5,7},{7,5},{8,10},{10,8},{12,... | collective-permute-start | bytes 983048 | tf_op jit(solution)/shard_map/ppermute | solution.py:203
  28.5 4.6 %collective-permute-start.4 = (f32[160,128]{1,0:T(8,128)S(1)}, f32[160,128]{1,0:T(8,128)S(1)}, u32[]{:S(2)}, u32[]{:S(2)}) collective-permute-start(f32[160,128]{1,0:T(8,128)S(1)} %get-tuple-element.13), channel_id=1, source_target_pairs={{0,4},{1,5},{2,6},{3,7},{4,0},{5,1},{6,2},{7,3},{8,12},{9,13},{10,... | collective-permute-start | bytes 245768 | tf_op jit(solution)/shard_map/ppermute | solution.py:203
  30.1 5.8 %collective-permute-start.6 = (f32[160,128]{1,0:T(8,128)S(1)}, f32[160,128]{1,0:T(8,128)S(1)}, u32[]{:S(2)}, u32[]{:S(2)}) collective-permute-start(f32[160,128]{1,0:T(8,128)S(1)} %get-tuple-element.14), channel_id=1, source_target_pairs={{0,5},{1,4},{2,7},{3,6},{4,1},{5,0},{6,3},{7,2},{8,13},{9,12},{10,... | collective-permute-start | bytes 245768 | tf_op jit(solution)/shard_map/ppermute | solution.py:203
  31.6 5.5 %collective-permute-start.5 = (f32[160,128]{1,0:T(8,128)S(1)}, f32[160,128]{1,0:T(8,128)S(1)}, u32[]{:S(2)}, u32[]{:S(2)}) collective-permute-start(f32[160,128]{1,0:T(8,128)S(1)} %get-tuple-element.15), channel_id=1, source_target_pairs={{0,1},{1,0},{2,3},{3,2},{4,5},{5,4},{6,7},{7,6},{8,9},{9,8},{10,11... | collective-permute-start | bytes 245768 | tf_op jit(solution)/shard_map/ppermute | solution.py:203
  37.1 4.5 %collective-permute-start.7 = (f32[160,128]{1,0:T(8,128)S(1)}, f32[160,128]{1,0:T(8,128)S(1)}, u32[]{:S(2)}, u32[]{:S(2)}) collective-permute-start(f32[160,128]{1,0:T(8,128)S(1)} %add_add_fusion), channel_id=1, source_target_pairs={{0,8},{8,0},{16,24},{24,16},{1,9},{9,1},{17,25},{25,17},{2,10},{10... | collective-permute-start | bytes 245768 | tf_op jit(solution)/shard_map/ppermute | solution.py:203
  41.7 5.8 %collective-permute-start.8 = (f32[160,128]{1,0:T(8,128)S(1)}, f32[160,128]{1,0:T(8,128)S(1)}, u32[]{:S(2)}, u32[]{:S(2)}) collective-permute-start(f32[160,128]{1,0:T(8,128)S(1)} %add.130), channel_id=1, source_target_pairs={{0,16},{8,24},{16,0},{24,8},{1,17},{9,25},{17,1},{25,9},{2,18},{10... | collective-permute-start | bytes 245768 | tf_op jit(solution)/shard_map/ppermute | solution.py:203
  47.6 4.5 %collective-permute-start.9 = (f32[160,128]{1,0:T(8,128)S(1)}, f32[160,128]{1,0:T(8,128)S(1)}, u32[]{:S(2)}, u32[]{:S(2)}) collective-permute-start(f32[160,128]{1,0:T(8,128)S(1)} %get-tuple-element.8), channel_id=1, source_target_pairs={{0,4},{1,5},{2,6},{3,7},{4,0},{5,1},{6,2},{7,3},{8,12},{9,13},{10,... | collective-permute-start | bytes 245768 | tf_op jit(solution)/shard_map/ppermute | solution.py:203
  49.0 4.4 %collective-permute-start.10 = (f32[160,128]{1,0:T(8,128)S(1)}, f32[160,128]{1,0:T(8,128)S(1)}, u32[]{:S(2)}, u32[]{:S(2)}) collective-permute-start(f32[160,128]{1,0:T(8,128)S(1)} %get-tuple-element.8), channel_id=1, source_target_pairs={{0,1},{1,0},{2,3},{3,2},{4,5},{5,4},{6,7},{7,6},{8,9},{9,8},{10,11... | collective-permute-start | bytes 245768 | tf_op jit(solution)/shard_map/ppermute | solution.py:203
  49.6 5.3 %collective-permute-start.11 = (f32[160,128]{1,0:T(8,128)S(1)}, f32[160,128]{1,0:T(8,128)S(1)}, u32[]{:S(2)}, u32[]{:S(2)}) collective-permute-start(f32[160,128]{1,0:T(8,128)S(1)} %get-tuple-element.8), channel_id=1, source_target_pairs={{0,5},{1,4},{2,7},{3,6},{4,1},{5,0},{6,3},{7,2},{8,13},{9,12},{10,... | collective-permute-start | bytes 245768 | tf_op jit(solution)/shard_map/ppermute | solution.py:203
  55.0 1.7 %collective-permute-start.12 = (f32[640,128]{1,0:T(8,128)S(1)}, f32[640,128]{1,0:T(8,128)S(1)}, u32[]{:S(2)}, u32[]{:S(2)}) collective-permute-start(f32[640,128]{1,0:T(8,128)S(1)} %bitcast.22), channel_id=1, source_target_pairs={{0,2},{2,0},{4,6},{6,4},{1,3},{3,1},{5,7},{7,5},{8,10},{10,8},{12,... | collective-permute-start | bytes 983048 | tf_op jit(solution)/shard_map/ppermute | solution.py:203
  55.1 1.6 %copy-start = (bf16[512,512]{1,0:T(8,128)(2,1)S(1)}, bf16[512,512]{1,0:T(8,128)(2,1)}, u32[]{:S(2)}) copy-start(bf16[512,512]{1,0:T(8,128)(2,1)} %get-tuple-element.6.cols_ref) | copy-start | bytes 1572868
  55.2 1.5 %copy-start.1 = (f32[512,128]{1,0:T(8,128)S(1)}, f32[512,128]{1,0:T(8,128)}, u32[]{:S(2)}) copy-start(f32[512,128]{1,0:T(8,128)} %basis_ref.1) | copy-start | bytes 786436

commit v2 on v1

--- a/solution.py
+++ b/solution.py
@@ -9,8 +9,9 @@
 from jax.sharding import PartitionSpec as P
 
 ITERS = 2
-GROUP = 16
-HIGH = lax.Precision.HIGHEST
+GROUP = 32
+BLOCK = 16
+TILE = 8
 
 
 def split3(x):
@@ -21,54 +22,94 @@
     return hi, mid, low
 
 
-def dot_nn(a, b):
-    return lax.dot_general(a, b, (((1,), (0,)), ((), ())), precision=HIGH, preferred_element_type=jnp.float32)
-
-
-def dot_nt(a, b):
-    return lax.dot_general(a, b, (((1,), (1,)), ((), ())), precision=HIGH, preferred_element_type=jnp.float32)
-
-
-def dot_tn(a, b):
-    return lax.dot_general(a, b, (((0,), (0,)), ((), ())), precision=HIGH, preferred_element_type=jnp.float32)
-
-
-def eliminate(state, start, n):
+def dot(a, b, dims):
+    return lax.dot_general(a, b, (dims, ((), ())), preferred_element_type=jnp.float32)
+
+
+NN, NT, TN = ((1,), (0,)), ((1,), (1,)), ((0,), (0,))
+
+
+def deep_dot(a, b, dims):
+    (ah, am, al), (bh, bm, bl) = a, b
+    left = jnp.concatenate([ah, am, ah, am, ah, al], axis=dims[0][0])
+    right = jnp.concatenate([bh, bh, bm, bm, bl, bh], axis=dims[1][0])
+    return dot(left, right, dims)
+
+
+def wide_dot(a, b, dims):
+    (ah, am, al), (bh, bm, bl) = a, b
+    n = bh.shape[1]
+    both = jnp.concatenate([bh, bm], axis=1)
+    first = dot(ah, both, dims)
+    second = dot(am, both, dims)
+    small = dot(
+        jnp.concatenate([ah, al], axis=dims[0][0]), jnp.concatenate([bl, bh], axis=0), dims
+    )
+    return first[:, :n] + (first[:, n:] + second[:, :n] + (second[:, n:] + small))
+
+
+def eliminate(states, start, n):
+    shape = (TILE, n)
+    tiles = GROUP // TILE
+    row = lax.broadcasted_iota(jnp.int32, shape, 0)
+
+    def spread(value, i):
+        return jnp.broadcast_to(value[i // TILE][i % TILE : i % TILE + 1, :], shape)
+
+    halves = [
+        [
+            [state[pl.ds(pl.multiple_of(start + t * TILE, TILE), TILE), side] for t in range(tiles)]
+            for side in (slice(0, n), slice(n, 2 * n))
+        ]
+        for state in states
+    ]
+    pivots = [[None] * tiles for _ in states]
+    for first in range(0, GROUP, BLOCK):
+        held = [
+            {
+                k: {
+                    t: jnp.take_along_axis(
+                        left[t], jnp.zeros(shape, jnp.int32) + (start + k), axis=1, mode="promise_in_bounds"
+                    )
+                    for t in range(k // TILE, tiles)
+                }
+                for k in range(first, first + BLOCK)
+            }
+            for left, _ in halves
+        ]
+        for i in range(first, first + BLOCK):
+            at = i // TILE
+            for cols, sides, pivot_of in zip(held, halves, pivots):
+                pivot = spread(cols[i], i)
+                pivot_of[at] = pivot if i % TILE == 0 else jnp.where(row == i % TILE, pivot, pivot_of[at])
+                if i == GROUP - 1:
+                    continue
+                inverse = 1.0 / pivot
+                below = dict(cols[i])
+                below[at] = jnp.where(row > i % TILE, below[at], 0.0)
+                factor = {t: below[t] * inverse for t in below}
+                for k in range(i + 1, first + BLOCK):
+                    across = spread(cols[i], k)
+                    for t in cols[k]:
+                        if k == i + 1:
+                            cols[k][t] = cols[k][t] - (below[t] * across) * inverse
+                        else:
+                            cols[k][t] = cols[k][t] - factor[t] * across
+                for side in sides:
+                    across = spread(side, i)
+                    for t in below:
+                        side[t] = side[t] - factor[t] * across
+    lane = lax.broadcasted_iota(jnp.int32, (GROUP, n), 1)
     rows = pl.ds(pl.multiple_of(start, GROUP), GROUP)
-    left = state[rows, :n]
-    right = state[rows, n:]
-    shape = (GROUP, n)
-    row = lax.broadcasted_iota(jnp.int32, shape, 0)
-    lane = lax.broadcasted_iota(jnp.int32, shape, 1)
-    cols = [
-        jnp.take_along_axis(left, jnp.full(shape, 0, jnp.int32) + (start + k), axis=1, mode="promise_in_bounds")
-        for k in range(GROUP)
-    ]
-    pivots = jnp.ones(shape, jnp.float32)
-    for i in range(GROUP):
-        pivot = jnp.broadcast_to(cols[i][i : i + 1, :], shape)
-        pivots = jnp.where(row == i, pivot, pivots)
-        if i == GROUP - 1:
-            break
-        inverse = 1.0 / pivot
-        below = jnp.where(row > i, cols[i], 0.0)
-        for k in range(i + 1, GROUP):
-            cols[k] = cols[k] - (below * cols[k][i : i + 1, :]) * inverse
-        factor = below * inverse
-        left = left - factor * left[i : i + 1, :]
-        right = right - factor * right[i : i + 1, :]
-    scale = lax.rsqrt(pivots)
-    left = left * scale
-    right = right * scale
-    state[rows, :n] = left
-    state[rows, n:] = right
-    hi, mid, low = split3(jnp.where(lane >= start + GROUP, left, 0.0))
-    first = jnp.concatenate([hi, hi, mid, mid, hi, low], axis=0)
-    wide = jnp.concatenate([left, right], axis=1)
-    hi, mid, low = split3(wide)
-    second = jnp.concatenate([hi, mid, hi, mid, low, hi], axis=0)
-    delta = lax.dot_general(first, second, (((0,), (0,)), ((), ())), preferred_element_type=jnp.float32)
-    state[...] = state[...] - delta
+    for state, sides, pivot_of in zip(states, halves, pivots):
+        scale = jnp.concatenate([lax.rsqrt(p) for p in pivot_of], axis=0)
+        left, right = [jnp.concatenate(side, axis=0) * scale for side in sides]
+        state[rows, :n] = left
+        state[rows, n:] = right
+        parts = split3(left)
+        lhs = [jnp.where(lane >= start + GROUP, part, jnp.zeros_like(part)) for part in parts]
+        rhs = [jnp.concatenate(pair, axis=1) for pair in zip(parts, split3(right))]
+        state[...] = state[...] - deep_dot(lhs, rhs, TN)
 
 
 def upper_blocks(size, n):
@@ -83,12 +124,8 @@
         start = pl.multiple_of(lax.bitwise_xor(place_ref[0], distance) * rows, rows)
         columns_ref[pl.ds(start, rows), :] = piece[...]
     for b, (i, j) in enumerate(upper_blocks(columns_ref.shape[0], n)):
-        gram_ref[b * n : (b + 1) * n, :] = lax.dot_general(
-            columns_ref[i * n : (i + 1) * n, :],
-            columns_ref[j * n : (j + 1) * n, :],
-            (((1,), (1,)), ((), ())),
-            preferred_element_type=jnp.float32,
-        ) * (1.0 / divisor)
+        product = dot(columns_ref[i * n : (i + 1) * n, :], columns_ref[j * n : (j + 1) * n, :], NT)
+        gram_ref[b * n : (b + 1) * n, :] = product / divisor
 
 
 def local_gram(place, pieces, divisor, n):
@@ -107,59 +144,65 @@
     )(place.reshape(1), *pieces)
 
 
-def factor_kernel(blocks_ref, basis_ref, cols_ref, tri_ref, out_ref, core_ref, gram_ref, work, one, two):
+def factor_kernel(blocks_ref, basis_ref, cols_ref, tri_ref, out_ref, core_ref, high, middle, lower, work, one, two):
     size = tri_ref.shape[0]
     n = basis_ref.shape[1]
+    phases = size // n
+    part = [slice(i * n, (i + 1) * n) for i in range(phases)]
     for b, (i, j) in enumerate(upper_blocks(size, n)):
         block = blocks_ref[b * n : (b + 1) * n, :]
-        gram_ref[i * n : (i + 1) * n, j * n : (j + 1) * n] = block
+        work[part[i], part[j]] = block
+        for ref, piece in zip((high, middle, lower), split3(block)):
+            ref[part[i], part[j]] = piece
+            if i != j:
+                ref[part[j], part[i]] = piece.T
         if i != j:
-            gram_ref[j * n : (j + 1) * n, i * n : (i + 1) * n] = block.T
-    phases = size // n
+            tri_ref[part[i], part[j]] = jnp.zeros((n, n), jnp.float32)
     eye = (
         lax.broadcasted_iota(jnp.int32, (n, n), 0) == lax.broadcasted_iota(jnp.int32, (n, n), 1)
     ).astype(jnp.float32)
     upper = lax.broadcasted_iota(jnp.int32, (n, n), 0) <= lax.broadcasted_iota(jnp.int32, (n, n), 1)
-    work[...] = gram_ref[...]
-    tri_ref[...] = jnp.zeros_like(tri_ref)
     basis = basis_ref[...]
     for phase in range(max(phases, 2 * ITERS)):
         if phase < phases:
-            at = slice(phase * n, (phase + 1) * n)
-            rest = slice((phase + 1) * n, size)
+            at = part[phase]
             one[:, :n] = work[at, at]
             one[:, n:] = eye
         if phase < 2 * ITERS:
             if phase % 2 == 0:
-                wide = dot_nn(gram_ref[...], basis)
-                two[:, :n] = dot_tn(basis, wide)
+                parts = split3(basis)
+                wide = split3(wide_dot((high[...], middle[...], lower[...]), parts, NN))
+                two[:, :n] = wide_dot(parts, wide, TN)
             else:
-                two[:, :n] = dot_tn(wide, wide)
+                wide = split3(wide)
+                two[:, :n] = wide_dot(wide, wide, TN)
             two[:, n:] = eye
 
         def step(group, carry):
-            if phase < phases:
-                eliminate(one, group * GROUP, n)
-            if phase < 2 * ITERS:
-                eliminate(two, group * GROUP, n)
+            states = [one] * (phase < phases) + [two] * (phase < 2 * ITERS)
+            eliminate(states, group * GROUP, n)
             return carry
 
         lax.fori_loop(0, n // GROUP, step, 0)
         if phase < phases:
             tri_ref[at, at] = jnp.where(upper, one[:, :n], 0.0).T
             if phase < phases - 1:
-                panel = dot_nn(one[:, n:], work[at, rest])
+                rest = slice((phase + 1) * n, size)
+                panel = deep_dot(split3(one[:, n:]), split3(work[at, rest]), NN)
                 tri_ref[rest, at] = panel.T
-                work[rest, rest] = work[rest, rest] - dot_tn(panel, panel)
+                pieces = split3(panel)
+                for i in range(phase + 1, phases):
+                    tail = slice((i - phase - 1) * n, None)
+                    mine = slice((i - phase - 1) * n, (i - phase) * n)
+                    work[part[i], i * n :] = work[part[i], i * n :] - deep_dot(
+                        [x[:, mine] for x in pieces], [x[:, tail] for x in pieces], TN
+                    )
         if phase < 2 * ITERS:
-            wide = dot_nt(wide, two[:, n:])
+            wide = deep_dot(wide, split3(two[:, n:]), NT)
             if phase % 2 == 1:
                 basis = wide
     out_ref[...] = basis
-    narrow = basis.astype(jnp.bfloat16)
-    core_ref[...] = lax.dot_general(
-        narrow, cols_ref[...], (((0,), (0,)), ((), ())), preferred_element_type=jnp.float32
-    ).astype(jnp.bfloat16)
+    core_ref[...] = dot(basis.astype(jnp.bfloat16), cols_ref[...], TN).astype(jnp.bfloat16)
 
 
 def factor(blocks, basis, columns):
@@ -172,7 +215,9 @@
             jax.ShapeDtypeStruct((n, columns.shape[1]), jnp.bfloat16),
         ),
         scratch_shapes=[
-            pltpu.VMEM((size, size), jnp.float32),
+            pltpu.VMEM((size, size), jnp.bfloat16),
+            pltpu.VMEM((size, size), jnp.bfloat16),
+            pltpu.VMEM((size, size), jnp.bfloat16),
             pltpu.VMEM((size, size), jnp.float32),
             pltpu.VMEM((n, 2 * n), jnp.float32),
             pltpu.VMEM((n, 2 * n), jnp.float32),

time: 84.4 us -> 79 us (0.936)
  Pallas kernels: 29.9 us -> 24.5 us
    pallas_call x1, Pallas kernels: 27.4 us -> 22 us  [factor(): pl.pallas_call(factor_kernel, out_shape=(jax.ShapeDtypeStruct((size, size...]
where the time goes in v2:
time: 79 us; the launch traced here: 78.8 us
  waiting for transfers between devices  31.6 us (40%)
  Pallas kernels  24.5 us (31%)
  starting transfers between devices  14 us (18%)
  local copies, waits for them, and re-layouts  5 us (6%)
  between operations  3.51 us (4%)
    ppermute x13, waiting for transfers between devices, swap(): return lax.ppermute(value, self.axes, pairs)  31.6 us
    pallas_call x1, Pallas kernels, factor(): pl.pallas_call(factor_kernel, out_shape=(jax.ShapeDtypeStruct((size, size...  22 us
    ppermute x13, starting transfers between devices, swap(): return lax.ppermute(value, self.axes, pairs)  14 us
    pallas_call x1, Pallas kernels, local_gram(): pl.pallas_call(functools.partial(gram_kernel, divisor, n), out_shape=(jax...  2.47 us
    dynamic_slice x1, local copies, waits for them, and re-layouts, block_of(): return lax.dynamic_slice_in_dim(slab, start, block_cols, 1)  1.81 us
  transfers between devices with their start and end apart: 13, of which 13 were waited for; matrix products, arithmetic and copies ran while one was open for 0% of the time, Pallas kernels for 0%

profile of v2, /device:TPU:0, one launch (start us, length us, event | category | flops | bytes accessed | tf_op | source)
XLA Modules:
  0.0 78.8 jit_solution(10846257126952013507)
XLA Ops:
  0.7 0.0 copy-start.6
  0.7 0.6 copy-done.6
  1.3 0.1 select_reduce_fusion
  1.4 0.6 fusion
  4.6 1.8 %constant_dynamic-slice_fusion.4 = (bf16[128,512]{1,0:T(8,128)(2,1)S(1)}, bf16[128,512]{1,0:T(8,128)(2,1)S(1)}, bf16[128,512]{1,0:T(8,128)(2,1)}, bf16[128,512]{1,0:T(8,128)(2,1)S(1)}) fusion(bf16[128,2048]{1,0:T(8,128)(2,1)} %param.3, s32[]{:T(128)S(6)} %select_n.103, s32[]{:T(128)S(6)} %select_n.99, s32[]{:T(128)S(6)} %select_n.97, s32[]{:T(128)S(6)} %select_n.101), kind=kLoop, calls=%fused_computation.12 | loop fusion | bytes 1048592 | tf_op jit(solution)/shard_map/dynamic_slice | solution.py:295
  6.5 5.0 %collective-permute-start.2 = (bf16[128,512]{1,0:T(8,128)(2,1)S(1)}, bf16[128,512]{1,0:T(8,128)(2,1)S(1)}, u32[]{:S(2)}, u32[]{:S(2)}) collective-permute-start(bf16[128,512]{1,0:T(8,128)(2,1)S(1)} %get-tuple-element.9), channel_id=1, source_target_pairs={{0,24},{8,16},{16,8},{24,0},{1,25},{9,17},{17,9},{25,1},{2,26},{10... | collective-permute-start | bytes 393224 | tf_op jit(solution)/shard_map/ppermute | solution.py:248
  11.5 0.0 collective-permute-start
  11.5 0.6 collective-permute-start.1
  12.1 3.8 %collective-permute-done.2.refs_3_ = bf16[128,512]{1,0:T(8,128)(2,1)S(1)} collective-permute-done((bf16[128,512]{1,0:T(8,128)(2,1)S(1)}, bf16[128,512]{1,0:T(8,128)(2,1)S(1)}, u32[]{:S(2)}, u32[]{:S(2)}) %collective-permute-start.2) | collective-permute-done | bytes 131104 | tf_op jit(solution)/shard_map/ppermute | solution.py:248
  15.9 0.0 copy-start.3
  15.9 3.0 %collective-permute-done.refs_1_ = bf16[128,512]{1,0:T(8,128)(2,1)S(1)} collective-permute-done((bf16[128,512]{1,0:T(8,128)(2,1)S(1)}, bf16[128,512]{1,0:T(8,128)(2,1)S(1)}, u32[]{:S(2)}, u32[]{:S(2)}) %collective-permute-start) | collective-permute-done | bytes 131104 | tf_op jit(solution)/shard_map/ppermute | solution.py:248
  18.9 0.0 copy-start.4
  18.9 3.7 %collective-permute-done.1.refs_2_ = bf16[128,512]{1,0:T(8,128)(2,1)S(1)} collective-permute-done((bf16[128,512]{1,0:T(8,128)(2,1)S(1)}, bf16[128,512]{1,0:T(8,128)(2,1)S(1)}, u32[]{:S(2)}, u32[]{:S(2)}) %collective-permute-start.1) | collective-permute-done | bytes 131104 | tf_op jit(solution)/shard_map/ppermute | solution.py:248
  22.6 0.0 copy-start.5
  22.6 0.0 copy-done.3
  22.6 0.0 copy-done.4
  22.6 0.6 copy-done.5
  23.2 2.5 %local_gram.1 = (bf16[512,512]{1,0:T(8,128)(2,1)}, f32[1280,128]{1,0:T(8,128)}) custom-call(s32[1]{0:T(128)} %bitcast.place_ref, bf16[128,512]{1,0:T(8,128)(2,1)} %get-tuple-element.11.refs_0_, bf16[128,512]{1,0:T(8,128)(2,1)} %copy-done.4, bf16[128,512]{1,0:T(8,128)(2,1)} %copy-done.5, bf16[128,512]{1,0:T(8,128)(2,1)} %copy-done.3), custom_call_target="tpu_custom_call" | custom-call | tf_op jit(solution)/shard_map/local_gram/pallas_call | solution.py:135
  25.7 0.0 copy-start.2
  25.7 1.1 %constant_dynamic-slice_fusion.3 = f32[640,128]{1,0:T(8,128)S(1)} fusion(f32[1280,128]{1,0:T(8,128)} %get-tuple-element.5, s32[]{:T(128)S(6)} %select_n.106), kind=kLoop, calls=%fused_computation.11 | loop fusion | bytes 655364 | tf_op jit(solution)/shard_map/dynamic_slice | solution.py:253
  26.8 0.1 collective-permute-start.3
  26.9 1.5 %collective-permute-done.3 = f32[640,128]{1,0:T(8,128)S(1)} collective-permute-done((f32[640,128]{1,0:T(8,128)S(1)}, f32[640,128]{1,0:T(8,128)S(1)}, u32[]{:S(2)}, u32[]{:S(2)}) %collective-permute-start.3) | collective-permute-done | bytes 327712 | tf_op jit(solution)/shard_map/ppermute | solution.py:248
  28.5 0.0 copy-done.2
  28.5 1.6 %collective-permute-start.4 = (f32[160,128]{1,0:T(8,128)S(1)}, f32[160,128]{1,0:T(8,128)S(1)}, u32[]{:S(2)}, u32[]{:S(2)}) collective-permute-start(f32[160,128]{1,0:T(8,128)S(1)} %get-tuple-element.13), channel_id=1, source_target_pairs={{0,4},{1,5},{2,6},{3,7},{4,0},{5,1},{6,2},{7,3},{8,12},{9,13},{10,... | collective-permute-start | bytes 245768 | tf_op jit(solution)/shard_map/ppermute | solution.py:248
  30.1 1.5 %collective-permute-start.6 = (f32[160,128]{1,0:T(8,128)S(1)}, f32[160,128]{1,0:T(8,128)S(1)}, u32[]{:S(2)}, u32[]{:S(2)}) collective-permute-start(f32[160,128]{1,0:T(8,128)S(1)} %get-tuple-element.14), channel_id=1, source_target_pairs={{0,5},{1,4},{2,7},{3,6},{4,1},{5,0},{6,3},{7,2},{8,13},{9,12},{10,... | collective-permute-start | bytes 245768 | tf_op jit(solution)/shard_map/ppermute | solution.py:248
  31.6 0.5 collective-permute-start.5
  32.1 1.0 %collective-permute-done.4 = f32[160,128]{1,0:T(8,128)S(1)} collective-permute-done((f32[160,128]{1,0:T(8,128)S(1)}, f32[160,128]{1,0:T(8,128)S(1)}, u32[]{:S(2)}, u32[]{:S(2)}) %collective-permute-start.4) | collective-permute-done | bytes 81952 | tf_op jit(solution)/shard_map/ppermute | solution.py:248
  33.1 2.8 %collective-permute-done.6 = f32[160,128]{1,0:T(8,128)S(1)} collective-permute-done((f32[160,128]{1,0:T(8,128)S(1)}, f32[160,128]{1,0:T(8,128)S(1)}, u32[]{:S(2)}, u32[]{:S(2)}) %collective-permute-start.6) | collective-permute-done | bytes 81952 | tf_op jit(solution)/shard_map/ppermute | solution.py:248
  35.9 1.2 %collective-permute-done.5 = f32[160,128]{1,0:T(8,128)S(1)} collective-permute-done((f32[160,128]{1,0:T(8,128)S(1)}, f32[160,128]{1,0:T(8,128)S(1)}, u32[]{:S(2)}, u32[]{:S(2)}) %collective-permute-start.5) | collective-permute-done | bytes 81952 | tf_op jit(solution)/shard_map/ppermute | solution.py:248
  37.1 0.1 collective-permute-start.7
  37.2 4.4 %collective-permute-done.7 = f32[160,128]{1,0:T(8,128)S(1)} collective-permute-done((f32[160,128]{1,0:T(8,128)S(1)}, f32[160,128]{1,0:T(8,128)S(1)}, u32[]{:S(2)}, u32[]{:S(2)}) %collective-permute-start.7) | collective-permute-done | bytes 81952 | tf_op jit(solution)/shard_map/ppermute | solution.py:248
  41.7 1.1 %collective-permute-start.8 = (f32[160,128]{1,0:T(8,128)S(1)}, f32[160,128]{1,0:T(8,128)S(1)}, u32[]{:S(2)}, u32[]{:S(2)}) collective-permute-start(f32[160,128]{1,0:T(8,128)S(1)} %add.130), channel_id=1, source_target_pairs={{0,16},{8,24},{16,0},{24,8},{1,17},{9,25},{17,1},{25,9},{2,18},{10... | collective-permute-start | bytes 245768 | tf_op jit(solution)/shard_map/ppermute | solution.py:248
  42.7 4.8 %collective-permute-done.8 = f32[160,128]{1,0:T(8,128)S(1)} collective-permute-done((f32[160,128]{1,0:T(8,128)S(1)}, f32[160,128]{1,0:T(8,128)S(1)}, u32[]{:S(2)}, u32[]{:S(2)}) %collective-permute-start.8) | collective-permute-done | bytes 81952 | tf_op jit(solution)/shard_map/ppermute | solution.py:248
  47.6 1.5 %collective-permute-start.9 = (f32[160,128]{1,0:T(8,128)S(1)}, f32[160,128]{1,0:T(8,128)S(1)}, u32[]{:S(2)}, u32[]{:S(2)}) collective-permute-start(f32[160,128]{1,0:T(8,128)S(1)} %get-tuple-element.8), channel_id=1, source_target_pairs={{0,4},{1,5},{2,6},{3,7},{4,0},{5,1},{6,2},{7,3},{8,12},{9,13},{10,... | collective-permute-start | bytes 245768 | tf_op jit(solution)/shard_map/ppermute | solution.py:248
  49.0 0.6 collective-permute-start.10
  49.6 1.5 %collective-permute-start.11 = (f32[160,128]{1,0:T(8,128)S(1)}, f32[160,128]{1,0:T(8,128)S(1)}, u32[]{:S(2)}, u32[]{:S(2)}) collective-permute-start(f32[160,128]{1,0:T(8,128)S(1)} %get-tuple-element.8), channel_id=1, source_target_pairs={{0,5},{1,4},{2,7},{3,6},{4,1},{5,0},{6,3},{7,2},{8,13},{9,12},{10,... | collective-permute-start | bytes 245768 | tf_op jit(solution)/shard_map/ppermute | solution.py:248
  51.1 1.0 %collective-permute-done.9 = f32[160,128]{1,0:T(8,128)S(1)} collective-permute-done((f32[160,128]{1,0:T(8,128)S(1)}, f32[160,128]{1,0:T(8,128)S(1)}, u32[]{:S(2)}, u32[]{:S(2)}) %collective-permute-start.9) | collective-permute-done | bytes 81952 | tf_op jit(solution)/shard_map/ppermute | solution.py:248
  52.1 1.4 %collective-permute-done.10 = f32[160,128]{1,0:T(8,128)S(1)} collective-permute-done((f32[160,128]{1,0:T(8,128)S(1)}, f32[160,128]{1,0:T(8,128)S(1)}, u32[]{:S(2)}, u32[]{:S(2)}) %collective-permute-start.10) | collective-permute-done | bytes 81952 | tf_op jit(solution)/shard_map/ppermute | solution.py:248
  53.5 1.5 %collective-permute-done.11 = f32[160,128]{1,0:T(8,128)S(1)} collective-permute-done((f32[160,128]{1,0:T(8,128)S(1)}, f32[160,128]{1,0:T(8,128)S(1)}, u32[]{:S(2)}, u32[]{:S(2)}) %collective-permute-start.11) | collective-permute-done | bytes 81952 | tf_op jit(solution)/shard_map/ppermute | solution.py:248
  55.0 0.1 collective-permute-start.12
  55.1 0.0 copy-start
  55.2 0.0 copy-start.1
  55.2 1.5 %collective-permute-done.12 = f32[640,128]{1,0:T(8,128)S(1)} collective-permute-done((f32[640,128]{1,0:T(8,128)S(1)}, f32[640,128]{1,0:T(8,128)S(1)}, u32[]{:S(2)}, u32[]{:S(2)}) %collective-permute-start.12) | collective-permute-done | bytes 327712 | tf_op jit(solution)/shard_map/ppermute | solution.py:248
  56.7 0.0 copy-done
  56.7 0.0 copy-done.1
  56.7 22.0 %factor.1 = (f32[512,512]{1,0:T(8,128)}, f32[512,128]{1,0:T(8,128)}, bf16[128,512]{1,0:T(8,128)(2,1)}) custom-call(f32[1280,128]{1,0:T(8,128)S(1)} %bitcast.21, f32[512,128]{1,0:T(8,128)S(1)} %copy-done.1, bf16[512,512]{1,0:T(8,128)(2,1)S(1)} %copy-done), custom_call_target="tpu_custom_call" | custom-call | tf_op jit(solution)/shard_map/factor/pallas_call | solution.py:210
  (12 shorter events, 0.3 us)
Async XLA Ops:
  0.7 0.7 copy-start.6
  6.5 9.4 %collective-permute-start.2 = (bf16[128,512]{1,0:T(8,128)(2,1)S(1)}, bf16[128,512]{1,0:T(8,128)(2,1)S(1)}, u32[]{:S(2)}, u32[]{:S(2)}) collective-permute-start(bf16[128,512]{1,0:T(8,128)(2,1)S(1)} %get-tuple-element.9), channel_id=1, source_target_pairs={{0,24},{8,16},{16,8},{24,0},{1,25},{9,17},{17,9},{25,1},{2,26},{10... | collective-permute-start | bytes 393224 | tf_op jit(solution)/shard_map/ppermute | solution.py:248
  11.5 7.4 %collective-permute-start = (bf16[128,512]{1,0:T(8,128)(2,1)S(1)}, bf16[128,512]{1,0:T(8,128)(2,1)S(1)}, u32[]{:S(2)}, u32[]{:S(2)}) collective-permute-start(bf16[128,512]{1,0:T(8,128)(2,1)S(1)} %get-tuple-element.10), channel_id=1, source_target_pairs={{0,8},{8,0},{16,24},{24,16},{1,9},{9,1},{17,25},{25,17},{2,10},{10... | collective-permute-start | bytes 393224 | tf_op jit(solution)/shard_map/ppermute | solution.py:248
  11.5 11.1 %collective-permute-start.1 = (bf16[128,512]{1,0:T(8,128)(2,1)S(1)}, bf16[128,512]{1,0:T(8,128)(2,1)S(1)}, u32[]{:S(2)}, u32[]{:S(2)}) collective-permute-start(bf16[128,512]{1,0:T(8,128)(2,1)S(1)} %get-tuple-element.12), channel_id=1, source_target_pairs={{0,16},{8,24},{16,0},{24,8},{1,17},{9,25},{17,1},{25,9},{2,18},{10... | collective-permute-start | bytes 393224 | tf_op jit(solution)/shard_map/ppermute | solution.py:248
  15.9 6.7 %copy-start.3 = (bf16[128,512]{1,0:T(8,128)(2,1)}, bf16[128,512]{1,0:T(8,128)(2,1)S(1)}, u32[]{:S(2)}) copy-start(bf16[128,512]{1,0:T(8,128)(2,1)S(1)} %collective-permute-done.2.refs_3_) | copy-start | bytes 393220
  18.9 3.7 %copy-start.4 = (bf16[128,512]{1,0:T(8,128)(2,1)}, bf16[128,512]{1,0:T(8,128)(2,1)S(1)}, u32[]{:S(2)}) copy-start(bf16[128,512]{1,0:T(8,128)(2,1)S(1)} %collective-permute-done.refs_1_) | copy-start | bytes 393220
  22.6 0.7 copy-start.5
  25.7 2.8 %copy-start.2 = (f32[1280,128]{1,0:T(8,128)S(1)}, f32[1280,128]{1,0:T(8,128)}, u32[]{:S(2)}) copy-start(f32[1280,128]{1,0:T(8,128)} %get-tuple-element.5) | copy-start | bytes 1966084
  26.8 1.7 %collective-permute-start.3 = (f32[640,128]{1,0:T(8,128)S(1)}, f32[640,128]{1,0:T(8,128)S(1)}, u32[]{:S(2)}, u32[]{:S(2)}) collective-permute-start(f32[640,128]{1,0:T(8,128)S(1)} %constant_dynamic-slice_fusion.3), channel_id=1, source_target_pairs={{0,2},{2,0},{4,6},{6,4},{1,3},{3,1},{5,7},{7,5},{8,10},{10,8},{12,... | collective-permute-start | bytes 983048 | tf_op jit(solution)/shard_map/ppermute | solution.py:248
  28.5 4.6 %collective-permute-start.4 = (f32[160,128]{1,0:T(8,128)S(1)}, f32[160,128]{1,0:T(8,128)S(1)}, u32[]{:S(2)}, u32[]{:S(2)}) collective-permute-start(f32[160,128]{1,0:T(8,128)S(1)} %get-tuple-element.13), channel_id=1, source_target_pairs={{0,4},{1,5},{2,6},{3,7},{4,0},{5,1},{6,2},{7,3},{8,12},{9,13},{10,... | collective-permute-start | bytes 245768 | tf_op jit(solution)/shard_map/ppermute | solution.py:248
  30.1 5.8 %collective-permute-start.6 = (f32[160,128]{1,0:T(8,128)S(1)}, f32[160,128]{1,0:T(8,128)S(1)}, u32[]{:S(2)}, u32[]{:S(2)}) collective-permute-start(f32[160,128]{1,0:T(8,128)S(1)} %get-tuple-element.14), channel_id=1, source_target_pairs={{0,5},{1,4},{2,7},{3,6},{4,1},{5,0},{6,3},{7,2},{8,13},{9,12},{10,... | collective-permute-start | bytes 245768 | tf_op jit(solution)/shard_map/ppermute | solution.py:248
  31.6 5.5 %collective-permute-start.5 = (f32[160,128]{1,0:T(8,128)S(1)}, f32[160,128]{1,0:T(8,128)S(1)}, u32[]{:S(2)}, u32[]{:S(2)}) collective-permute-start(f32[160,128]{1,0:T(8,128)S(1)} %get-tuple-element.15), channel_id=1, source_target_pairs={{0,1},{1,0},{2,3},{3,2},{4,5},{5,4},{6,7},{7,6},{8,9},{9,8},{10,11... | collective-permute-start | bytes 245768 | tf_op jit(solution)/shard_map/ppermute | solution.py:248
  37.1 4.5 %collective-permute-start.7 = (f32[160,128]{1,0:T(8,128)S(1)}, f32[160,128]{1,0:T(8,128)S(1)}, u32[]{:S(2)}, u32[]{:S(2)}) collective-permute-start(f32[160,128]{1,0:T(8,128)S(1)} %add_add_fusion), channel_id=1, source_target_pairs={{0,8},{8,0},{16,24},{24,16},{1,9},{9,1},{17,25},{25,17},{2,10},{10... | collective-permute-start | bytes 245768 | tf_op jit(solution)/shard_map/ppermute | solution.py:248
  41.7 5.8 %collective-permute-start.8 = (f32[160,128]{1,0:T(8,128)S(1)}, f32[160,128]{1,0:T(8,128)S(1)}, u32[]{:S(2)}, u32[]{:S(2)}) collective-permute-start(f32[160,128]{1,0:T(8,128)S(1)} %add.130), channel_id=1, source_target_pairs={{0,16},{8,24},{16,0},{24,8},{1,17},{9,25},{17,1},{25,9},{2,18},{10... | collective-permute-start | bytes 245768 | tf_op jit(solution)/shard_map/ppermute | solution.py:248
  47.6 4.5 %collective-permute-start.9 = (f32[160,128]{1,0:T(8,128)S(1)}, f32[160,128]{1,0:T(8,128)S(1)}, u32[]{:S(2)}, u32[]{:S(2)}) collective-permute-start(f32[160,128]{1,0:T(8,128)S(1)} %get-tuple-element.8), channel_id=1, source_target_pairs={{0,4},{1,5},{2,6},{3,7},{4,0},{5,1},{6,2},{7,3},{8,12},{9,13},{10,... | collective-permute-start | bytes 245768 | tf_op jit(solution)/shard_map/ppermute | solution.py:248
  49.0 4.4 %collective-permute-start.10 = (f32[160,128]{1,0:T(8,128)S(1)}, f32[160,128]{1,0:T(8,128)S(1)}, u32[]{:S(2)}, u32[]{:S(2)}) collective-permute-start(f32[160,128]{1,0:T(8,128)S(1)} %get-tuple-element.8), channel_id=1, source_target_pairs={{0,1},{1,0},{2,3},{3,2},{4,5},{5,4},{6,7},{7,6},{8,9},{9,8},{10,11... | collective-permute-start | bytes 245768 | tf_op jit(solution)/shard_map/ppermute | solution.py:248
  49.6 5.3 %collective-permute-start.11 = (f32[160,128]{1,0:T(8,128)S(1)}, f32[160,128]{1,0:T(8,128)S(1)}, u32[]{:S(2)}, u32[]{:S(2)}) collective-permute-start(f32[160,128]{1,0:T(8,128)S(1)} %get-tuple-element.8), channel_id=1, source_target_pairs={{0,5},{1,4},{2,7},{3,6},{4,1},{5,0},{6,3},{7,2},{8,13},{9,12},{10,... | collective-permute-start | bytes 245768 | tf_op jit(solution)/shard_map/ppermute | solution.py:248
  55.0 1.7 %collective-permute-start.12 = (f32[640,128]{1,0:T(8,128)S(1)}, f32[640,128]{1,0:T(8,128)S(1)}, u32[]{:S(2)}, u32[]{:S(2)}) collective-permute-start(f32[640,128]{1,0:T(8,128)S(1)} %bitcast.22), channel_id=1, source_target_pairs={{0,2},{2,0},{4,6},{6,4},{1,3},{3,1},{5,7},{7,5},{8,10},{10,8},{12,... | collective-permute-start | bytes 983048 | tf_op jit(solution)/shard_map/ppermute | solution.py:248
  55.1 1.6 %copy-start = (bf16[512,512]{1,0:T(8,128)(2,1)S(1)}, bf16[512,512]{1,0:T(8,128)(2,1)}, u32[]{:S(2)}) copy-start(bf16[512,512]{1,0:T(8,128)(2,1)} %get-tuple-element.6.cols_ref) | copy-start | bytes 1572868
  55.2 1.5 %copy-start.1 = (f32[512,128]{1,0:T(8,128)S(1)}, f32[512,128]{1,0:T(8,128)}, u32[]{:S(2)}) copy-start(f32[512,128]{1,0:T(8,128)} %basis_ref.1) | copy-start | bytes 786436

commit v3 on v2

--- a/solution.py
+++ b/solution.py
@@ -117,36 +117,120 @@
     return [(i, j) for i in range(count) for j in range(i, count)]
 
 
-def gram_kernel(divisor, n, place_ref, *refs):
-    pieces, (columns_ref, gram_ref) = refs[:-2], refs[-2:]
+def axis_bits(axis):
+    size = lax.axis_size(axis)
+    assert size & (size - 1) == 0, axis
+    return [(axis, 1 << b) for b in range(size.bit_length() - 1)]
+
+
+def plane_groups():
+    first, *rest = axis_bits("gy") + axis_bits("gz")
+    return [[first]] + [rest[b : b + 2] for b in range(0, len(rest), 2)]
+
+
+def place_in(bits):
+    place = 0
+    for axis, distance in bits:
+        place = place * 2 + lax.bitwise_and(lax.axis_index(axis) // distance, 1)
+    return place
+
+
+def plane_place():
+    return place_in(sum(plane_groups(), []))
+
+
+def fiber_place():
+    return lax.axis_index("af")
+
+
+def pick_kernel(owner_ref, slab_ref, *refs):
+    pieces, sems = refs[:-1], refs[-1]
+    fibers = len(pieces)
+    width = pieces[0].shape[1]
+    me = fiber_place()
+    copies = []
+    for distance in range(fibers):
+        block = 0
+        for b in range(fibers):
+            mine = owner_ref[0, 0, b] == lax.bitwise_xor(me, distance)
+            block = jnp.where(mine, b, block)
+        start = pl.multiple_of(block * width, width)
+        copies.append(
+            pltpu.make_async_copy(slab_ref.at[:, pl.ds(start, width)], pieces[distance], sems.at[distance])
+        )
+    for copy in copies:
+        copy.start()
+    for copy in copies:
+        copy.wait()
+
+
+def pick_blocks(owners, slab):
+    fibers = owners.shape[-1]
+    piece = jax.ShapeDtypeStruct((slab.shape[0], slab.shape[1] // fibers), slab.dtype)
+    return pl.pallas_call(
+        pick_kernel,
+        out_shape=(piece,) * fibers,
+        in_specs=[pl.BlockSpec(memory_space=pltpu.SMEM), pl.BlockSpec(memory_space=pl.ANY)],
+        out_specs=(pl.BlockSpec(memory_space=pl.ANY),) * fibers,
+        scratch_shapes=[pltpu.SemaphoreType.DMA((fibers,))],
+        name="pick_blocks",
+    )(owners, slab)
+
+
+def in_row_order(pieces, columns):
     rows = pieces[0].shape[0]
+    me = fiber_place()
     for distance, piece in enumerate(pieces):
-        start = pl.multiple_of(lax.bitwise_xor(place_ref[0], distance) * rows, rows)
-        columns_ref[pl.ds(start, rows), :] = piece[...]
-    for b, (i, j) in enumerate(upper_blocks(columns_ref.shape[0], n)):
-        product = dot(columns_ref[i * n : (i + 1) * n, :], columns_ref[j * n : (j + 1) * n, :], NT)
-        gram_ref[b * n : (b + 1) * n, :] = product / divisor
-
-
-def local_gram(place, pieces, divisor, n):
+        start = pl.multiple_of(lax.bitwise_xor(me, distance) * rows, rows)
+        columns[pl.ds(start, rows), :] = piece[...]
+
+
+def gram_kernel(divisor, n, chunks, *refs):
+    pieces, (kept_ref, sent_ref, columns, blocks) = refs[:-4], refs[-4:]
+    in_row_order(pieces, columns)
+    for b, (i, j) in enumerate(upper_blocks(columns.shape[0], n)):
+        product = dot(columns[i * n : (i + 1) * n, :], columns[j * n : (j + 1) * n, :], NT)
+        blocks[b * n : (b + 1) * n, :] = product / divisor
+    place = plane_place()
+    rows = blocks.shape[0] // chunks
+    for slot in range(chunks):
+        start = pl.multiple_of(lax.bitwise_xor(place, slot) * rows, rows)
+        target = kept_ref if slot < chunks // 2 else sent_ref
+        at = slot % (chunks // 2) * rows
+        target[at : at + rows, :] = blocks[pl.ds(start, rows), :]
+
+
+def local_gram(pieces, divisor, n, chunks):
     rows, width = pieces[0].shape
     size = rows * len(pieces)
-    vmem = pl.BlockSpec(memory_space=pltpu.VMEM)
+    total = len(upper_blocks(size, n)) * n
+    half = jax.ShapeDtypeStruct((total // 2, n), jnp.float32)
     return pl.pallas_call(
-        functools.partial(gram_kernel, divisor, n),
-        out_shape=(
-            jax.ShapeDtypeStruct((size, width), pieces[0].dtype),
-            jax.ShapeDtypeStruct((len(upper_blocks(size, n)) * n, n), jnp.float32),
-        ),
-        in_specs=[pl.BlockSpec(memory_space=pltpu.SMEM)] + [vmem] * len(pieces),
-        out_specs=(vmem, vmem),
+        functools.partial(gram_kernel, divisor, n, chunks),
+        out_shape=(half, half),
+        scratch_shapes=[pltpu.VMEM((size, width), pieces[0].dtype), pltpu.VMEM((total, n), jnp.float32)],
+        compiler_params=pltpu.CompilerParams(vmem_limit_bytes=32 * 1024 * 1024),
         name="local_gram",
-    )(place.reshape(1), *pieces)
-
-
-def factor_kernel(blocks_ref, basis_ref, cols_ref, tri_ref, out_ref, core_ref, high, middle, lower, work, one, two):
+    )(*pieces)
+
+
+def factor_kernel(chunks, fibers, *refs):
+    slots, refs = refs[: chunks // 2], refs[chunks // 2 :]
+    other_ref, basis_ref, refs = refs[0], refs[1], refs[2:]
+    pieces, refs = refs[:fibers], refs[fibers:]
+    tri_ref, out_ref, core_ref, blocks_ref, columns, high, middle, lower, work, one, two = refs
     size = tri_ref.shape[0]
     n = basis_ref.shape[1]
+    in_row_order(pieces, columns)
+    place = plane_place()
+    rows = slots[0].shape[0]
+    for slot in range(chunks):
+        start = pl.multiple_of(lax.bitwise_xor(place, slot) * rows, rows)
+        at = slot % (chunks // 2)
+        if slot < chunks // 2:
+            blocks_ref[pl.ds(start, rows), :] = slots[at][...]
+        else:
+            blocks_ref[pl.ds(start, rows), :] = other_ref[at * rows : (at + 1) * rows, :]
     phases = size // n
     part = [slice(i * n, (i + 1) * n) for i in range(phases)]
     for b, (i, j) in enumerate(upper_blocks(size, n)):
@@ -202,19 +286,23 @@
             if phase % 2 == 1:
                 basis = wide
     out_ref[...] = basis
-    core_ref[...] = dot(basis.astype(jnp.bfloat16), cols_ref[...], TN).astype(jnp.bfloat16)
-
-
-def factor(blocks, basis, columns):
+    core_ref[...] = dot(basis.astype(jnp.bfloat16), columns[...], TN).astype(jnp.bfloat16)
+
+
+def factor(slots, other, basis, pieces):
     size, n = basis.shape
+    width = pieces[0].shape[1]
+    chunks = 2 * len(slots)
     return pl.pallas_call(
-        factor_kernel,
+        functools.partial(factor_kernel, chunks, len(pieces)),
         out_shape=(
             jax.ShapeDtypeStruct((size, size), jnp.float32),
             jax.ShapeDtypeStruct((size, n), jnp.float32),
-            jax.ShapeDtypeStruct((n, columns.shape[1]), jnp.bfloat16),
+            jax.ShapeDtypeStruct((n, width), jnp.bfloat16),
         ),
         scratch_shapes=[
+            pltpu.VMEM((2 * other.shape[0], n), jnp.float32),
+            pltpu.VMEM((size, width), jnp.bfloat16),
             pltpu.VMEM((size, size), jnp.bfloat16),
             pltpu.VMEM((size, size), jnp.bfloat16),
             pltpu.VMEM((size, size), jnp.bfloat16),
@@ -224,82 +312,52 @@
         ],
         compiler_params=pltpu.CompilerParams(vmem_limit_bytes=32 * 1024 * 1024),
         name="factor",
-    )(blocks, basis, columns)
-
-
-class Group:
-    def __init__(self, bits):
-        self.axes = tuple(dict.fromkeys(axis for axis, _ in bits))
-        self.bits = bits
-        self.size = 2 ** len(bits)
-        self.me = 0
-        for b, (axis, distance) in enumerate(bits):
-            self.me = self.me + (((lax.axis_index(axis) // distance) % 2) << b)
-
-    def swap(self, value, change):
-        sizes = [lax.axis_size(axis) for axis in self.axes]
-        pairs = []
-        for source, place in enumerate(np.ndindex(*sizes)):
-            place = list(place)
-            for b, (axis, distance) in enumerate(self.bits):
-                if (change >> b) & 1:
-                    place[self.axes.index(axis)] ^= distance
-            pairs.append((source, int(np.ravel_multi_index(place, sizes))))
-        return lax.ppermute(value, self.axes, pairs)
-
-    def scatter_sum(self, value):
-        part = value.shape[0] // self.size
-        got = [
-            self.swap(lax.dynamic_slice_in_dim(value, (self.me ^ d) * part, part, 0), d)
-            for d in range(1, self.size)
+    )(*slots, other, basis, *pieces)
+
+
+def swap(value, bits, change):
+    axes = tuple(dict.fromkeys(axis for axis, _ in bits))
+    sizes = [lax.axis_size(axis) for axis in axes]
+    pairs = []
+    for source, place in enumerate(np.ndindex(*sizes)):
+        place = list(place)
+        for b, (axis, distance) in enumerate(reversed(bits)):
+            if (change >> b) & 1:
+                place[axes.index(axis)] ^= distance
+        pairs.append((source, int(np.ravel_multi_index(place, sizes))))
+    return lax.ppermute(value, axes, pairs)
+
+
+def sum_over_devices(kept, sent):
+    first, *groups = plane_groups()
+    value = kept + swap(sent, first, 1)
+    for bits in groups:
+        part = value.shape[0] >> len(bits)
+        cuts = [value[d * part : (d + 1) * part] for d in range(1 << len(bits))]
+        value = sum([swap(cuts[d], bits, d) for d in range(1, len(cuts))], cuts[0])
+    for bit in axis_bits("af"):
+        value = value + swap(value, [bit], 1)
+    slots = [value]
+    for bits in reversed(groups):
+        whole = jnp.concatenate(slots, axis=0) if len(slots) > 1 else slots[0]
+        slots = slots + [
+            piece
+            for d in range(1, 1 << len(bits))
+            for piece in jnp.split(swap(whole, bits, d), len(slots), axis=0)
         ]
-        return sum(got, lax.dynamic_slice_in_dim(value, self.me * part, part, 0))
-
-    def gather(self, value):
-        got = [value] + [self.swap(value, d) for d in range(1, self.size)]
-        whole = jnp.zeros((self.size, *value.shape), value.dtype)
-        for d in range(self.size):
-            whole = lax.dynamic_update_slice_in_dim(whole, got[d][None], self.me ^ d, 0)
-        return whole.reshape(self.size * value.shape[0], *value.shape[1:])
-
-
-def axis_bits(axis):
-    size = lax.axis_size(axis)
-    assert size & (size - 1) == 0, axis
-    return [(axis, 1 << b) for b in range(size.bit_length() - 1)]
-
-
-def reduce_all(value):
-    first, *rest = axis_bits("gy") + axis_bits("gz")
-    groups = [Group([first])] + [Group(rest[b : b + 2]) for b in range(0, len(rest), 2)]
-    for group in groups:
-        value = group.scatter_sum(value)
-    for bit in axis_bits("af"):
-        value = value + Group([bit]).swap(value, 1)
-    for group in reversed(groups):
-        value = group.gather(value)
-    return value
+    return slots, swap(jnp.concatenate(slots, axis=0), first, 1)
 
 
 def on_device(slab, block_owner, basis_init):
     fibers = lax.axis_size("af")
-    block_cols = slab.shape[1] // fibers
-    owners = block_owner.reshape(fibers)
-    labels = jnp.arange(fibers, dtype=jnp.int32)
-    onehot = (owners[:, None] == labels[None, :]).astype(jnp.int32)
-    source = jnp.sum(onehot * labels[:, None], axis=0)
-    along = Group(axis_bits("af"))
-
-    def block_of(distance):
-        start = source[along.me ^ distance] * block_cols
-        return lax.dynamic_slice_in_dim(slab, start, block_cols, 1)
-
-    pieces = [block_of(0)]
-    for distance in range(1, fibers):
-        pieces.append(along.swap(block_of(distance), distance))
-    devices_all = fibers * lax.axis_size("gy") * lax.axis_size("gz")
-    columns, blocks = local_gram(along.me, pieces, block_cols * devices_all, basis_init.shape[1])
-    return factor(reduce_all(blocks), basis_init, columns)
+    chunks = lax.axis_size("gy") * lax.axis_size("gz")
+    along = axis_bits("af")
+    pieces = pick_blocks(block_owner, slab)
+    pieces = [pieces[0]] + [swap(pieces[d], along[::-1], d) for d in range(1, fibers)]
+    divisor = pieces[0].shape[1] * fibers * chunks
+    kept, sent = local_gram(pieces, divisor, basis_init.shape[1], chunks)
+    slots, other = sum_over_devices(kept, sent)
+    return factor(slots, other, basis_init, pieces)
 
 
 def solution(mesh):

time: 79 us -> 87.1 us (1.10)
  Pallas kernels: 24.5 us -> 40.4 us
  waiting for transfers between devices: 31.6 us -> 26.8 us
  local copies, waits for them, and re-layouts: 5 us -> 0.93 us
  starting transfers between devices: 14 us -> 18 us
  between operations: 3.51 us -> 0.71 us
    pallas_call x2 -> x3, Pallas kernels: 24.5 us -> 40.4 us  [the longest x1 22.1 us: factor(): pl.pallas_call(functools.partial(factor_kernel, chunks, len(pieces)), out...]
    ppermute x13, waiting for transfers between devices: 31.6 us -> 26.8 us  [swap(): return lax.ppermute(value, axes, pairs)]
    ppermute x13, starting transfers between devices: 14 us -> 18 us  [swap(): return lax.ppermute(value, axes, pairs)]
    dynamic_slice x4 -> x0, local copies, waits for them, and re-layouts: 3.53 us -> none  [the longest x1 1.81 us: block_of(): return lax.dynamic_slice_in_dim(slab, start, block_cols, 1)]
  transfers between devices with their start and end apart: 13 -> 13, of which waited for: 13 -> 11; matrix products, arithmetic and copies ran while one was open for 0% -> 0% of each run, Pallas kernels for 0% -> 0%
where the time goes in v3:
time: 87.1 us; the launch traced here: 86.9 us
  Pallas kernels  40.4 us (46%)
  waiting for transfers between devices  26.8 us (31%)
  starting transfers between devices  18 us (21%)
  local copies, waits for them, and re-layouts  0.93 us (1%)
    ppermute x13, waiting for transfers between devices, swap(): return lax.ppermute(value, axes, pairs)  26.8 us
    pallas_call x1, Pallas kernels, factor(): pl.pallas_call(functools.partial(factor_kernel, chunks, len(pieces)), out...  22.1 us
    ppermute x13, starting transfers between devices, swap(): return lax.ppermute(value, axes, pairs)  18 us
    pallas_call x1, Pallas kernels, pick_blocks(): pl.pallas_call(pick_kernel, out_shape=(piece,) * fibers, in_specs=[pl.Blo...  17.7 us
  transfers between devices with their start and end apart: 13, of which 11 were waited for; matrix products, arithmetic and copies ran while one was open for 0% of the time, Pallas kernels for 0%

profile of v3, /device:TPU:0, one launch (start us, length us, event | category | flops | bytes accessed | tf_op | source)
XLA Modules:
  0.0 86.9 jit_solution(2081662265271647847)
XLA Ops:
  0.6 17.7 %pick_blocks.1 = (bf16[128,512]{1,0:T(8,128)(2,1)}, bf16[128,512]{1,0:T(8,128)(2,1)}, bf16[128,512]{1,0:T(8,128)(2,1)}, bf16[128,512]{1,0:T(8,128)(2,1)}) custom-call(s32[1,1,4]{2,1,0:T(1,128)} %owner_ref.1, bf16[128,2048]{1,0:T(8,128)(2,1)} %slab_ref.1), custom_call_target="tpu_custom_call" | custom-call | tf_op jit(solution)/shard_map/pick_blocks/pallas_call | solution.py:170
  18.3 3.1 %collective-permute-start = (bf16[128,512]{1,0:T(8,128)(2,1)}, bf16[128,512]{1,0:T(8,128)(2,1)S(1)}, u32[]{:S(2)}, u32[]{:S(2)}) collective-permute-start(bf16[128,512]{1,0:T(8,128)(2,1)} %get-tuple-element.10), channel_id=1, source_target_pairs={{0,8},{8,0},{16,24},{24,16},{1,9},{9,1},{17,25},{25,17},{2,10},{10... | collective-permute-start | bytes 393224 | tf_op jit(solution)/shard_map/ppermute | solution.py:328
  21.4 2.6 %collective-permute-start.1 = (bf16[128,512]{1,0:T(8,128)(2,1)}, bf16[128,512]{1,0:T(8,128)(2,1)S(1)}, u32[]{:S(2)}, u32[]{:S(2)}) collective-permute-start(bf16[128,512]{1,0:T(8,128)(2,1)} %get-tuple-element.11), channel_id=1, source_target_pairs={{0,16},{8,24},{16,0},{24,8},{1,17},{9,25},{17,1},{25,9},{2,18},{10... | collective-permute-start | bytes 393224 | tf_op jit(solution)/shard_map/ppermute | solution.py:328
  24.0 0.0 collective-permute-start.2
  24.0 2.6 %collective-permute-done.refs_1_.refs_7_ = bf16[128,512]{1,0:T(8,128)(2,1)S(1)} collective-permute-done((bf16[128,512]{1,0:T(8,128)(2,1)}, bf16[128,512]{1,0:T(8,128)(2,1)S(1)}, u32[]{:S(2)}, u32[]{:S(2)}) %collective-permute-start) | collective-permute-done | bytes 131104 | tf_op jit(solution)/shard_map/ppermute | solution.py:328
  26.7 7.9 %collective-permute-done.1.refs_2_.refs_8_ = bf16[128,512]{1,0:T(8,128)(2,1)S(1)} collective-permute-done((bf16[128,512]{1,0:T(8,128)(2,1)}, bf16[128,512]{1,0:T(8,128)(2,1)S(1)}, u32[]{:S(2)}, u32[]{:S(2)}) %collective-permute-start.1) | collective-permute-done | bytes 131104 | tf_op jit(solution)/shard_map/ppermute | solution.py:328
  34.6 0.0 collective-permute-done.2.refs_3_.refs_9_
  34.6 0.0 copy-start
  34.6 0.9 %copy-done = bf16[128,512]{1,0:T(8,128)(2,1)S(1)} copy-done((bf16[128,512]{1,0:T(8,128)(2,1)S(1)}, bf16[128,512]{1,0:T(8,128)(2,1)}, u32[]{:S(2)}) %copy-start) | copy-done | bytes 131096
  35.5 0.6 local_gram.1
  36.1 0.1 collective-permute-start.3
  36.2 1.6 %collective-permute-done.3 = f32[640,128]{1,0:T(8,128)S(1)} collective-permute-done((f32[640,128]{1,0:T(8,128)S(1)}, f32[640,128]{1,0:T(8,128)S(1)}, u32[]{:S(2)}, u32[]{:S(2)}) %collective-permute-start.3) | collective-permute-done | bytes 327712 | tf_op jit(solution)/shard_map/ppermute | solution.py:328
  37.8 1.6 %collective-permute-start.4 = (f32[160,128]{1,0:T(8,128)S(1)}, f32[160,128]{1,0:T(8,128)S(1)}, u32[]{:S(2)}, u32[]{:S(2)}) collective-permute-start(f32[160,128]{1,0:T(8,128)S(1)} %get-tuple-element.15), channel_id=1, source_target_pairs={{0,1},{1,0},{2,3},{3,2},{4,5},{5,4},{6,7},{7,6},{8,9},{9,8},{10,11... | collective-permute-start | bytes 245768 | tf_op jit(solution)/shard_map/ppermute | solution.py:328
  39.4 1.4 %collective-permute-start.6 = (f32[160,128]{1,0:T(8,128)S(1)}, f32[160,128]{1,0:T(8,128)S(1)}, u32[]{:S(2)}, u32[]{:S(2)}) collective-permute-start(f32[160,128]{1,0:T(8,128)S(1)} %get-tuple-element.16), channel_id=1, source_target_pairs={{0,5},{1,4},{2,7},{3,6},{4,1},{5,0},{6,3},{7,2},{8,13},{9,12},{10,... | collective-permute-start | bytes 245768 | tf_op jit(solution)/shard_map/ppermute | solution.py:328
  40.9 0.5 collective-permute-start.5
  41.4 1.3 %collective-permute-done.4 = f32[160,128]{1,0:T(8,128)S(1)} collective-permute-done((f32[160,128]{1,0:T(8,128)S(1)}, f32[160,128]{1,0:T(8,128)S(1)}, u32[]{:S(2)}, u32[]{:S(2)}) %collective-permute-start.4) | collective-permute-done | bytes 81952 | tf_op jit(solution)/shard_map/ppermute | solution.py:328
  42.7 2.9 %collective-permute-done.6 = f32[160,128]{1,0:T(8,128)S(1)} collective-permute-done((f32[160,128]{1,0:T(8,128)S(1)}, f32[160,128]{1,0:T(8,128)S(1)}, u32[]{:S(2)}, u32[]{:S(2)}) %collective-permute-start.6) | collective-permute-done | bytes 81952 | tf_op jit(solution)/shard_map/ppermute | solution.py:328
  45.5 0.0 collective-permute-done.5
  45.6 2.0 %collective-permute-start.7 = (f32[160,128]{1,0:T(8,128)S(1)}, f32[160,128]{1,0:T(8,128)S(1)}, u32[]{:S(2)}, u32[]{:S(2)}) collective-permute-start(f32[160,128]{1,0:T(8,128)S(1)} %fusion.1), channel_id=1, source_target_pairs={{0,8},{8,0},{16,24},{24,16},{1,9},{9,1},{17,25},{25,17},{2,10},{10... | collective-permute-start | bytes 245768 | tf_op jit(solution)/shard_map/ppermute | solution.py:328
  47.6 2.5 %collective-permute-done.7 = f32[160,128]{1,0:T(8,128)S(1)} collective-permute-done((f32[160,128]{1,0:T(8,128)S(1)}, f32[160,128]{1,0:T(8,128)S(1)}, u32[]{:S(2)}, u32[]{:S(2)}) %collective-permute-start.7) | collective-permute-done | bytes 81952 | tf_op jit(solution)/shard_map/ppermute | solution.py:328
  50.1 3.0 %collective-permute-start.8 = (f32[160,128]{1,0:T(8,128)S(1)}, f32[160,128]{1,0:T(8,128)S(1)}, u32[]{:S(2)}, u32[]{:S(2)}) collective-permute-start(f32[160,128]{1,0:T(8,128)S(1)} %add.22), channel_id=1, source_target_pairs={{0,16},{8,24},{16,0},{24,8},{1,17},{9,25},{17,1},{25,9},{2,18},{10... | collective-permute-start | bytes 245768 | tf_op jit(solution)/shard_map/ppermute | solution.py:328
  53.1 2.4 %collective-permute-done.8 = f32[160,128]{1,0:T(8,128)S(1)} collective-permute-done((f32[160,128]{1,0:T(8,128)S(1)}, f32[160,128]{1,0:T(8,128)S(1)}, u32[]{:S(2)}, u32[]{:S(2)}) %collective-permute-start.8) | collective-permute-done | bytes 81952 | tf_op jit(solution)/shard_map/ppermute | solution.py:328
  55.6 0.0 copy-start.1
  55.6 2.3 %collective-permute-start.11 = (f32[160,128]{1,0:T(8,128)S(1)}, f32[160,128]{1,0:T(8,128)S(1)}, u32[]{:S(2)}, u32[]{:S(2)}) collective-permute-start(f32[160,128]{1,0:T(8,128)S(1)} %add.23.refs_0_), channel_id=1, source_target_pairs={{0,5},{1,4},{2,7},{3,6},{4,1},{5,0},{6,3},{7,2},{8,13},{9,12},{10,... | collective-permute-start | bytes 245768 | tf_op jit(solution)/shard_map/ppermute | solution.py:328
  57.9 0.8 collective-permute-start.10
  58.6 0.5 collective-permute-start.9
  59.1 1.9 %collective-permute-done.11.refs_3_ = f32[160,128]{1,0:T(8,128)S(1)} collective-permute-done((f32[160,128]{1,0:T(8,128)S(1)}, f32[160,128]{1,0:T(8,128)S(1)}, u32[]{:S(2)}, u32[]{:S(2)}) %collective-permute-start.11) | collective-permute-done | bytes 81952 | tf_op jit(solution)/shard_map/ppermute | solution.py:328
  61.0 1.3 %collective-permute-done.10.refs_2_ = f32[160,128]{1,0:T(8,128)S(1)} collective-permute-done((f32[160,128]{1,0:T(8,128)S(1)}, f32[160,128]{1,0:T(8,128)S(1)}, u32[]{:S(2)}, u32[]{:S(2)}) %collective-permute-start.10) | collective-permute-done | bytes 81952 | tf_op jit(solution)/shard_map/ppermute | solution.py:328
  62.3 0.8 collective-permute-done.9.refs_1_
  63.1 0.1 collective-permute-start.12
  63.2 1.6 %collective-permute-done.12.refs_4_ = f32[640,128]{1,0:T(8,128)S(1)} collective-permute-done((f32[640,128]{1,0:T(8,128)S(1)}, f32[640,128]{1,0:T(8,128)S(1)}, u32[]{:S(2)}, u32[]{:S(2)}) %collective-permute-start.12) | collective-permute-done | bytes 327712 | tf_op jit(solution)/shard_map/ppermute | solution.py:328
  64.8 0.0 copy-done.1
  64.8 22.1 %factor.1 = (f32[512,512]{1,0:T(8,128)}, f32[512,128]{1,0:T(8,128)}, bf16[128,512]{1,0:T(8,128)(2,1)}) custom-call(f32[160,128]{1,0:T(8,128)S(1)} %add.23.refs_0_, f32[160,128]{1,0:T(8,128)S(1)} %collective-permute-done.9.refs_1_, f32[160,128]{1,0:T(8,128)S(1)} %collective-permute-done.10.refs_2_, f32[160,128]{1,0:T(8,128)S(1)} %collective-permute-done.11.refs_3_, ...), custom_call_target="tpu_custom_call" | custom-call | tf_op jit(solution)/shard_map/factor/pallas_call | solution.py:296
  (6 shorter events, 0.1 us)
Async XLA Ops:
  18.3 8.3 %collective-permute-start = (bf16[128,512]{1,0:T(8,128)(2,1)}, bf16[128,512]{1,0:T(8,128)(2,1)S(1)}, u32[]{:S(2)}, u32[]{:S(2)}) collective-permute-start(bf16[128,512]{1,0:T(8,128)(2,1)} %get-tuple-element.10), channel_id=1, source_target_pairs={{0,8},{8,0},{16,24},{24,16},{1,9},{9,1},{17,25},{25,17},{2,10},{10... | collective-permute-start | bytes 393224 | tf_op jit(solution)/shard_map/ppermute | solution.py:328
  21.4 13.1 %collective-permute-start.1 = (bf16[128,512]{1,0:T(8,128)(2,1)}, bf16[128,512]{1,0:T(8,128)(2,1)S(1)}, u32[]{:S(2)}, u32[]{:S(2)}) collective-permute-start(bf16[128,512]{1,0:T(8,128)(2,1)} %get-tuple-element.11), channel_id=1, source_target_pairs={{0,16},{8,24},{16,0},{24,8},{1,17},{9,25},{17,1},{25,9},{2,18},{10... | collective-permute-start | bytes 393224 | tf_op jit(solution)/shard_map/ppermute | solution.py:328
  24.0 10.6 %collective-permute-start.2 = (bf16[128,512]{1,0:T(8,128)(2,1)}, bf16[128,512]{1,0:T(8,128)(2,1)S(1)}, u32[]{:S(2)}, u32[]{:S(2)}) collective-permute-start(bf16[128,512]{1,0:T(8,128)(2,1)} %get-tuple-element.12), channel_id=1, source_target_pairs={{0,24},{8,16},{16,8},{24,0},{1,25},{9,17},{17,9},{25,1},{2,26},{10... | collective-permute-start | bytes 393224 | tf_op jit(solution)/shard_map/ppermute | solution.py:328
  34.6 0.9 %copy-start = (bf16[128,512]{1,0:T(8,128)(2,1)S(1)}, bf16[128,512]{1,0:T(8,128)(2,1)}, u32[]{:S(2)}) copy-start(bf16[128,512]{1,0:T(8,128)(2,1)} %get-tuple-element.9.refs_0_.refs_6_) | copy-start | bytes 393220
  36.1 1.7 %collective-permute-start.3 = (f32[640,128]{1,0:T(8,128)S(1)}, f32[640,128]{1,0:T(8,128)S(1)}, u32[]{:S(2)}, u32[]{:S(2)}) collective-permute-start(f32[640,128]{1,0:T(8,128)S(1)} %get-tuple-element.14), channel_id=1, source_target_pairs={{0,2},{2,0},{4,6},{6,4},{1,3},{3,1},{5,7},{7,5},{8,10},{10,8},{12,... | collective-permute-start | bytes 983048 | tf_op jit(solution)/shard_map/ppermute | solution.py:328
  37.8 4.8 %collective-permute-start.4 = (f32[160,128]{1,0:T(8,128)S(1)}, f32[160,128]{1,0:T(8,128)S(1)}, u32[]{:S(2)}, u32[]{:S(2)}) collective-permute-start(f32[160,128]{1,0:T(8,128)S(1)} %get-tuple-element.15), channel_id=1, source_target_pairs={{0,1},{1,0},{2,3},{3,2},{4,5},{5,4},{6,7},{7,6},{8,9},{9,8},{10,11... | collective-permute-start | bytes 245768 | tf_op jit(solution)/shard_map/ppermute | solution.py:328
  39.4 6.1 %collective-permute-start.6 = (f32[160,128]{1,0:T(8,128)S(1)}, f32[160,128]{1,0:T(8,128)S(1)}, u32[]{:S(2)}, u32[]{:S(2)}) collective-permute-start(f32[160,128]{1,0:T(8,128)S(1)} %get-tuple-element.16), channel_id=1, source_target_pairs={{0,5},{1,4},{2,7},{3,6},{4,1},{5,0},{6,3},{7,2},{8,13},{9,12},{10,... | collective-permute-start | bytes 245768 | tf_op jit(solution)/shard_map/ppermute | solution.py:328
  40.9 4.7 %collective-permute-start.5 = (f32[160,128]{1,0:T(8,128)S(1)}, f32[160,128]{1,0:T(8,128)S(1)}, u32[]{:S(2)}, u32[]{:S(2)}) collective-permute-start(f32[160,128]{1,0:T(8,128)S(1)} %get-tuple-element.17), channel_id=1, source_target_pairs={{0,4},{1,5},{2,6},{3,7},{4,0},{5,1},{6,2},{7,3},{8,12},{9,13},{10,... | collective-permute-start | bytes 245768 | tf_op jit(solution)/shard_map/ppermute | solution.py:328
  45.6 4.5 %collective-permute-start.7 = (f32[160,128]{1,0:T(8,128)S(1)}, f32[160,128]{1,0:T(8,128)S(1)}, u32[]{:S(2)}, u32[]{:S(2)}) collective-permute-start(f32[160,128]{1,0:T(8,128)S(1)} %fusion.1), channel_id=1, source_target_pairs={{0,8},{8,0},{16,24},{24,16},{1,9},{9,1},{17,25},{25,17},{2,10},{10... | collective-permute-start | bytes 245768 | tf_op jit(solution)/shard_map/ppermute | solution.py:328
  50.1 5.5 %collective-permute-start.8 = (f32[160,128]{1,0:T(8,128)S(1)}, f32[160,128]{1,0:T(8,128)S(1)}, u32[]{:S(2)}, u32[]{:S(2)}) collective-permute-start(f32[160,128]{1,0:T(8,128)S(1)} %add.22), channel_id=1, source_target_pairs={{0,16},{8,24},{16,0},{24,8},{1,17},{9,25},{17,1},{25,9},{2,18},{10... | collective-permute-start | bytes 245768 | tf_op jit(solution)/shard_map/ppermute | solution.py:328
  55.6 9.2 %copy-start.1 = (f32[512,128]{1,0:T(8,128)S(1)}, f32[512,128]{1,0:T(8,128)}, u32[]{:S(2)}) copy-start(f32[512,128]{1,0:T(8,128)} %refs_5_.1) | copy-start | bytes 786436
  55.6 5.4 %collective-permute-start.11 = (f32[160,128]{1,0:T(8,128)S(1)}, f32[160,128]{1,0:T(8,128)S(1)}, u32[]{:S(2)}, u32[]{:S(2)}) collective-permute-start(f32[160,128]{1,0:T(8,128)S(1)} %add.23.refs_0_), channel_id=1, source_target_pairs={{0,5},{1,4},{2,7},{3,6},{4,1},{5,0},{6,3},{7,2},{8,13},{9,12},{10,... | collective-permute-start | bytes 245768 | tf_op jit(solution)/shard_map/ppermute | solution.py:328
  57.9 4.4 %collective-permute-start.10 = (f32[160,128]{1,0:T(8,128)S(1)}, f32[160,128]{1,0:T(8,128)S(1)}, u32[]{:S(2)}, u32[]{:S(2)}) collective-permute-start(f32[160,128]{1,0:T(8,128)S(1)} %add.23.refs_0_), channel_id=1, source_target_pairs={{0,4},{1,5},{2,6},{3,7},{4,0},{5,1},{6,2},{7,3},{8,12},{9,13},{10,... | collective-permute-start | bytes 245768 | tf_op jit(solution)/shard_map/ppermute | solution.py:328
  58.6 4.4 %collective-permute-start.9 = (f32[160,128]{1,0:T(8,128)S(1)}, f32[160,128]{1,0:T(8,128)S(1)}, u32[]{:S(2)}, u32[]{:S(2)}) collective-permute-start(f32[160,128]{1,0:T(8,128)S(1)} %add.23.refs_0_), channel_id=1, source_target_pairs={{0,1},{1,0},{2,3},{3,2},{4,5},{5,4},{6,7},{7,6},{8,9},{9,8},{10,11... | collective-permute-start | bytes 245768 | tf_op jit(solution)/shard_map/ppermute | solution.py:328
  63.1 1.7 %collective-permute-start.12 = (f32[640,128]{1,0:T(8,128)S(1)}, f32[640,128]{1,0:T(8,128)S(1)}, u32[]{:S(2)}, u32[]{:S(2)}) collective-permute-start(f32[640,128]{1,0:T(8,128)S(1)} %pad_maximum_fusion), channel_id=1, source_target_pairs={{0,2},{2,0},{4,6},{6,4},{1,3},{3,1},{5,7},{7,5},{8,10},{10,8},{12,... | collective-permute-start | bytes 983048 | tf_op jit(solution)/shard_map/ppermute | solution.py:328

commit v4 on v3

--- a/solution.py
+++ b/solution.py
@@ -143,25 +143,15 @@
     return lax.axis_index("af")
 
 
-def pick_kernel(owner_ref, slab_ref, *refs):
-    pieces, sems = refs[:-1], refs[-1]
+def pick_kernel(owner_ref, slab_ref, *pieces):
     fibers = len(pieces)
     width = pieces[0].shape[1]
     me = fiber_place()
-    copies = []
-    for distance in range(fibers):
+    for distance, piece in enumerate(pieces):
         block = 0
         for b in range(fibers):
-            mine = owner_ref[0, 0, b] == lax.bitwise_xor(me, distance)
-            block = jnp.where(mine, b, block)
-        start = pl.multiple_of(block * width, width)
-        copies.append(
-            pltpu.make_async_copy(slab_ref.at[:, pl.ds(start, width)], pieces[distance], sems.at[distance])
-        )
-    for copy in copies:
-        copy.start()
-    for copy in copies:
-        copy.wait()
+            block = jnp.where(owner_ref[0, 0, b] == lax.bitwise_xor(me, distance), b, block)
+        piece[...] = slab_ref[:, pl.ds(pl.multiple_of(block * width, width), width)]
 
 
 def pick_blocks(owners, slab):
@@ -170,9 +160,7 @@
     return pl.pallas_call(
         pick_kernel,
         out_shape=(piece,) * fibers,
-        in_specs=[pl.BlockSpec(memory_space=pltpu.SMEM), pl.BlockSpec(memory_space=pl.ANY)],
-        out_specs=(pl.BlockSpec(memory_space=pl.ANY),) * fibers,
-        scratch_shapes=[pltpu.SemaphoreType.DMA((fibers,))],
+        in_specs=[pl.BlockSpec(memory_space=pltpu.SMEM), pl.BlockSpec(memory_space=pltpu.VMEM)],
         name="pick_blocks",
     )(owners, slab)
 

time: 87.1 us -> 71.2 us (0.82)
  Pallas kernels: 40.4 us -> 24.6 us
    pallas_call x1, Pallas kernels: 17.7 us -> 1.89 us  [pick_blocks(): pl.pallas_call(pick_kernel, out_shape=(piece,) * fibers, in_specs=[pl.Blo...]
where the time goes in v4:
time: 71.2 us; the launch traced here: 71 us
  waiting for transfers between devices  26.8 us (38%)
  Pallas kernels  24.6 us (35%)
  starting transfers between devices  17.9 us (25%)
  local copies, waits for them, and re-layouts  0.93 us (1%)
    ppermute x13, waiting for transfers between devices, swap(): return lax.ppermute(value, axes, pairs)  26.8 us
    pallas_call x1, Pallas kernels, factor(): pl.pallas_call(functools.partial(factor_kernel, chunks, len(pieces)), out...  22.1 us
    ppermute x13, starting transfers between devices, swap(): return lax.ppermute(value, axes, pairs)  17.9 us
    pallas_call x1, Pallas kernels, pick_blocks(): pl.pallas_call(pick_kernel, out_shape=(piece,) * fibers, in_specs=[pl.Blo...  1.89 us
  transfers between devices with their start and end apart: 13, of which 11 were waited for; matrix products, arithmetic and copies ran while one was open for 0% of the time, Pallas kernels for 0%

profile of v4, /device:TPU:0, one launch (start us, length us, event | category | flops | bytes accessed | tf_op | source)
XLA Modules:
  0.0 71.0 jit_solution(4904630792804720013)
XLA Ops:
  0.6 1.9 %pick_blocks.1 = (bf16[128,512]{1,0:T(8,128)(2,1)}, bf16[128,512]{1,0:T(8,128)(2,1)}, bf16[128,512]{1,0:T(8,128)(2,1)}, bf16[128,512]{1,0:T(8,128)(2,1)}) custom-call(s32[1,1,4]{2,1,0:T(1,128)} %owner_ref.1, bf16[128,2048]{1,0:T(8,128)(2,1)} %slab_ref.1), custom_call_target="tpu_custom_call" | custom-call | tf_op jit(solution)/shard_map/pick_blocks/pallas_call | solution.py:160
  2.5 3.0 %collective-permute-start = (bf16[128,512]{1,0:T(8,128)(2,1)}, bf16[128,512]{1,0:T(8,128)(2,1)S(1)}, u32[]{:S(2)}, u32[]{:S(2)}) collective-permute-start(bf16[128,512]{1,0:T(8,128)(2,1)} %get-tuple-element.10), channel_id=1, source_target_pairs={{0,8},{8,0},{16,24},{24,16},{1,9},{9,1},{17,25},{25,17},{2,10},{10... | collective-permute-start | bytes 393224 | tf_op jit(solution)/shard_map/ppermute | solution.py:316
  5.5 2.6 %collective-permute-start.1 = (bf16[128,512]{1,0:T(8,128)(2,1)}, bf16[128,512]{1,0:T(8,128)(2,1)S(1)}, u32[]{:S(2)}, u32[]{:S(2)}) collective-permute-start(bf16[128,512]{1,0:T(8,128)(2,1)} %get-tuple-element.11), channel_id=1, source_target_pairs={{0,16},{8,24},{16,0},{24,8},{1,17},{9,25},{17,1},{25,9},{2,18},{10... | collective-permute-start | bytes 393224 | tf_op jit(solution)/shard_map/ppermute | solution.py:316
  8.1 0.0 collective-permute-start.2
  8.1 2.6 %collective-permute-done.refs_1_.refs_7_ = bf16[128,512]{1,0:T(8,128)(2,1)S(1)} collective-permute-done((bf16[128,512]{1,0:T(8,128)(2,1)}, bf16[128,512]{1,0:T(8,128)(2,1)S(1)}, u32[]{:S(2)}, u32[]{:S(2)}) %collective-permute-start) | collective-permute-done | bytes 131104 | tf_op jit(solution)/shard_map/ppermute | solution.py:316
  10.8 7.9 %collective-permute-done.1.refs_2_.refs_8_ = bf16[128,512]{1,0:T(8,128)(2,1)S(1)} collective-permute-done((bf16[128,512]{1,0:T(8,128)(2,1)}, bf16[128,512]{1,0:T(8,128)(2,1)S(1)}, u32[]{:S(2)}, u32[]{:S(2)}) %collective-permute-start.1) | collective-permute-done | bytes 131104 | tf_op jit(solution)/shard_map/ppermute | solution.py:316
  18.7 0.0 collective-permute-done.2.refs_3_.refs_9_
  18.7 0.0 copy-start
  18.7 0.9 %copy-done = bf16[128,512]{1,0:T(8,128)(2,1)S(1)} copy-done((bf16[128,512]{1,0:T(8,128)(2,1)S(1)}, bf16[128,512]{1,0:T(8,128)(2,1)}, u32[]{:S(2)}) %copy-start) | copy-done | bytes 131096
  19.6 0.6 local_gram.1
  20.2 0.1 collective-permute-start.3
  20.3 1.6 %collective-permute-done.3 = f32[640,128]{1,0:T(8,128)S(1)} collective-permute-done((f32[640,128]{1,0:T(8,128)S(1)}, f32[640,128]{1,0:T(8,128)S(1)}, u32[]{:S(2)}, u32[]{:S(2)}) %collective-permute-start.3) | collective-permute-done | bytes 327712 | tf_op jit(solution)/shard_map/ppermute | solution.py:316
  21.9 1.6 %collective-permute-start.4 = (f32[160,128]{1,0:T(8,128)S(1)}, f32[160,128]{1,0:T(8,128)S(1)}, u32[]{:S(2)}, u32[]{:S(2)}) collective-permute-start(f32[160,128]{1,0:T(8,128)S(1)} %get-tuple-element.15), channel_id=1, source_target_pairs={{0,1},{1,0},{2,3},{3,2},{4,5},{5,4},{6,7},{7,6},{8,9},{9,8},{10,11... | collective-permute-start | bytes 245768 | tf_op jit(solution)/shard_map/ppermute | solution.py:316
  23.5 1.4 %collective-permute-start.6 = (f32[160,128]{1,0:T(8,128)S(1)}, f32[160,128]{1,0:T(8,128)S(1)}, u32[]{:S(2)}, u32[]{:S(2)}) collective-permute-start(f32[160,128]{1,0:T(8,128)S(1)} %get-tuple-element.16), channel_id=1, source_target_pairs={{0,5},{1,4},{2,7},{3,6},{4,1},{5,0},{6,3},{7,2},{8,13},{9,12},{10,... | collective-permute-start | bytes 245768 | tf_op jit(solution)/shard_map/ppermute | solution.py:316
  25.0 0.5 collective-permute-start.5
  25.5 1.3 %collective-permute-done.4 = f32[160,128]{1,0:T(8,128)S(1)} collective-permute-done((f32[160,128]{1,0:T(8,128)S(1)}, f32[160,128]{1,0:T(8,128)S(1)}, u32[]{:S(2)}, u32[]{:S(2)}) %collective-permute-start.4) | collective-permute-done | bytes 81952 | tf_op jit(solution)/shard_map/ppermute | solution.py:316
  26.8 2.9 %collective-permute-done.6 = f32[160,128]{1,0:T(8,128)S(1)} collective-permute-done((f32[160,128]{1,0:T(8,128)S(1)}, f32[160,128]{1,0:T(8,128)S(1)}, u32[]{:S(2)}, u32[]{:S(2)}) %collective-permute-start.6) | collective-permute-done | bytes 81952 | tf_op jit(solution)/shard_map/ppermute | solution.py:316
  29.7 0.0 collective-permute-done.5
  29.7 2.0 %collective-permute-start.7 = (f32[160,128]{1,0:T(8,128)S(1)}, f32[160,128]{1,0:T(8,128)S(1)}, u32[]{:S(2)}, u32[]{:S(2)}) collective-permute-start(f32[160,128]{1,0:T(8,128)S(1)} %fusion.1), channel_id=1, source_target_pairs={{0,8},{8,0},{16,24},{24,16},{1,9},{9,1},{17,25},{25,17},{2,10},{10... | collective-permute-start | bytes 245768 | tf_op jit(solution)/shard_map/ppermute | solution.py:316
  31.7 2.5 %collective-permute-done.7 = f32[160,128]{1,0:T(8,128)S(1)} collective-permute-done((f32[160,128]{1,0:T(8,128)S(1)}, f32[160,128]{1,0:T(8,128)S(1)}, u32[]{:S(2)}, u32[]{:S(2)}) %collective-permute-start.7) | collective-permute-done | bytes 81952 | tf_op jit(solution)/shard_map/ppermute | solution.py:316
  34.2 3.0 %collective-permute-start.8 = (f32[160,128]{1,0:T(8,128)S(1)}, f32[160,128]{1,0:T(8,128)S(1)}, u32[]{:S(2)}, u32[]{:S(2)}) collective-permute-start(f32[160,128]{1,0:T(8,128)S(1)} %add.22), channel_id=1, source_target_pairs={{0,16},{8,24},{16,0},{24,8},{1,17},{9,25},{17,1},{25,9},{2,18},{10... | collective-permute-start | bytes 245768 | tf_op jit(solution)/shard_map/ppermute | solution.py:316
  37.3 2.4 %collective-permute-done.8 = f32[160,128]{1,0:T(8,128)S(1)} collective-permute-done((f32[160,128]{1,0:T(8,128)S(1)}, f32[160,128]{1,0:T(8,128)S(1)}, u32[]{:S(2)}, u32[]{:S(2)}) %collective-permute-start.8) | collective-permute-done | bytes 81952 | tf_op jit(solution)/shard_map/ppermute | solution.py:316
  39.7 0.0 copy-start.1
  39.7 2.3 %collective-permute-start.11 = (f32[160,128]{1,0:T(8,128)S(1)}, f32[160,128]{1,0:T(8,128)S(1)}, u32[]{:S(2)}, u32[]{:S(2)}) collective-permute-start(f32[160,128]{1,0:T(8,128)S(1)} %add.23.refs_0_), channel_id=1, source_target_pairs={{0,5},{1,4},{2,7},{3,6},{4,1},{5,0},{6,3},{7,2},{8,13},{9,12},{10,... | collective-permute-start | bytes 245768 | tf_op jit(solution)/shard_map/ppermute | solution.py:316
  42.0 0.8 %collective-permute-start.10 = (f32[160,128]{1,0:T(8,128)S(1)}, f32[160,128]{1,0:T(8,128)S(1)}, u32[]{:S(2)}, u32[]{:S(2)}) collective-permute-start(f32[160,128]{1,0:T(8,128)S(1)} %add.23.refs_0_), channel_id=1, source_target_pairs={{0,4},{1,5},{2,6},{3,7},{4,0},{5,1},{6,2},{7,3},{8,12},{9,13},{10,... | collective-permute-start | bytes 245768 | tf_op jit(solution)/shard_map/ppermute | solution.py:316
  42.8 0.5 collective-permute-start.9
  43.3 1.9 %collective-permute-done.11.refs_3_ = f32[160,128]{1,0:T(8,128)S(1)} collective-permute-done((f32[160,128]{1,0:T(8,128)S(1)}, f32[160,128]{1,0:T(8,128)S(1)}, u32[]{:S(2)}, u32[]{:S(2)}) %collective-permute-start.11) | collective-permute-done | bytes 81952 | tf_op jit(solution)/shard_map/ppermute | solution.py:316
  45.1 1.3 %collective-permute-done.10.refs_2_ = f32[160,128]{1,0:T(8,128)S(1)} collective-permute-done((f32[160,128]{1,0:T(8,128)S(1)}, f32[160,128]{1,0:T(8,128)S(1)}, u32[]{:S(2)}, u32[]{:S(2)}) %collective-permute-start.10) | collective-permute-done | bytes 81952 | tf_op jit(solution)/shard_map/ppermute | solution.py:316
  46.4 0.8 %collective-permute-done.9.refs_1_ = f32[160,128]{1,0:T(8,128)S(1)} collective-permute-done((f32[160,128]{1,0:T(8,128)S(1)}, f32[160,128]{1,0:T(8,128)S(1)}, u32[]{:S(2)}, u32[]{:S(2)}) %collective-permute-start.9) | collective-permute-done | bytes 81952 | tf_op jit(solution)/shard_map/ppermute | solution.py:316
  47.2 0.1 collective-permute-start.12
  47.3 1.6 %collective-permute-done.12.refs_4_ = f32[640,128]{1,0:T(8,128)S(1)} collective-permute-done((f32[640,128]{1,0:T(8,128)S(1)}, f32[640,128]{1,0:T(8,128)S(1)}, u32[]{:S(2)}, u32[]{:S(2)}) %collective-permute-start.12) | collective-permute-done | bytes 327712 | tf_op jit(solution)/shard_map/ppermute | solution.py:316
  48.9 0.0 copy-done.1
  48.9 22.1 %factor.1 = (f32[512,512]{1,0:T(8,128)}, f32[512,128]{1,0:T(8,128)}, bf16[128,512]{1,0:T(8,128)(2,1)}) custom-call(f32[160,128]{1,0:T(8,128)S(1)} %add.23.refs_0_, f32[160,128]{1,0:T(8,128)S(1)} %collective-permute-done.9.refs_1_, f32[160,128]{1,0:T(8,128)S(1)} %collective-permute-done.10.refs_2_, f32[160,128]{1,0:T(8,128)S(1)} %collective-permute-done.11.refs_3_, ...), custom_call_target="tpu_custom_call" | custom-call | tf_op jit(solution)/shard_map/factor/pallas_call | solution.py:284
  (6 shorter events, 0.1 us)
Async XLA Ops:
  2.5 8.3 %collective-permute-start = (bf16[128,512]{1,0:T(8,128)(2,1)}, bf16[128,512]{1,0:T(8,128)(2,1)S(1)}, u32[]{:S(2)}, u32[]{:S(2)}) collective-permute-start(bf16[128,512]{1,0:T(8,128)(2,1)} %get-tuple-element.10), channel_id=1, source_target_pairs={{0,8},{8,0},{16,24},{24,16},{1,9},{9,1},{17,25},{25,17},{2,10},{10... | collective-permute-start | bytes 393224 | tf_op jit(solution)/shard_map/ppermute | solution.py:316
  5.5 13.1 %collective-permute-start.1 = (bf16[128,512]{1,0:T(8,128)(2,1)}, bf16[128,512]{1,0:T(8,128)(2,1)S(1)}, u32[]{:S(2)}, u32[]{:S(2)}) collective-permute-start(bf16[128,512]{1,0:T(8,128)(2,1)} %get-tuple-element.11), channel_id=1, source_target_pairs={{0,16},{8,24},{16,0},{24,8},{1,17},{9,25},{17,1},{25,9},{2,18},{10... | collective-permute-start | bytes 393224 | tf_op jit(solution)/shard_map/ppermute | solution.py:316
  8.1 10.5 %collective-permute-start.2 = (bf16[128,512]{1,0:T(8,128)(2,1)}, bf16[128,512]{1,0:T(8,128)(2,1)S(1)}, u32[]{:S(2)}, u32[]{:S(2)}) collective-permute-start(bf16[128,512]{1,0:T(8,128)(2,1)} %get-tuple-element.12), channel_id=1, source_target_pairs={{0,24},{8,16},{16,8},{24,0},{1,25},{9,17},{17,9},{25,1},{2,26},{10... | collective-permute-start | bytes 393224 | tf_op jit(solution)/shard_map/ppermute | solution.py:316
  18.7 0.9 %copy-start = (bf16[128,512]{1,0:T(8,128)(2,1)S(1)}, bf16[128,512]{1,0:T(8,128)(2,1)}, u32[]{:S(2)}) copy-start(bf16[128,512]{1,0:T(8,128)(2,1)} %get-tuple-element.9.refs_0_.refs_6_) | copy-start | bytes 393220
  20.2 1.7 %collective-permute-start.3 = (f32[640,128]{1,0:T(8,128)S(1)}, f32[640,128]{1,0:T(8,128)S(1)}, u32[]{:S(2)}, u32[]{:S(2)}) collective-permute-start(f32[640,128]{1,0:T(8,128)S(1)} %get-tuple-element.14), channel_id=1, source_target_pairs={{0,2},{2,0},{4,6},{6,4},{1,3},{3,1},{5,7},{7,5},{8,10},{10,8},{12,... | collective-permute-start | bytes 983048 | tf_op jit(solution)/shard_map/ppermute | solution.py:316
  21.9 4.8 %collective-permute-start.4 = (f32[160,128]{1,0:T(8,128)S(1)}, f32[160,128]{1,0:T(8,128)S(1)}, u32[]{:S(2)}, u32[]{:S(2)}) collective-permute-start(f32[160,128]{1,0:T(8,128)S(1)} %get-tuple-element.15), channel_id=1, source_target_pairs={{0,1},{1,0},{2,3},{3,2},{4,5},{5,4},{6,7},{7,6},{8,9},{9,8},{10,11... | collective-permute-start | bytes 245768 | tf_op jit(solution)/shard_map/ppermute | solution.py:316
  23.5 6.1 %collective-permute-start.6 = (f32[160,128]{1,0:T(8,128)S(1)}, f32[160,128]{1,0:T(8,128)S(1)}, u32[]{:S(2)}, u32[]{:S(2)}) collective-permute-start(f32[160,128]{1,0:T(8,128)S(1)} %get-tuple-element.16), channel_id=1, source_target_pairs={{0,5},{1,4},{2,7},{3,6},{4,1},{5,0},{6,3},{7,2},{8,13},{9,12},{10,... | collective-permute-start | bytes 245768 | tf_op jit(solution)/shard_map/ppermute | solution.py:316
  25.0 4.7 %collective-permute-start.5 = (f32[160,128]{1,0:T(8,128)S(1)}, f32[160,128]{1,0:T(8,128)S(1)}, u32[]{:S(2)}, u32[]{:S(2)}) collective-permute-start(f32[160,128]{1,0:T(8,128)S(1)} %get-tuple-element.17), channel_id=1, source_target_pairs={{0,4},{1,5},{2,6},{3,7},{4,0},{5,1},{6,2},{7,3},{8,12},{9,13},{10,... | collective-permute-start | bytes 245768 | tf_op jit(solution)/shard_map/ppermute | solution.py:316
  29.7 4.5 %collective-permute-start.7 = (f32[160,128]{1,0:T(8,128)S(1)}, f32[160,128]{1,0:T(8,128)S(1)}, u32[]{:S(2)}, u32[]{:S(2)}) collective-permute-start(f32[160,128]{1,0:T(8,128)S(1)} %fusion.1), channel_id=1, source_target_pairs={{0,8},{8,0},{16,24},{24,16},{1,9},{9,1},{17,25},{25,17},{2,10},{10... | collective-permute-start | bytes 245768 | tf_op jit(solution)/shard_map/ppermute | solution.py:316
  34.2 5.5 %collective-permute-start.8 = (f32[160,128]{1,0:T(8,128)S(1)}, f32[160,128]{1,0:T(8,128)S(1)}, u32[]{:S(2)}, u32[]{:S(2)}) collective-permute-start(f32[160,128]{1,0:T(8,128)S(1)} %add.22), channel_id=1, source_target_pairs={{0,16},{8,24},{16,0},{24,8},{1,17},{9,25},{17,1},{25,9},{2,18},{10... | collective-permute-start | bytes 245768 | tf_op jit(solution)/shard_map/ppermute | solution.py:316
  39.7 9.2 %copy-start.1 = (f32[512,128]{1,0:T(8,128)S(1)}, f32[512,128]{1,0:T(8,128)}, u32[]{:S(2)}) copy-start(f32[512,128]{1,0:T(8,128)} %refs_5_.1) | copy-start | bytes 786436
  39.7 5.4 %collective-permute-start.11 = (f32[160,128]{1,0:T(8,128)S(1)}, f32[160,128]{1,0:T(8,128)S(1)}, u32[]{:S(2)}, u32[]{:S(2)}) collective-permute-start(f32[160,128]{1,0:T(8,128)S(1)} %add.23.refs_0_), channel_id=1, source_target_pairs={{0,5},{1,4},{2,7},{3,6},{4,1},{5,0},{6,3},{7,2},{8,13},{9,12},{10,... | collective-permute-start | bytes 245768 | tf_op jit(solution)/shard_map/ppermute | solution.py:316
  42.0 4.4 %collective-permute-start.10 = (f32[160,128]{1,0:T(8,128)S(1)}, f32[160,128]{1,0:T(8,128)S(1)}, u32[]{:S(2)}, u32[]{:S(2)}) collective-permute-start(f32[160,128]{1,0:T(8,128)S(1)} %add.23.refs_0_), channel_id=1, source_target_pairs={{0,4},{1,5},{2,6},{3,7},{4,0},{5,1},{6,2},{7,3},{8,12},{9,13},{10,... | collective-permute-start | bytes 245768 | tf_op jit(solution)/shard_map/ppermute | solution.py:316
  42.8 4.4 %collective-permute-start.9 = (f32[160,128]{1,0:T(8,128)S(1)}, f32[160,128]{1,0:T(8,128)S(1)}, u32[]{:S(2)}, u32[]{:S(2)}) collective-permute-start(f32[160,128]{1,0:T(8,128)S(1)} %add.23.refs_0_), channel_id=1, source_target_pairs={{0,1},{1,0},{2,3},{3,2},{4,5},{5,4},{6,7},{7,6},{8,9},{9,8},{10,11... | collective-permute-start | bytes 245768 | tf_op jit(solution)/shard_map/ppermute | solution.py:316
  47.2 1.7 %collective-permute-start.12 = (f32[640,128]{1,0:T(8,128)S(1)}, f32[640,128]{1,0:T(8,128)S(1)}, u32[]{:S(2)}, u32[]{:S(2)}) collective-permute-start(f32[640,128]{1,0:T(8,128)S(1)} %pad_maximum_fusion), channel_id=1, source_target_pairs={{0,2},{2,0},{4,6},{6,4},{1,3},{3,1},{5,7},{7,5},{8,10},{10,8},{12,... | collective-permute-start | bytes 983048 | tf_op jit(solution)/shard_map/ppermute | solution.py:316

commit v5 on v4

--- a/solution.py
+++ b/solution.py
@@ -58,7 +58,7 @@
 
     halves = [
         [
-            [state[pl.ds(pl.multiple_of(start + t * TILE, TILE), TILE), side] for t in range(tiles)]
+            [state[start + t * TILE : start + (t + 1) * TILE, side] for t in range(tiles)]
             for side in (slice(0, n), slice(n, 2 * n))
         ]
         for state in states
@@ -68,9 +68,7 @@
         held = [
             {
                 k: {
-                    t: jnp.take_along_axis(
-                        left[t], jnp.zeros(shape, jnp.int32) + (start + k), axis=1, mode="promise_in_bounds"
-                    )
+                    t: jnp.take_along_axis(left[t], jnp.full(shape, start + k, jnp.int32), axis=1, mode="promise_in_bounds")
                     for t in range(k // TILE, tiles)
                 }
                 for k in range(first, first + BLOCK)
@@ -99,17 +97,17 @@
                     across = spread(side, i)
                     for t in below:
                         side[t] = side[t] - factor[t] * across
-    lane = lax.broadcasted_iota(jnp.int32, (GROUP, n), 1)
-    rows = pl.ds(pl.multiple_of(start, GROUP), GROUP)
+    rows = slice(start, start + GROUP)
+    rest = slice(start + GROUP, n)
     for state, sides, pivot_of in zip(states, halves, pivots):
         scale = jnp.concatenate([lax.rsqrt(p) for p in pivot_of], axis=0)
         left, right = [jnp.concatenate(side, axis=0) * scale for side in sides]
         state[rows, :n] = left
         state[rows, n:] = right
-        parts = split3(left)
-        lhs = [jnp.where(lane >= start + GROUP, part, jnp.zeros_like(part)) for part in parts]
-        rhs = [jnp.concatenate(pair, axis=1) for pair in zip(parts, split3(right))]
-        state[...] = state[...] - deep_dot(lhs, rhs, TN)
+        if start + GROUP < n:
+            lhs = split3(left)
+            rhs = [jnp.concatenate(pair, axis=1) for pair in zip(lhs, split3(right))]
+            state[rest, :] = state[rest, :] - deep_dot(lhs, rhs, TN)[rest, :]
 
 
 def upper_blocks(size, n):
@@ -143,26 +141,26 @@
     return lax.axis_index("af")
 
 
-def pick_kernel(owner_ref, slab_ref, *pieces):
-    fibers = len(pieces)
+def pick_kernel(distances, owner_ref, slab_ref, *pieces):
     width = pieces[0].shape[1]
     me = fiber_place()
-    for distance, piece in enumerate(pieces):
+    for distance, piece in zip(distances, pieces):
         block = 0
-        for b in range(fibers):
+        for b in range(owner_ref.shape[-1]):
             block = jnp.where(owner_ref[0, 0, b] == lax.bitwise_xor(me, distance), b, block)
         piece[...] = slab_ref[:, pl.ds(pl.multiple_of(block * width, width), width)]
 
 
-def pick_blocks(owners, slab):
-    fibers = owners.shape[-1]
-    piece = jax.ShapeDtypeStruct((slab.shape[0], slab.shape[1] // fibers), slab.dtype)
-    return pl.pallas_call(
-        pick_kernel,
-        out_shape=(piece,) * fibers,
+def pick_blocks(distances, owners, slab, **params):
+    piece = jax.ShapeDtypeStruct((slab.shape[0], slab.shape[1] // owners.shape[-1]), slab.dtype)
+    picked = pl.pallas_call(
+        functools.partial(pick_kernel, distances),
+        out_shape=(piece,) * len(distances),
         in_specs=[pl.BlockSpec(memory_space=pltpu.SMEM), pl.BlockSpec(memory_space=pltpu.VMEM)],
+        compiler_params=pltpu.CompilerParams(**params),
         name="pick_blocks",
     )(owners, slab)
+    return dict(zip(distances, picked))
 
 
 def in_row_order(pieces, columns):
@@ -250,12 +248,9 @@
                 two[:, :n] = wide_dot(wide, wide, TN)
             two[:, n:] = eye
 
-        def step(group, carry):
-            states = [one] * (phase < phases) + [two] * (phase < 2 * ITERS)
+        states = [one] * (phase < phases) + [two] * (phase < 2 * ITERS)
+        for group in range(n // GROUP):
             eliminate(states, group * GROUP, n)
-            return carry
-
-        lax.fori_loop(0, n // GROUP, step, 0)
         if phase < phases:
             tri_ref[at, at] = jnp.where(upper, one[:, :n], 0.0).T
             if phase < phases - 1:
@@ -339,9 +334,13 @@
 def on_device(slab, block_owner, basis_init):
     fibers = lax.axis_size("af")
     chunks = lax.axis_size("gy") * lax.axis_size("gz")
-    along = axis_bits("af")
-    pieces = pick_blocks(block_owner, slab)
-    pieces = [pieces[0]] + [swap(pieces[d], along[::-1], d) for d in range(1, fibers)]
+    along = axis_bits("af")[::-1]
+    far = fibers // 2
+    pieces = pick_blocks([far], block_owner, slab)
+    slab, _ = lax.optimization_barrier((slab, pieces[far]))
+    others = [d for d in range(fibers) if d != far]
+    pieces.update(pick_blocks(others, block_owner, slab, vmem_limit_bytes=8 * 1024 * 1024))
+    pieces = [pieces[0]] + [swap(pieces[d], along, d) for d in range(1, fibers)]
     divisor = pieces[0].shape[1] * fibers * chunks
     kept, sent = local_gram(pieces, divisor, basis_init.shape[1], chunks)
     slots, other = sum_over_devices(kept, sent)

time: 71.2 us -> 67.8 us (0.952)
  Pallas kernels: 24.6 us -> 22 us
  starting transfers between devices: 17.9 us -> 19.5 us
  waiting for transfers between devices: 26.8 us -> 25.4 us
  local copies, waits for them, and re-layouts: 0.93 us -> 0.03 us
    pallas_call x1, Pallas kernels: 22.1 us -> 19 us  [factor(): pl.pallas_call(functools.partial(factor_kernel, chunks, len(pieces)), out...]
    ppermute x13, starting transfers between devices: 17.9 us -> 19.5 us  [swap(): return lax.ppermute(value, axes, pairs)]
    ppermute x13, waiting for transfers between devices: 26.8 us -> 25.4 us  [swap(): return lax.ppermute(value, axes, pairs)]
    unnamed x4 -> x6, local copies, waits for them, and re-layouts: 0.91 us -> 0.01 us
    pallas_call x1 -> x2, Pallas kernels: 1.89 us -> 2.37 us  [pick_blocks(): pl.pallas_call(functools.partial(pick_kernel, distances), out_shape=(piec...]
  transfers between devices with their start and end apart: 13 -> 13, of which waited for: 11 -> 11; matrix products, arithmetic and copies ran while one was open for 0% -> 0% of each run, Pallas kernels for 0% -> 1%
where the time goes in v5:
time: 67.8 us; the launch traced here: 67.7 us
  waiting for transfers between devices  25.4 us (37%)
  Pallas kernels  22 us (32%)
  starting transfers between devices  19.5 us (29%)
  between operations  0.72 us (1%)
    ppermute x13, waiting for transfers between devices, swap(): return lax.ppermute(value, axes, pairs)  25.4 us
    ppermute x13, starting transfers between devices, swap(): return lax.ppermute(value, axes, pairs)  19.5 us
    pallas_call x1, Pallas kernels, factor(): pl.pallas_call(functools.partial(factor_kernel, chunks, len(pieces)), out...  19 us
    pallas_call x2, Pallas kernels, pick_blocks(): pl.pallas_call(functools.partial(pick_kernel, distances), out_shape=(piec...  2.37 us
  transfers between devices with their start and end apart: 13, of which 11 were waited for; matrix products, arithmetic and copies ran while one was open for 0% of the time, Pallas kernels for 1%

profile of v5, /device:TPU:0, one launch (start us, length us, event | category | flops | bytes accessed | tf_op | source)
XLA Modules:
  0.0 67.7 jit_solution(16673020248424087624)
XLA Ops:
  0.6 0.0 copy-start.2
  0.6 0.0 copy-start
  0.6 1.8 %pick_blocks.2 = bf16[128,512]{1,0:T(8,128)(2,1)} custom-call(s32[1,1,4]{2,1,0:T(1,128)} %owner_ref.3, bf16[128,2048]{1,0:T(8,128)(2,1)} %slab_ref.2), custom_call_target="tpu_custom_call" | custom-call | tf_op jit(solution)/shard_map/pick_blocks/pallas_call | solution.py:156
  2.4 4.0 %collective-permute-start.1 = (bf16[128,512]{1,0:T(8,128)(2,1)}, bf16[128,512]{1,0:T(8,128)(2,1)S(1)}, u32[]{:S(2)}, u32[]{:S(2)}) collective-permute-start(bf16[128,512]{1,0:T(8,128)(2,1)} %pick_blocks.2), channel_id=1, source_target_pairs={{0,16},{8,24},{16,0},{24,8},{1,17},{9,25},{17,1},{25,9},{2,18},{10... | collective-permute-start | bytes 393224 | tf_op jit(solution)/shard_map/ppermute | solution.py:311
  6.5 0.0 copy-done.2
  6.5 0.0 copy-done
  6.5 0.6 pick_blocks.3
  7.1 1.6 %collective-permute-start = (bf16[128,512]{1,0:T(8,128)(2,1)S(1)}, bf16[128,512]{1,0:T(8,128)(2,1)S(1)}, u32[]{:S(2)}, u32[]{:S(2)}) collective-permute-start(bf16[128,512]{1,0:T(8,128)(2,1)S(1)} %get-tuple-element.11), channel_id=1, source_target_pairs={{0,8},{8,0},{16,24},{24,16},{1,9},{9,1},{17,25},{25,17},{2,10},{10... | collective-permute-start | bytes 393224 | tf_op jit(solution)/shard_map/ppermute | solution.py:311
  8.7 0.0 collective-permute-start.2
  8.7 5.9 %collective-permute-done.1.refs_2_.refs_8_ = bf16[128,512]{1,0:T(8,128)(2,1)S(1)} collective-permute-done((bf16[128,512]{1,0:T(8,128)(2,1)}, bf16[128,512]{1,0:T(8,128)(2,1)S(1)}, u32[]{:S(2)}, u32[]{:S(2)}) %collective-permute-start.1) | collective-permute-done | bytes 131104 | tf_op jit(solution)/shard_map/ppermute | solution.py:311
  14.6 0.0 collective-permute-done.refs_1_.refs_7_
  14.6 2.4 %collective-permute-done.2.refs_3_.refs_9_ = bf16[128,512]{1,0:T(8,128)(2,1)S(1)} collective-permute-done((bf16[128,512]{1,0:T(8,128)(2,1)S(1)}, bf16[128,512]{1,0:T(8,128)(2,1)S(1)}, u32[]{:S(2)}, u32[]{:S(2)}) %collective-permute-start.2) | collective-permute-done | bytes 131104 | tf_op jit(solution)/shard_map/ppermute | solution.py:311
  17.0 0.6 local_gram.1
  17.6 0.1 collective-permute-start.3
  17.7 1.6 %collective-permute-done.3 = f32[640,128]{1,0:T(8,128)S(1)} collective-permute-done((f32[640,128]{1,0:T(8,128)S(1)}, f32[640,128]{1,0:T(8,128)S(1)}, u32[]{:S(2)}, u32[]{:S(2)}) %collective-permute-start.3) | collective-permute-done | bytes 327712 | tf_op jit(solution)/shard_map/ppermute | solution.py:311
  19.4 1.6 %collective-permute-start.4 = (f32[160,128]{1,0:T(8,128)S(1)}, f32[160,128]{1,0:T(8,128)S(1)}, u32[]{:S(2)}, u32[]{:S(2)}) collective-permute-start(f32[160,128]{1,0:T(8,128)S(1)} %get-tuple-element.15), channel_id=1, source_target_pairs={{0,1},{1,0},{2,3},{3,2},{4,5},{5,4},{6,7},{7,6},{8,9},{9,8},{10,11... | collective-permute-start | bytes 245768 | tf_op jit(solution)/shard_map/ppermute | solution.py:311
  21.0 1.4 %collective-permute-start.6 = (f32[160,128]{1,0:T(8,128)S(1)}, f32[160,128]{1,0:T(8,128)S(1)}, u32[]{:S(2)}, u32[]{:S(2)}) collective-permute-start(f32[160,128]{1,0:T(8,128)S(1)} %get-tuple-element.16), channel_id=1, source_target_pairs={{0,5},{1,4},{2,7},{3,6},{4,1},{5,0},{6,3},{7,2},{8,13},{9,12},{10,... | collective-permute-start | bytes 245768 | tf_op jit(solution)/shard_map/ppermute | solution.py:311
  22.4 0.5 collective-permute-start.5
  22.9 1.3 %collective-permute-done.4 = f32[160,128]{1,0:T(8,128)S(1)} collective-permute-done((f32[160,128]{1,0:T(8,128)S(1)}, f32[160,128]{1,0:T(8,128)S(1)}, u32[]{:S(2)}, u32[]{:S(2)}) %collective-permute-start.4) | collective-permute-done | bytes 81952 | tf_op jit(solution)/shard_map/ppermute | solution.py:311
  24.2 2.9 %collective-permute-done.6 = f32[160,128]{1,0:T(8,128)S(1)} collective-permute-done((f32[160,128]{1,0:T(8,128)S(1)}, f32[160,128]{1,0:T(8,128)S(1)}, u32[]{:S(2)}, u32[]{:S(2)}) %collective-permute-start.6) | collective-permute-done | bytes 81952 | tf_op jit(solution)/shard_map/ppermute | solution.py:311
  27.1 0.0 collective-permute-done.5
  27.1 2.4 %collective-permute-start.7 = (f32[160,128]{1,0:T(8,128)S(1)}, f32[160,128]{1,0:T(8,128)S(1)}, u32[]{:S(2)}, u32[]{:S(2)}) collective-permute-start(f32[160,128]{1,0:T(8,128)S(1)} %fusion.1), channel_id=1, source_target_pairs={{0,8},{8,0},{16,24},{24,16},{1,9},{9,1},{17,25},{25,17},{2,10},{10... | collective-permute-start | bytes 245768 | tf_op jit(solution)/shard_map/ppermute | solution.py:311
  29.5 2.4 %collective-permute-done.7 = f32[160,128]{1,0:T(8,128)S(1)} collective-permute-done((f32[160,128]{1,0:T(8,128)S(1)}, f32[160,128]{1,0:T(8,128)S(1)}, u32[]{:S(2)}, u32[]{:S(2)}) %collective-permute-start.7) | collective-permute-done | bytes 81952 | tf_op jit(solution)/shard_map/ppermute | solution.py:311
  32.0 4.2 %collective-permute-start.8 = (f32[160,128]{1,0:T(8,128)S(1)}, f32[160,128]{1,0:T(8,128)S(1)}, u32[]{:S(2)}, u32[]{:S(2)}) collective-permute-start(f32[160,128]{1,0:T(8,128)S(1)} %add.22), channel_id=1, source_target_pairs={{0,16},{8,24},{16,0},{24,8},{1,17},{9,25},{17,1},{25,9},{2,18},{10... | collective-permute-start | bytes 245768 | tf_op jit(solution)/shard_map/ppermute | solution.py:311
  36.2 3.3 %collective-permute-done.8 = f32[160,128]{1,0:T(8,128)S(1)} collective-permute-done((f32[160,128]{1,0:T(8,128)S(1)}, f32[160,128]{1,0:T(8,128)S(1)}, u32[]{:S(2)}, u32[]{:S(2)}) %collective-permute-start.8) | collective-permute-done | bytes 81952 | tf_op jit(solution)/shard_map/ppermute | solution.py:311
  39.5 0.0 copy-start.1
  39.5 2.5 %collective-permute-start.11 = (f32[160,128]{1,0:T(8,128)S(1)}, f32[160,128]{1,0:T(8,128)S(1)}, u32[]{:S(2)}, u32[]{:S(2)}) collective-permute-start(f32[160,128]{1,0:T(8,128)S(1)} %add.23.refs_0_), channel_id=1, source_target_pairs={{0,5},{1,4},{2,7},{3,6},{4,1},{5,0},{6,3},{7,2},{8,13},{9,12},{10,... | collective-permute-start | bytes 245768 | tf_op jit(solution)/shard_map/ppermute | solution.py:311
  42.0 0.5 collective-permute-start.10
  42.5 0.5 collective-permute-start.9
  43.0 1.9 %collective-permute-done.11.refs_3_ = f32[160,128]{1,0:T(8,128)S(1)} collective-permute-done((f32[160,128]{1,0:T(8,128)S(1)}, f32[160,128]{1,0:T(8,128)S(1)}, u32[]{:S(2)}, u32[]{:S(2)}) %collective-permute-start.11) | collective-permute-done | bytes 81952 | tf_op jit(solution)/shard_map/ppermute | solution.py:311
  44.9 1.5 %collective-permute-done.10.refs_2_ = f32[160,128]{1,0:T(8,128)S(1)} collective-permute-done((f32[160,128]{1,0:T(8,128)S(1)}, f32[160,128]{1,0:T(8,128)S(1)}, u32[]{:S(2)}, u32[]{:S(2)}) %collective-permute-start.10) | collective-permute-done | bytes 81952 | tf_op jit(solution)/shard_map/ppermute | solution.py:311
  46.4 0.5 collective-permute-done.9.refs_1_
  47.0 0.1 collective-permute-start.12
  47.1 1.6 %collective-permute-done.12.refs_4_ = f32[640,128]{1,0:T(8,128)S(1)} collective-permute-done((f32[640,128]{1,0:T(8,128)S(1)}, f32[640,128]{1,0:T(8,128)S(1)}, u32[]{:S(2)}, u32[]{:S(2)}) %collective-permute-start.12) | collective-permute-done | bytes 327712 | tf_op jit(solution)/shard_map/ppermute | solution.py:311
  48.7 0.0 copy-done.1
  48.7 19.0 %factor.1 = (f32[512,512]{1,0:T(8,128)}, f32[512,128]{1,0:T(8,128)}, bf16[128,512]{1,0:T(8,128)(2,1)}) custom-call(f32[160,128]{1,0:T(8,128)S(1)} %add.23.refs_0_, f32[160,128]{1,0:T(8,128)S(1)} %collective-permute-done.9.refs_1_, f32[160,128]{1,0:T(8,128)S(1)} %collective-permute-done.10.refs_2_, f32[160,128]{1,0:T(8,128)S(1)} %collective-permute-done.11.refs_3_, ...), custom_call_target="tpu_custom_call" | custom-call | tf_op jit(solution)/shard_map/factor/pallas_call | solution.py:279
  (6 shorter events, 0.1 us)
Async XLA Ops:
  0.6 5.9 %copy-start.2 = (s32[1,1,4]{2,1,0:T(1,128)S(1)}, s32[1,1,4]{2,1,0:T(1,128)}, u32[]{:S(2)}) copy-start(s32[1,1,4]{2,1,0:T(1,128)} %owner_ref.3) | copy-start | bytes 52
  0.6 5.8 %copy-start = (bf16[128,2048]{1,0:T(8,128)(2,1)S(1)}, bf16[128,2048]{1,0:T(8,128)(2,1)}, u32[]{:S(2)}) copy-start(bf16[128,2048]{1,0:T(8,128)(2,1)} %slab_ref.2) | copy-start | bytes 1572868
  2.4 12.2 %collective-permute-start.1 = (bf16[128,512]{1,0:T(8,128)(2,1)}, bf16[128,512]{1,0:T(8,128)(2,1)S(1)}, u32[]{:S(2)}, u32[]{:S(2)}) collective-permute-start(bf16[128,512]{1,0:T(8,128)(2,1)} %pick_blocks.2), channel_id=1, source_target_pairs={{0,16},{8,24},{16,0},{24,8},{1,17},{9,25},{17,1},{25,9},{2,18},{10... | collective-permute-start | bytes 393224 | tf_op jit(solution)/shard_map/ppermute | solution.py:311
  7.1 7.6 %collective-permute-start = (bf16[128,512]{1,0:T(8,128)(2,1)S(1)}, bf16[128,512]{1,0:T(8,128)(2,1)S(1)}, u32[]{:S(2)}, u32[]{:S(2)}) collective-permute-start(bf16[128,512]{1,0:T(8,128)(2,1)S(1)} %get-tuple-element.11), channel_id=1, source_target_pairs={{0,8},{8,0},{16,24},{24,16},{1,9},{9,1},{17,25},{25,17},{2,10},{10... | collective-permute-start | bytes 393224 | tf_op jit(solution)/shard_map/ppermute | solution.py:311
  8.7 8.3 %collective-permute-start.2 = (bf16[128,512]{1,0:T(8,128)(2,1)S(1)}, bf16[128,512]{1,0:T(8,128)(2,1)S(1)}, u32[]{:S(2)}, u32[]{:S(2)}) collective-permute-start(bf16[128,512]{1,0:T(8,128)(2,1)S(1)} %get-tuple-element.12), channel_id=1, source_target_pairs={{0,24},{8,16},{16,8},{24,0},{1,25},{9,17},{17,9},{25,1},{2,26},{10... | collective-permute-start | bytes 393224 | tf_op jit(solution)/shard_map/ppermute | solution.py:311
  17.6 1.7 %collective-permute-start.3 = (f32[640,128]{1,0:T(8,128)S(1)}, f32[640,128]{1,0:T(8,128)S(1)}, u32[]{:S(2)}, u32[]{:S(2)}) collective-permute-start(f32[640,128]{1,0:T(8,128)S(1)} %get-tuple-element.14), channel_id=1, source_target_pairs={{0,2},{2,0},{4,6},{6,4},{1,3},{3,1},{5,7},{7,5},{8,10},{10,8},{12,... | collective-permute-start | bytes 983048 | tf_op jit(solution)/shard_map/ppermute | solution.py:311
  19.4 4.8 %collective-permute-start.4 = (f32[160,128]{1,0:T(8,128)S(1)}, f32[160,128]{1,0:T(8,128)S(1)}, u32[]{:S(2)}, u32[]{:S(2)}) collective-permute-start(f32[160,128]{1,0:T(8,128)S(1)} %get-tuple-element.15), channel_id=1, source_target_pairs={{0,1},{1,0},{2,3},{3,2},{4,5},{5,4},{6,7},{7,6},{8,9},{9,8},{10,11... | collective-permute-start | bytes 245768 | tf_op jit(solution)/shard_map/ppermute | solution.py:311
  21.0 6.1 %collective-permute-start.6 = (f32[160,128]{1,0:T(8,128)S(1)}, f32[160,128]{1,0:T(8,128)S(1)}, u32[]{:S(2)}, u32[]{:S(2)}) collective-permute-start(f32[160,128]{1,0:T(8,128)S(1)} %get-tuple-element.16), channel_id=1, source_target_pairs={{0,5},{1,4},{2,7},{3,6},{4,1},{5,0},{6,3},{7,2},{8,13},{9,12},{10,... | collective-permute-start | bytes 245768 | tf_op jit(solution)/shard_map/ppermute | solution.py:311
  22.4 4.7 %collective-permute-start.5 = (f32[160,128]{1,0:T(8,128)S(1)}, f32[160,128]{1,0:T(8,128)S(1)}, u32[]{:S(2)}, u32[]{:S(2)}) collective-permute-start(f32[160,128]{1,0:T(8,128)S(1)} %get-tuple-element.17), channel_id=1, source_target_pairs={{0,4},{1,5},{2,6},{3,7},{4,0},{5,1},{6,2},{7,3},{8,12},{9,13},{10,... | collective-permute-start | bytes 245768 | tf_op jit(solution)/shard_map/ppermute | solution.py:311
  27.1 4.8 %collective-permute-start.7 = (f32[160,128]{1,0:T(8,128)S(1)}, f32[160,128]{1,0:T(8,128)S(1)}, u32[]{:S(2)}, u32[]{:S(2)}) collective-permute-start(f32[160,128]{1,0:T(8,128)S(1)} %fusion.1), channel_id=1, source_target_pairs={{0,8},{8,0},{16,24},{24,16},{1,9},{9,1},{17,25},{25,17},{2,10},{10... | collective-permute-start | bytes 245768 | tf_op jit(solution)/shard_map/ppermute | solution.py:311
  32.0 7.5 %collective-permute-start.8 = (f32[160,128]{1,0:T(8,128)S(1)}, f32[160,128]{1,0:T(8,128)S(1)}, u32[]{:S(2)}, u32[]{:S(2)}) collective-permute-start(f32[160,128]{1,0:T(8,128)S(1)} %add.22), channel_id=1, source_target_pairs={{0,16},{8,24},{16,0},{24,8},{1,17},{9,25},{17,1},{25,9},{2,18},{10... | collective-permute-start | bytes 245768 | tf_op jit(solution)/shard_map/ppermute | solution.py:311
  39.5 9.2 %copy-start.1 = (f32[512,128]{1,0:T(8,128)S(1)}, f32[512,128]{1,0:T(8,128)}, u32[]{:S(2)}) copy-start(f32[512,128]{1,0:T(8,128)} %refs_5_.1) | copy-start | bytes 786436
  39.5 5.4 %collective-permute-start.11 = (f32[160,128]{1,0:T(8,128)S(1)}, f32[160,128]{1,0:T(8,128)S(1)}, u32[]{:S(2)}, u32[]{:S(2)}) collective-permute-start(f32[160,128]{1,0:T(8,128)S(1)} %add.23.refs_0_), channel_id=1, source_target_pairs={{0,5},{1,4},{2,7},{3,6},{4,1},{5,0},{6,3},{7,2},{8,13},{9,12},{10,... | collective-permute-start | bytes 245768 | tf_op jit(solution)/shard_map/ppermute | solution.py:311
  42.0 4.4 %collective-permute-start.10 = (f32[160,128]{1,0:T(8,128)S(1)}, f32[160,128]{1,0:T(8,128)S(1)}, u32[]{:S(2)}, u32[]{:S(2)}) collective-permute-start(f32[160,128]{1,0:T(8,128)S(1)} %add.23.refs_0_), channel_id=1, source_target_pairs={{0,4},{1,5},{2,6},{3,7},{4,0},{5,1},{6,2},{7,3},{8,12},{9,13},{10,... | collective-permute-start | bytes 245768 | tf_op jit(solution)/shard_map/ppermute | solution.py:311
  42.5 4.4 %collective-permute-start.9 = (f32[160,128]{1,0:T(8,128)S(1)}, f32[160,128]{1,0:T(8,128)S(1)}, u32[]{:S(2)}, u32[]{:S(2)}) collective-permute-start(f32[160,128]{1,0:T(8,128)S(1)} %add.23.refs_0_), channel_id=1, source_target_pairs={{0,1},{1,0},{2,3},{3,2},{4,5},{5,4},{6,7},{7,6},{8,9},{9,8},{10,11... | collective-permute-start | bytes 245768 | tf_op jit(solution)/shard_map/ppermute | solution.py:311
  47.0 1.7 %collective-permute-start.12 = (f32[640,128]{1,0:T(8,128)S(1)}, f32[640,128]{1,0:T(8,128)S(1)}, u32[]{:S(2)}, u32[]{:S(2)}) collective-permute-start(f32[640,128]{1,0:T(8,128)S(1)} %pad_maximum_fusion), channel_id=1, source_target_pairs={{0,2},{2,0},{4,6},{6,4},{1,3},{3,1},{5,7},{7,5},{8,10},{10,8},{12,... | collective-permute-start | bytes 983048 | tf_op jit(solution)/shard_map/ppermute | solution.py:311

commit v6 on v5

--- a/solution.py
+++ b/solution.py
@@ -33,6 +33,13 @@
     (ah, am, al), (bh, bm, bl) = a, b
     left = jnp.concatenate([ah, am, ah, am, ah, al], axis=dims[0][0])
     right = jnp.concatenate([bh, bh, bm, bm, bl, bh], axis=dims[1][0])
+    return dot(left, right, dims)
+
+
+def short_dot(a, b, dims):
+    (ah, am, _), (bh, bm, _) = a, b
+    left = jnp.concatenate([ah, am, ah], axis=dims[0][0])
+    right = jnp.concatenate([bh, bh, bm], axis=dims[1][0])
     return dot(left, right, dims)
 
 
@@ -265,7 +272,7 @@
                         [x[:, mine] for x in pieces], [x[:, tail] for x in pieces], TN
                     )
         if phase < 2 * ITERS:
-            wide = deep_dot(wide, split3(two[:, n:]), NT)
+            wide = short_dot(wide, split3(two[:, n:]), NT)
             if phase % 2 == 1:
                 basis = wide
     out_ref[...] = basis

time: 67.8 us -> 66.8 us (0.985)
  Pallas kernels: 22 us -> 20.9 us
    pallas_call x1, Pallas kernels: 19 us -> 17.9 us  [factor(): pl.pallas_call(functools.partial(factor_kernel, chunks, len(pieces)), out...]
where the time goes in v6:
time: 66.8 us; the launch traced here: 66.6 us
  waiting for transfers between devices  25.4 us (38%)
  Pallas kernels  20.9 us (31%)
  starting transfers between devices  19.5 us (29%)
  between operations  0.72 us (1%)
    ppermute x13, waiting for transfers between devices, swap(): return lax.ppermute(value, axes, pairs)  25.4 us
    ppermute x13, starting transfers between devices, swap(): return lax.ppermute(value, axes, pairs)  19.5 us
    pallas_call x1, Pallas kernels, factor(): pl.pallas_call(functools.partial(factor_kernel, chunks, len(pieces)), out...  17.9 us
    pallas_call x2, Pallas kernels, pick_blocks(): pl.pallas_call(functools.partial(pick_kernel, distances), out_shape=(piec...  2.37 us
  transfers between devices with their start and end apart: 13, of which 11 were waited for; matrix products, arithmetic and copies ran while one was open for 0% of the time, Pallas kernels for 1%

profile of v6, /device:TPU:0, one launch (start us, length us, event | category | flops | bytes accessed | tf_op | source)
XLA Modules:
  0.0 66.6 jit_solution(7888837208330495802)
XLA Ops:
  0.6 0.0 copy-start.2
  0.6 0.0 copy-start
  0.6 1.8 %pick_blocks.2 = bf16[128,512]{1,0:T(8,128)(2,1)} custom-call(s32[1,1,4]{2,1,0:T(1,128)} %owner_ref.3, bf16[128,2048]{1,0:T(8,128)(2,1)} %slab_ref.2), custom_call_target="tpu_custom_call" | custom-call | tf_op jit(solution)/shard_map/pick_blocks/pallas_call | solution.py:163
  2.4 4.0 %collective-permute-start.1 = (bf16[128,512]{1,0:T(8,128)(2,1)}, bf16[128,512]{1,0:T(8,128)(2,1)S(1)}, u32[]{:S(2)}, u32[]{:S(2)}) collective-permute-start(bf16[128,512]{1,0:T(8,128)(2,1)} %pick_blocks.2), channel_id=1, source_target_pairs={{0,16},{8,24},{16,0},{24,8},{1,17},{9,25},{17,1},{25,9},{2,18},{10... | collective-permute-start | bytes 393224 | tf_op jit(solution)/shard_map/ppermute | solution.py:318
  6.5 0.0 copy-done.2
  6.5 0.0 copy-done
  6.5 0.6 pick_blocks.3
  7.1 1.6 %collective-permute-start = (bf16[128,512]{1,0:T(8,128)(2,1)S(1)}, bf16[128,512]{1,0:T(8,128)(2,1)S(1)}, u32[]{:S(2)}, u32[]{:S(2)}) collective-permute-start(bf16[128,512]{1,0:T(8,128)(2,1)S(1)} %get-tuple-element.11), channel_id=1, source_target_pairs={{0,8},{8,0},{16,24},{24,16},{1,9},{9,1},{17,25},{25,17},{2,10},{10... | collective-permute-start | bytes 393224 | tf_op jit(solution)/shard_map/ppermute | solution.py:318
  8.7 0.0 collective-permute-start.2
  8.7 5.9 %collective-permute-done.1.refs_2_.refs_8_ = bf16[128,512]{1,0:T(8,128)(2,1)S(1)} collective-permute-done((bf16[128,512]{1,0:T(8,128)(2,1)}, bf16[128,512]{1,0:T(8,128)(2,1)S(1)}, u32[]{:S(2)}, u32[]{:S(2)}) %collective-permute-start.1) | collective-permute-done | bytes 131104 | tf_op jit(solution)/shard_map/ppermute | solution.py:318
  14.6 0.0 collective-permute-done.refs_1_.refs_7_
  14.6 2.4 %collective-permute-done.2.refs_3_.refs_9_ = bf16[128,512]{1,0:T(8,128)(2,1)S(1)} collective-permute-done((bf16[128,512]{1,0:T(8,128)(2,1)S(1)}, bf16[128,512]{1,0:T(8,128)(2,1)S(1)}, u32[]{:S(2)}, u32[]{:S(2)}) %collective-permute-start.2) | collective-permute-done | bytes 131104 | tf_op jit(solution)/shard_map/ppermute | solution.py:318
  17.0 0.6 local_gram.1
  17.6 0.1 collective-permute-start.3
  17.7 1.6 %collective-permute-done.3 = f32[640,128]{1,0:T(8,128)S(1)} collective-permute-done((f32[640,128]{1,0:T(8,128)S(1)}, f32[640,128]{1,0:T(8,128)S(1)}, u32[]{:S(2)}, u32[]{:S(2)}) %collective-permute-start.3) | collective-permute-done | bytes 327712 | tf_op jit(solution)/shard_map/ppermute | solution.py:318
  19.4 1.6 %collective-permute-start.4 = (f32[160,128]{1,0:T(8,128)S(1)}, f32[160,128]{1,0:T(8,128)S(1)}, u32[]{:S(2)}, u32[]{:S(2)}) collective-permute-start(f32[160,128]{1,0:T(8,128)S(1)} %get-tuple-element.15), channel_id=1, source_target_pairs={{0,1},{1,0},{2,3},{3,2},{4,5},{5,4},{6,7},{7,6},{8,9},{9,8},{10,11... | collective-permute-start | bytes 245768 | tf_op jit(solution)/shard_map/ppermute | solution.py:318
  21.0 1.4 %collective-permute-start.6 = (f32[160,128]{1,0:T(8,128)S(1)}, f32[160,128]{1,0:T(8,128)S(1)}, u32[]{:S(2)}, u32[]{:S(2)}) collective-permute-start(f32[160,128]{1,0:T(8,128)S(1)} %get-tuple-element.16), channel_id=1, source_target_pairs={{0,5},{1,4},{2,7},{3,6},{4,1},{5,0},{6,3},{7,2},{8,13},{9,12},{10,... | collective-permute-start | bytes 245768 | tf_op jit(solution)/shard_map/ppermute | solution.py:318
  22.4 0.5 collective-permute-start.5
  22.9 1.3 %collective-permute-done.4 = f32[160,128]{1,0:T(8,128)S(1)} collective-permute-done((f32[160,128]{1,0:T(8,128)S(1)}, f32[160,128]{1,0:T(8,128)S(1)}, u32[]{:S(2)}, u32[]{:S(2)}) %collective-permute-start.4) | collective-permute-done | bytes 81952 | tf_op jit(solution)/shard_map/ppermute | solution.py:318
  24.2 2.9 %collective-permute-done.6 = f32[160,128]{1,0:T(8,128)S(1)} collective-permute-done((f32[160,128]{1,0:T(8,128)S(1)}, f32[160,128]{1,0:T(8,128)S(1)}, u32[]{:S(2)}, u32[]{:S(2)}) %collective-permute-start.6) | collective-permute-done | bytes 81952 | tf_op jit(solution)/shard_map/ppermute | solution.py:318
  27.1 0.0 collective-permute-done.5
  27.1 2.4 %collective-permute-start.7 = (f32[160,128]{1,0:T(8,128)S(1)}, f32[160,128]{1,0:T(8,128)S(1)}, u32[]{:S(2)}, u32[]{:S(2)}) collective-permute-start(f32[160,128]{1,0:T(8,128)S(1)} %fusion.1), channel_id=1, source_target_pairs={{0,8},{8,0},{16,24},{24,16},{1,9},{9,1},{17,25},{25,17},{2,10},{10... | collective-permute-start | bytes 245768 | tf_op jit(solution)/shard_map/ppermute | solution.py:318
  29.5 2.4 %collective-permute-done.7 = f32[160,128]{1,0:T(8,128)S(1)} collective-permute-done((f32[160,128]{1,0:T(8,128)S(1)}, f32[160,128]{1,0:T(8,128)S(1)}, u32[]{:S(2)}, u32[]{:S(2)}) %collective-permute-start.7) | collective-permute-done | bytes 81952 | tf_op jit(solution)/shard_map/ppermute | solution.py:318
  32.0 4.2 %collective-permute-start.8 = (f32[160,128]{1,0:T(8,128)S(1)}, f32[160,128]{1,0:T(8,128)S(1)}, u32[]{:S(2)}, u32[]{:S(2)}) collective-permute-start(f32[160,128]{1,0:T(8,128)S(1)} %add.22), channel_id=1, source_target_pairs={{0,16},{8,24},{16,0},{24,8},{1,17},{9,25},{17,1},{25,9},{2,18},{10... | collective-permute-start | bytes 245768 | tf_op jit(solution)/shard_map/ppermute | solution.py:318
  36.2 3.3 %collective-permute-done.8 = f32[160,128]{1,0:T(8,128)S(1)} collective-permute-done((f32[160,128]{1,0:T(8,128)S(1)}, f32[160,128]{1,0:T(8,128)S(1)}, u32[]{:S(2)}, u32[]{:S(2)}) %collective-permute-start.8) | collective-permute-done | bytes 81952 | tf_op jit(solution)/shard_map/ppermute | solution.py:318
  39.5 0.0 copy-start.1
  39.5 2.5 %collective-permute-start.11 = (f32[160,128]{1,0:T(8,128)S(1)}, f32[160,128]{1,0:T(8,128)S(1)}, u32[]{:S(2)}, u32[]{:S(2)}) collective-permute-start(f32[160,128]{1,0:T(8,128)S(1)} %add.23.refs_0_), channel_id=1, source_target_pairs={{0,5},{1,4},{2,7},{3,6},{4,1},{5,0},{6,3},{7,2},{8,13},{9,12},{10,... | collective-permute-start | bytes 245768 | tf_op jit(solution)/shard_map/ppermute | solution.py:318
  42.0 0.5 collective-permute-start.10
  42.5 0.5 collective-permute-start.9
  43.0 1.9 %collective-permute-done.11.refs_3_ = f32[160,128]{1,0:T(8,128)S(1)} collective-permute-done((f32[160,128]{1,0:T(8,128)S(1)}, f32[160,128]{1,0:T(8,128)S(1)}, u32[]{:S(2)}, u32[]{:S(2)}) %collective-permute-start.11) | collective-permute-done | bytes 81952 | tf_op jit(solution)/shard_map/ppermute | solution.py:318
  44.9 1.5 %collective-permute-done.10.refs_2_ = f32[160,128]{1,0:T(8,128)S(1)} collective-permute-done((f32[160,128]{1,0:T(8,128)S(1)}, f32[160,128]{1,0:T(8,128)S(1)}, u32[]{:S(2)}, u32[]{:S(2)}) %collective-permute-start.10) | collective-permute-done | bytes 81952 | tf_op jit(solution)/shard_map/ppermute | solution.py:318
  46.4 0.5 collective-permute-done.9.refs_1_
  47.0 0.1 collective-permute-start.12
  47.1 1.6 %collective-permute-done.12.refs_4_ = f32[640,128]{1,0:T(8,128)S(1)} collective-permute-done((f32[640,128]{1,0:T(8,128)S(1)}, f32[640,128]{1,0:T(8,128)S(1)}, u32[]{:S(2)}, u32[]{:S(2)}) %collective-permute-start.12) | collective-permute-done | bytes 327712 | tf_op jit(solution)/shard_map/ppermute | solution.py:318
  48.7 0.0 copy-done.1
  48.7 17.9 %factor.1 = (f32[512,512]{1,0:T(8,128)}, f32[512,128]{1,0:T(8,128)}, bf16[128,512]{1,0:T(8,128)(2,1)}) custom-call(f32[160,128]{1,0:T(8,128)S(1)} %add.23.refs_0_, f32[160,128]{1,0:T(8,128)S(1)} %collective-permute-done.9.refs_1_, f32[160,128]{1,0:T(8,128)S(1)} %collective-permute-done.10.refs_2_, f32[160,128]{1,0:T(8,128)S(1)} %collective-permute-done.11.refs_3_, ...), custom_call_target="tpu_custom_call" | custom-call | tf_op jit(solution)/shard_map/factor/pallas_call | solution.py:286
  (6 shorter events, 0.1 us)
Async XLA Ops:
  0.6 5.9 %copy-start.2 = (s32[1,1,4]{2,1,0:T(1,128)S(1)}, s32[1,1,4]{2,1,0:T(1,128)}, u32[]{:S(2)}) copy-start(s32[1,1,4]{2,1,0:T(1,128)} %owner_ref.3) | copy-start | bytes 52
  0.6 5.8 %copy-start = (bf16[128,2048]{1,0:T(8,128)(2,1)S(1)}, bf16[128,2048]{1,0:T(8,128)(2,1)}, u32[]{:S(2)}) copy-start(bf16[128,2048]{1,0:T(8,128)(2,1)} %slab_ref.2) | copy-start | bytes 1572868
  2.4 12.2 %collective-permute-start.1 = (bf16[128,512]{1,0:T(8,128)(2,1)}, bf16[128,512]{1,0:T(8,128)(2,1)S(1)}, u32[]{:S(2)}, u32[]{:S(2)}) collective-permute-start(bf16[128,512]{1,0:T(8,128)(2,1)} %pick_blocks.2), channel_id=1, source_target_pairs={{0,16},{8,24},{16,0},{24,8},{1,17},{9,25},{17,1},{25,9},{2,18},{10... | collective-permute-start | bytes 393224 | tf_op jit(solution)/shard_map/ppermute | solution.py:318
  7.1 7.6 %collective-permute-start = (bf16[128,512]{1,0:T(8,128)(2,1)S(1)}, bf16[128,512]{1,0:T(8,128)(2,1)S(1)}, u32[]{:S(2)}, u32[]{:S(2)}) collective-permute-start(bf16[128,512]{1,0:T(8,128)(2,1)S(1)} %get-tuple-element.11), channel_id=1, source_target_pairs={{0,8},{8,0},{16,24},{24,16},{1,9},{9,1},{17,25},{25,17},{2,10},{10... | collective-permute-start | bytes 393224 | tf_op jit(solution)/shard_map/ppermute | solution.py:318
  8.7 8.3 %collective-permute-start.2 = (bf16[128,512]{1,0:T(8,128)(2,1)S(1)}, bf16[128,512]{1,0:T(8,128)(2,1)S(1)}, u32[]{:S(2)}, u32[]{:S(2)}) collective-permute-start(bf16[128,512]{1,0:T(8,128)(2,1)S(1)} %get-tuple-element.12), channel_id=1, source_target_pairs={{0,24},{8,16},{16,8},{24,0},{1,25},{9,17},{17,9},{25,1},{2,26},{10... | collective-permute-start | bytes 393224 | tf_op jit(solution)/shard_map/ppermute | solution.py:318
  17.6 1.7 %collective-permute-start.3 = (f32[640,128]{1,0:T(8,128)S(1)}, f32[640,128]{1,0:T(8,128)S(1)}, u32[]{:S(2)}, u32[]{:S(2)}) collective-permute-start(f32[640,128]{1,0:T(8,128)S(1)} %get-tuple-element.14), channel_id=1, source_target_pairs={{0,2},{2,0},{4,6},{6,4},{1,3},{3,1},{5,7},{7,5},{8,10},{10,8},{12,... | collective-permute-start | bytes 983048 | tf_op jit(solution)/shard_map/ppermute | solution.py:318
  19.4 4.8 %collective-permute-start.4 = (f32[160,128]{1,0:T(8,128)S(1)}, f32[160,128]{1,0:T(8,128)S(1)}, u32[]{:S(2)}, u32[]{:S(2)}) collective-permute-start(f32[160,128]{1,0:T(8,128)S(1)} %get-tuple-element.15), channel_id=1, source_target_pairs={{0,1},{1,0},{2,3},{3,2},{4,5},{5,4},{6,7},{7,6},{8,9},{9,8},{10,11... | collective-permute-start | bytes 245768 | tf_op jit(solution)/shard_map/ppermute | solution.py:318
  21.0 6.1 %collective-permute-start.6 = (f32[160,128]{1,0:T(8,128)S(1)}, f32[160,128]{1,0:T(8,128)S(1)}, u32[]{:S(2)}, u32[]{:S(2)}) collective-permute-start(f32[160,128]{1,0:T(8,128)S(1)} %get-tuple-element.16), channel_id=1, source_target_pairs={{0,5},{1,4},{2,7},{3,6},{4,1},{5,0},{6,3},{7,2},{8,13},{9,12},{10,... | collective-permute-start | bytes 245768 | tf_op jit(solution)/shard_map/ppermute | solution.py:318
  22.4 4.7 %collective-permute-start.5 = (f32[160,128]{1,0:T(8,128)S(1)}, f32[160,128]{1,0:T(8,128)S(1)}, u32[]{:S(2)}, u32[]{:S(2)}) collective-permute-start(f32[160,128]{1,0:T(8,128)S(1)} %get-tuple-element.17), channel_id=1, source_target_pairs={{0,4},{1,5},{2,6},{3,7},{4,0},{5,1},{6,2},{7,3},{8,12},{9,13},{10,... | collective-permute-start | bytes 245768 | tf_op jit(solution)/shard_map/ppermute | solution.py:318
  27.1 4.8 %collective-permute-start.7 = (f32[160,128]{1,0:T(8,128)S(1)}, f32[160,128]{1,0:T(8,128)S(1)}, u32[]{:S(2)}, u32[]{:S(2)}) collective-permute-start(f32[160,128]{1,0:T(8,128)S(1)} %fusion.1), channel_id=1, source_target_pairs={{0,8},{8,0},{16,24},{24,16},{1,9},{9,1},{17,25},{25,17},{2,10},{10... | collective-permute-start | bytes 245768 | tf_op jit(solution)/shard_map/ppermute | solution.py:318
  32.0 7.5 %collective-permute-start.8 = (f32[160,128]{1,0:T(8,128)S(1)}, f32[160,128]{1,0:T(8,128)S(1)}, u32[]{:S(2)}, u32[]{:S(2)}) collective-permute-start(f32[160,128]{1,0:T(8,128)S(1)} %add.22), channel_id=1, source_target_pairs={{0,16},{8,24},{16,0},{24,8},{1,17},{9,25},{17,1},{25,9},{2,18},{10... | collective-permute-start | bytes 245768 | tf_op jit(solution)/shard_map/ppermute | solution.py:318
  39.5 9.2 %copy-start.1 = (f32[512,128]{1,0:T(8,128)S(1)}, f32[512,128]{1,0:T(8,128)}, u32[]{:S(2)}) copy-start(f32[512,128]{1,0:T(8,128)} %refs_5_.1) | copy-start | bytes 786436
  39.5 5.4 %collective-permute-start.11 = (f32[160,128]{1,0:T(8,128)S(1)}, f32[160,128]{1,0:T(8,128)S(1)}, u32[]{:S(2)}, u32[]{:S(2)}) collective-permute-start(f32[160,128]{1,0:T(8,128)S(1)} %add.23.refs_0_), channel_id=1, source_target_pairs={{0,5},{1,4},{2,7},{3,6},{4,1},{5,0},{6,3},{7,2},{8,13},{9,12},{10,... | collective-permute-start | bytes 245768 | tf_op jit(solution)/shard_map/ppermute | solution.py:318
  42.0 4.4 %collective-permute-start.10 = (f32[160,128]{1,0:T(8,128)S(1)}, f32[160,128]{1,0:T(8,128)S(1)}, u32[]{:S(2)}, u32[]{:S(2)}) collective-permute-start(f32[160,128]{1,0:T(8,128)S(1)} %add.23.refs_0_), channel_id=1, source_target_pairs={{0,4},{1,5},{2,6},{3,7},{4,0},{5,1},{6,2},{7,3},{8,12},{9,13},{10,... | collective-permute-start | bytes 245768 | tf_op jit(solution)/shard_map/ppermute | solution.py:318
  42.5 4.4 %collective-permute-start.9 = (f32[160,128]{1,0:T(8,128)S(1)}, f32[160,128]{1,0:T(8,128)S(1)}, u32[]{:S(2)}, u32[]{:S(2)}) collective-permute-start(f32[160,128]{1,0:T(8,128)S(1)} %add.23.refs_0_), channel_id=1, source_target_pairs={{0,1},{1,0},{2,3},{3,2},{4,5},{5,4},{6,7},{7,6},{8,9},{9,8},{10,11... | collective-permute-start | bytes 245768 | tf_op jit(solution)/shard_map/ppermute | solution.py:318
  47.0 1.7 %collective-permute-start.12 = (f32[640,128]{1,0:T(8,128)S(1)}, f32[640,128]{1,0:T(8,128)S(1)}, u32[]{:S(2)}, u32[]{:S(2)}) collective-permute-start(f32[640,128]{1,0:T(8,128)S(1)} %pad_maximum_fusion), channel_id=1, source_target_pairs={{0,2},{2,0},{4,6},{6,4},{1,3},{3,1},{5,7},{7,5},{8,10},{10,8},{12,... | collective-permute-start | bytes 983048 | tf_op jit(solution)/shard_map/ppermute | solution.py:318

commit v7 on v6

--- a/solution.py
+++ b/solution.py
@@ -122,6 +122,10 @@
     return [(i, j) for i in range(count) for j in range(i, count)]
 
 
+def summed_blocks(size, n, rows):
+    return [(i, j) for i, j in upper_blocks(size, n) if i < j or rows != n]
+
+
 def axis_bits(axis):
     size = lax.axis_size(axis)
     assert size & (size - 1) == 0, axis
@@ -179,55 +183,79 @@
 
 
 def gram_kernel(divisor, n, chunks, *refs):
-    pieces, (kept_ref, sent_ref, columns, blocks) = refs[:-4], refs[-4:]
+    slab_ref, pieces, (kept_ref, sent_ref, columns, blocks, own) = refs[0], refs[1:-5], refs[-5:]
     in_row_order(pieces, columns)
-    for b, (i, j) in enumerate(upper_blocks(columns.shape[0], n)):
+    shared = summed_blocks(columns.shape[0], n, slab_ref.shape[0])
+    for b, (i, j) in enumerate(shared):
         product = dot(columns[i * n : (i + 1) * n, :], columns[j * n : (j + 1) * n, :], NT)
         blocks[b * n : (b + 1) * n, :] = product / divisor
+    parts = [blocks]
+    if slab_ref.shape[0] == n:
+        own[...] = dot(slab_ref[...], slab_ref[...], NT) / divisor
+        parts.append(own)
     place = plane_place()
-    rows = blocks.shape[0] // chunks
+    rows = kept_ref.shape[0] // (chunks // 2)
     for slot in range(chunks):
-        start = pl.multiple_of(lax.bitwise_xor(place, slot) * rows, rows)
         target = kept_ref if slot < chunks // 2 else sent_ref
         at = slot % (chunks // 2) * rows
-        target[at : at + rows, :] = blocks[pl.ds(start, rows), :]
-
-
-def local_gram(pieces, divisor, n, chunks):
+        for part in parts:
+            height = part.shape[0] // chunks
+            start = pl.multiple_of(lax.bitwise_xor(place, slot) * height, height)
+            target[at : at + height, :] = part[pl.ds(start, height), :]
+            at += height
+
+
+def local_gram(slab, pieces, divisor, n, chunks):
     rows, width = pieces[0].shape
     size = rows * len(pieces)
-    total = len(upper_blocks(size, n)) * n
-    half = jax.ShapeDtypeStruct((total // 2, n), jnp.float32)
+    total = len(summed_blocks(size, n, rows)) * n
+    half = jax.ShapeDtypeStruct(((total + n * (rows == n)) // 2, n), jnp.float32)
     return pl.pallas_call(
         functools.partial(gram_kernel, divisor, n, chunks),
         out_shape=(half, half),
-        scratch_shapes=[pltpu.VMEM((size, width), pieces[0].dtype), pltpu.VMEM((total, n), jnp.float32)],
-        compiler_params=pltpu.CompilerParams(vmem_limit_bytes=32 * 1024 * 1024),
+        scratch_shapes=[
+            pltpu.VMEM((size, width), pieces[0].dtype),
+            pltpu.VMEM((total, n), jnp.float32),
+            pltpu.VMEM((n, n), jnp.float32),
+        ],
+        compiler_params=pltpu.CompilerParams(vmem_limit_bytes=16 * 1024 * 1024),
         name="local_gram",
-    )(*pieces)
+    )(slab, *pieces)
 
 
 def factor_kernel(chunks, fibers, *refs):
     slots, refs = refs[: chunks // 2], refs[chunks // 2 :]
     other_ref, basis_ref, refs = refs[0], refs[1], refs[2:]
     pieces, refs = refs[:fibers], refs[fibers:]
-    tri_ref, out_ref, core_ref, blocks_ref, columns, high, middle, lower, work, one, two = refs
+    tri_ref, out_ref, core_ref, blocks_ref, own_ref, columns, high, middle, lower, work, one, two = refs
     size = tri_ref.shape[0]
     n = basis_ref.shape[1]
     in_row_order(pieces, columns)
     place = plane_place()
+    me = fiber_place()
     rows = slots[0].shape[0]
+    height = blocks_ref.shape[0] // chunks
+    own = n // chunks
     for slot in range(chunks):
-        start = pl.multiple_of(lax.bitwise_xor(place, slot) * rows, rows)
-        at = slot % (chunks // 2)
         if slot < chunks // 2:
-            blocks_ref[pl.ds(start, rows), :] = slots[at][...]
+            chunk, at = slots[slot], 0
         else:
-            blocks_ref[pl.ds(start, rows), :] = other_ref[at * rows : (at + 1) * rows, :]
+            chunk, at = other_ref, (slot - chunks // 2) * rows
+        c = lax.bitwise_xor(place, slot)
+        blocks_ref[pl.ds(pl.multiple_of(c * height, height), height), :] = chunk[at : at + height, :]
+        for distance in range((rows - height) // own):
+            start = pl.multiple_of(lax.bitwise_xor(me, distance) * n + c * own, own)
+            low = at + height + distance * own
+            own_ref[pl.ds(start, own), :] = chunk[low : low + own, :]
     phases = size // n
     part = [slice(i * n, (i + 1) * n) for i in range(phases)]
-    for b, (i, j) in enumerate(upper_blocks(size, n)):
-        block = blocks_ref[b * n : (b + 1) * n, :]
+    shared = summed_blocks(size, n, pieces[0].shape[0])
+    for i, j in upper_blocks(size, n):
+        if (i, j) in shared:
+            b = shared.index((i, j))
+            block = blocks_ref[b * n : (b + 1) * n, :]
+        else:
+            block = own_ref[part[i], :]
         work[part[i], part[j]] = block
         for ref, piece in zip((high, middle, lower), split3(block)):
             ref[part[i], part[j]] = piece
@@ -291,7 +319,8 @@
             jax.ShapeDtypeStruct((n, width), jnp.bfloat16),
         ),
         scratch_shapes=[
-            pltpu.VMEM((2 * other.shape[0], n), jnp.float32),
+            pltpu.VMEM((len(summed_blocks(size, n, pieces[0].shape[0])) * n, n), jnp.float32),
+            pltpu.VMEM((size, n), jnp.float32),
             pltpu.VMEM((size, width), jnp.bfloat16),
             pltpu.VMEM((size, size), jnp.bfloat16),
             pltpu.VMEM((size, size), jnp.bfloat16),
@@ -318,15 +347,17 @@
     return lax.ppermute(value, axes, pairs)
 
 
-def sum_over_devices(kept, sent):
+def sum_over_devices(kept, sent, own):
     first, *groups = plane_groups()
     value = kept + swap(sent, first, 1)
     for bits in groups:
         part = value.shape[0] >> len(bits)
         cuts = [value[d * part : (d + 1) * part] for d in range(1 << len(bits))]
         value = sum([swap(cuts[d], bits, d) for d in range(1, len(cuts))], cuts[0])
+    height = value.shape[0] - own
     for bit in axis_bits("af"):
-        value = value + swap(value, [bit], 1)
+        got = swap(value, [bit], 1)
+        value = jnp.concatenate([value[:height] + got[:height], value[height:], got[height:]], axis=0)
     slots = [value]
     for bits in reversed(groups):
         whole = jnp.concatenate(slots, axis=0) if len(slots) > 1 else slots[0]
@@ -349,8 +380,9 @@
     pieces.update(pick_blocks(others, block_owner, slab, vmem_limit_bytes=8 * 1024 * 1024))
     pieces = [pieces[0]] + [swap(pieces[d], along, d) for d in range(1, fibers)]
     divisor = pieces[0].shape[1] * fibers * chunks
-    kept, sent = local_gram(pieces, divisor, basis_init.shape[1], chunks)
-    slots, other = sum_over_devices(kept, sent)
+    n = basis_init.shape[1]
+    kept, sent = local_gram(slab, pieces, divisor, n, chunks)
+    slots, other = sum_over_devices(kept, sent, n // chunks if slab.shape[0] == n else 0)
     return factor(slots, other, basis_init, pieces)
 
 

time: 66.8 us -> 65.3 us (0.978)
  waiting for transfers between devices: 25.4 us -> 23.7 us
    ppermute x13, waiting for transfers between devices: 25.4 us -> 23.7 us  [swap(): return lax.ppermute(value, axes, pairs)]
  transfers between devices with their start and end apart: 13 -> 13, of which waited for: 11 -> 10; matrix products, arithmetic and copies ran while one was open for 0% -> 0% of each run, Pallas kernels for 1% -> 1%
where the time goes in v7:
time: 65.3 us; the launch traced here: 65.2 us
  waiting for transfers between devices  23.7 us (36%)
  Pallas kernels  20.9 us (32%)
  starting transfers between devices  19.7 us (30%)
  between operations  0.77 us (1%)
    ppermute x13, waiting for transfers between devices, swap(): return lax.ppermute(value, axes, pairs)  23.7 us
    ppermute x13, starting transfers between devices, swap(): return lax.ppermute(value, axes, pairs)  19.7 us
    pallas_call x1, Pallas kernels, factor(): pl.pallas_call(functools.partial(factor_kernel, chunks, len(pieces)), out...  17.9 us
    pallas_call x2, Pallas kernels, pick_blocks(): pl.pallas_call(functools.partial(pick_kernel, distances), out_shape=(piec...  2.37 us
  transfers between devices with their start and end apart: 13, of which 10 were waited for; matrix products, arithmetic and copies ran while one was open for 0% of the time, Pallas kernels for 1%

profile of v7, /device:TPU:0, one launch (start us, length us, event | category | flops | bytes accessed | tf_op | source)
XLA Modules:
  0.0 65.2 jit_solution(8496763544509557426)
XLA Ops:
  0.6 0.0 copy-start.2
  0.6 0.0 copy-start
  0.6 1.8 %pick_blocks.2 = bf16[128,512]{1,0:T(8,128)(2,1)} custom-call(s32[1,1,4]{2,1,0:T(1,128)} %owner_ref.3, bf16[128,2048]{1,0:T(8,128)(2,1)} %refs_0_), custom_call_target="tpu_custom_call" | custom-call | tf_op jit(solution)/shard_map/pick_blocks/pallas_call | solution.py:167
  2.4 4.0 %collective-permute-start.1 = (bf16[128,512]{1,0:T(8,128)(2,1)}, bf16[128,512]{1,0:T(8,128)(2,1)S(1)}, u32[]{:S(2)}, u32[]{:S(2)}) collective-permute-start(bf16[128,512]{1,0:T(8,128)(2,1)} %pick_blocks.2), channel_id=1, source_target_pairs={{0,16},{8,24},{16,0},{24,8},{1,17},{9,25},{17,1},{25,9},{2,18},{10... | collective-permute-start | bytes 393224 | tf_op jit(solution)/shard_map/ppermute | solution.py:347
  6.5 0.0 copy-done.2
  6.5 0.0 copy-done
  6.5 0.6 pick_blocks.3
  7.1 1.6 %collective-permute-start = (bf16[128,512]{1,0:T(8,128)(2,1)S(1)}, bf16[128,512]{1,0:T(8,128)(2,1)S(1)}, u32[]{:S(2)}, u32[]{:S(2)}) collective-permute-start(bf16[128,512]{1,0:T(8,128)(2,1)S(1)} %get-tuple-element.11), channel_id=1, source_target_pairs={{0,8},{8,0},{16,24},{24,16},{1,9},{9,1},{17,25},{25,17},{2,10},{10... | collective-permute-start | bytes 393224 | tf_op jit(solution)/shard_map/ppermute | solution.py:347
  8.7 0.0 collective-permute-start.2
  8.7 5.9 %collective-permute-done.1.refs_3_.refs_8_ = bf16[128,512]{1,0:T(8,128)(2,1)S(1)} collective-permute-done((bf16[128,512]{1,0:T(8,128)(2,1)}, bf16[128,512]{1,0:T(8,128)(2,1)S(1)}, u32[]{:S(2)}, u32[]{:S(2)}) %collective-permute-start.1) | collective-permute-done | bytes 131104 | tf_op jit(solution)/shard_map/ppermute | solution.py:347
  14.6 0.0 collective-permute-done.refs_2_.refs_7_
  14.6 2.4 %collective-permute-done.2.refs_4_.refs_9_ = bf16[128,512]{1,0:T(8,128)(2,1)S(1)} collective-permute-done((bf16[128,512]{1,0:T(8,128)(2,1)S(1)}, bf16[128,512]{1,0:T(8,128)(2,1)S(1)}, u32[]{:S(2)}, u32[]{:S(2)}) %collective-permute-start.2) | collective-permute-done | bytes 131104 | tf_op jit(solution)/shard_map/ppermute | solution.py:347
  17.0 0.6 local_gram.1
  17.6 0.1 collective-permute-start.3
  17.7 1.5 %collective-permute-done.3 = f32[448,128]{1,0:T(8,128)S(1)} collective-permute-done((f32[448,128]{1,0:T(8,128)S(1)}, f32[448,128]{1,0:T(8,128)S(1)}, u32[]{:S(2)}, u32[]{:S(2)}) %collective-permute-start.3) | collective-permute-done | bytes 229408 | tf_op jit(solution)/shard_map/ppermute | solution.py:347
  19.2 1.6 %collective-permute-start.4 = (f32[112,128]{1,0:T(8,128)S(1)}, f32[112,128]{1,0:T(8,128)S(1)}, u32[]{:S(2)}, u32[]{:S(2)}) collective-permute-start(f32[112,128]{1,0:T(8,128)S(1)} %get-tuple-element.17), channel_id=1, source_target_pairs={{0,1},{1,0},{2,3},{3,2},{4,5},{5,4},{6,7},{7,6},{8,9},{9,8},{10,11... | collective-permute-start | bytes 172040 | tf_op jit(solution)/shard_map/ppermute | solution.py:347
  20.8 1.4 %collective-permute-start.6 = (f32[112,128]{1,0:T(8,128)S(1)}, f32[112,128]{1,0:T(8,128)S(1)}, u32[]{:S(2)}, u32[]{:S(2)}) collective-permute-start(f32[112,128]{1,0:T(8,128)S(1)} %get-tuple-element.18), channel_id=1, source_target_pairs={{0,5},{1,4},{2,7},{3,6},{4,1},{5,0},{6,3},{7,2},{8,13},{9,12},{10,... | collective-permute-start | bytes 172040 | tf_op jit(solution)/shard_map/ppermute | solution.py:347
  22.2 0.5 collective-permute-start.5
  22.8 0.7 %collective-permute-done.4 = f32[112,128]{1,0:T(8,128)S(1)} collective-permute-done((f32[112,128]{1,0:T(8,128)S(1)}, f32[112,128]{1,0:T(8,128)S(1)}, u32[]{:S(2)}, u32[]{:S(2)}) %collective-permute-start.4) | collective-permute-done | bytes 57376 | tf_op jit(solution)/shard_map/ppermute | solution.py:347
  23.5 2.9 %collective-permute-done.6 = f32[112,128]{1,0:T(8,128)S(1)} collective-permute-done((f32[112,128]{1,0:T(8,128)S(1)}, f32[112,128]{1,0:T(8,128)S(1)}, u32[]{:S(2)}, u32[]{:S(2)}) %collective-permute-start.6) | collective-permute-done | bytes 57376 | tf_op jit(solution)/shard_map/ppermute | solution.py:347
  26.4 0.0 collective-permute-done.5
  26.4 2.4 %collective-permute-start.7 = (f32[112,128]{1,0:T(8,128)S(1)}, f32[112,128]{1,0:T(8,128)S(1)}, u32[]{:S(2)}, u32[]{:S(2)}) collective-permute-start(f32[112,128]{1,0:T(8,128)S(1)} %fusion.1), channel_id=1, source_target_pairs={{0,8},{8,0},{16,24},{24,16},{1,9},{9,1},{17,25},{25,17},{2,10},{10... | collective-permute-start | bytes 172040 | tf_op jit(solution)/shard_map/ppermute | solution.py:347
  28.8 2.2 %collective-permute-done.7 = f32[112,128]{1,0:T(8,128)S(1)} collective-permute-done((f32[112,128]{1,0:T(8,128)S(1)}, f32[112,128]{1,0:T(8,128)S(1)}, u32[]{:S(2)}, u32[]{:S(2)}) %collective-permute-start.7) | collective-permute-done | bytes 57376 | tf_op jit(solution)/shard_map/ppermute | solution.py:347
  31.0 4.3 %collective-permute-start.8 = (f32[128,128]{1,0:T(8,128)S(1)}, f32[128,128]{1,0:T(8,128)S(1)}, u32[]{:S(2)}, u32[]{:S(2)}) collective-permute-start(f32[128,128]{1,0:T(8,128)S(1)} %pad_maximum_fusion.1), channel_id=1, source_target_pairs={{0,16},{8,24},{16,0},{24,8},{1,17},{9,25},{17,1},{25,9},{2,18},{10... | collective-permute-start | bytes 196616 | tf_op jit(solution)/shard_map/ppermute | solution.py:347
  35.3 2.9 %collective-permute-done.8 = f32[128,128]{1,0:T(8,128)S(1)} collective-permute-done((f32[128,128]{1,0:T(8,128)S(1)}, f32[128,128]{1,0:T(8,128)S(1)}, u32[]{:S(2)}, u32[]{:S(2)}) %collective-permute-start.8) | collective-permute-done | bytes 65568 | tf_op jit(solution)/shard_map/ppermute | solution.py:347
  38.3 0.0 copy-start.1
  38.4 1.7 %collective-permute-start.9 = (f32[160,128]{1,0:T(8,128)S(1)}, f32[160,128]{1,0:T(8,128)S(1)}, u32[]{:S(2)}, u32[]{:S(2)}) collective-permute-start(f32[160,128]{1,0:T(8,128)S(1)} %pad_maximum_fusion.refs_0_), channel_id=1, source_target_pairs={{0,1},{1,0},{2,3},{3,2},{4,5},{5,4},{6,7},{7,6},{8,9},{9,8},{10,11... | collective-permute-start | bytes 245768 | tf_op jit(solution)/shard_map/ppermute | solution.py:347
  40.0 1.0 %collective-permute-start.11 = (f32[160,128]{1,0:T(8,128)S(1)}, f32[160,128]{1,0:T(8,128)S(1)}, u32[]{:S(2)}, u32[]{:S(2)}) collective-permute-start(f32[160,128]{1,0:T(8,128)S(1)} %pad_maximum_fusion.refs_0_), channel_id=1, source_target_pairs={{0,5},{1,4},{2,7},{3,6},{4,1},{5,0},{6,3},{7,2},{8,13},{9,12},{10,... | collective-permute-start | bytes 245768 | tf_op jit(solution)/shard_map/ppermute | solution.py:347
  41.1 0.9 %collective-permute-start.10 = (f32[160,128]{1,0:T(8,128)S(1)}, f32[160,128]{1,0:T(8,128)S(1)}, u32[]{:S(2)}, u32[]{:S(2)}) collective-permute-start(f32[160,128]{1,0:T(8,128)S(1)} %pad_maximum_fusion.refs_0_), channel_id=1, source_target_pairs={{0,4},{1,5},{2,6},{3,7},{4,0},{5,1},{6,2},{7,3},{8,12},{9,13},{10,... | collective-permute-start | bytes 245768 | tf_op jit(solution)/shard_map/ppermute | solution.py:347
  41.9 1.0 %collective-permute-done.9.refs_1_ = f32[160,128]{1,0:T(8,128)S(1)} collective-permute-done((f32[160,128]{1,0:T(8,128)S(1)}, f32[160,128]{1,0:T(8,128)S(1)}, u32[]{:S(2)}, u32[]{:S(2)}) %collective-permute-start.9) | collective-permute-done | bytes 81952 | tf_op jit(solution)/shard_map/ppermute | solution.py:347
  42.9 2.6 %collective-permute-done.10.refs_2_ = f32[160,128]{1,0:T(8,128)S(1)} collective-permute-done((f32[160,128]{1,0:T(8,128)S(1)}, f32[160,128]{1,0:T(8,128)S(1)}, u32[]{:S(2)}, u32[]{:S(2)}) %collective-permute-start.10) | collective-permute-done | bytes 81952 | tf_op jit(solution)/shard_map/ppermute | solution.py:347
  45.5 0.0 collective-permute-done.11.refs_3_
  45.5 0.1 collective-permute-start.12
  45.6 1.6 %collective-permute-done.12.refs_4_ = f32[640,128]{1,0:T(8,128)S(1)} collective-permute-done((f32[640,128]{1,0:T(8,128)S(1)}, f32[640,128]{1,0:T(8,128)S(1)}, u32[]{:S(2)}, u32[]{:S(2)}) %collective-permute-start.12) | collective-permute-done | bytes 327712 | tf_op jit(solution)/shard_map/ppermute | solution.py:347
  47.2 0.0 copy-done.1
  47.2 17.9 %factor.1 = (f32[512,512]{1,0:T(8,128)}, f32[512,128]{1,0:T(8,128)}, bf16[128,512]{1,0:T(8,128)(2,1)}) custom-call(f32[160,128]{1,0:T(8,128)S(1)} %pad_maximum_fusion.refs_0_, f32[160,128]{1,0:T(8,128)S(1)} %collective-permute-done.9.refs_1_, f32[160,128]{1,0:T(8,128)S(1)} %collective-permute-done.10.refs_2_, ...), custom_call_target="tpu_custom_call" | custom-call | tf_op jit(solution)/shard_map/factor/pallas_call | solution.py:314
  (15 shorter events, 0.1 us)
Async XLA Ops:
  0.6 5.9 %copy-start.2 = (s32[1,1,4]{2,1,0:T(1,128)S(1)}, s32[1,1,4]{2,1,0:T(1,128)}, u32[]{:S(2)}) copy-start(s32[1,1,4]{2,1,0:T(1,128)} %owner_ref.3) | copy-start | bytes 52
  0.6 5.8 %copy-start = (bf16[128,2048]{1,0:T(8,128)(2,1)S(1)}, bf16[128,2048]{1,0:T(8,128)(2,1)}, u32[]{:S(2)}) copy-start(bf16[128,2048]{1,0:T(8,128)(2,1)} %refs_0_) | copy-start | bytes 1572868
  2.4 12.2 %collective-permute-start.1 = (bf16[128,512]{1,0:T(8,128)(2,1)}, bf16[128,512]{1,0:T(8,128)(2,1)S(1)}, u32[]{:S(2)}, u32[]{:S(2)}) collective-permute-start(bf16[128,512]{1,0:T(8,128)(2,1)} %pick_blocks.2), channel_id=1, source_target_pairs={{0,16},{8,24},{16,0},{24,8},{1,17},{9,25},{17,1},{25,9},{2,18},{10... | collective-permute-start | bytes 393224 | tf_op jit(solution)/shard_map/ppermute | solution.py:347
  7.1 7.6 %collective-permute-start = (bf16[128,512]{1,0:T(8,128)(2,1)S(1)}, bf16[128,512]{1,0:T(8,128)(2,1)S(1)}, u32[]{:S(2)}, u32[]{:S(2)}) collective-permute-start(bf16[128,512]{1,0:T(8,128)(2,1)S(1)} %get-tuple-element.11), channel_id=1, source_target_pairs={{0,8},{8,0},{16,24},{24,16},{1,9},{9,1},{17,25},{25,17},{2,10},{10... | collective-permute-start | bytes 393224 | tf_op jit(solution)/shard_map/ppermute | solution.py:347
  8.7 8.3 %collective-permute-start.2 = (bf16[128,512]{1,0:T(8,128)(2,1)S(1)}, bf16[128,512]{1,0:T(8,128)(2,1)S(1)}, u32[]{:S(2)}, u32[]{:S(2)}) collective-permute-start(bf16[128,512]{1,0:T(8,128)(2,1)S(1)} %get-tuple-element.12), channel_id=1, source_target_pairs={{0,24},{8,16},{16,8},{24,0},{1,25},{9,17},{17,9},{25,1},{2,26},{10... | collective-permute-start | bytes 393224 | tf_op jit(solution)/shard_map/ppermute | solution.py:347
  17.6 1.6 %collective-permute-start.3 = (f32[448,128]{1,0:T(8,128)S(1)}, f32[448,128]{1,0:T(8,128)S(1)}, u32[]{:S(2)}, u32[]{:S(2)}) collective-permute-start(f32[448,128]{1,0:T(8,128)S(1)} %get-tuple-element.14), channel_id=1, source_target_pairs={{0,2},{2,0},{4,6},{6,4},{1,3},{3,1},{5,7},{7,5},{8,10},{10,8},{12,... | collective-permute-start | bytes 688136 | tf_op jit(solution)/shard_map/ppermute | solution.py:347
  19.2 4.2 %collective-permute-start.4 = (f32[112,128]{1,0:T(8,128)S(1)}, f32[112,128]{1,0:T(8,128)S(1)}, u32[]{:S(2)}, u32[]{:S(2)}) collective-permute-start(f32[112,128]{1,0:T(8,128)S(1)} %get-tuple-element.17), channel_id=1, source_target_pairs={{0,1},{1,0},{2,3},{3,2},{4,5},{5,4},{6,7},{7,6},{8,9},{9,8},{10,11... | collective-permute-start | bytes 172040 | tf_op jit(solution)/shard_map/ppermute | solution.py:347
  20.8 5.6 %collective-permute-start.6 = (f32[112,128]{1,0:T(8,128)S(1)}, f32[112,128]{1,0:T(8,128)S(1)}, u32[]{:S(2)}, u32[]{:S(2)}) collective-permute-start(f32[112,128]{1,0:T(8,128)S(1)} %get-tuple-element.18), channel_id=1, source_target_pairs={{0,5},{1,4},{2,7},{3,6},{4,1},{5,0},{6,3},{7,2},{8,13},{9,12},{10,... | collective-permute-start | bytes 172040 | tf_op jit(solution)/shard_map/ppermute | solution.py:347
  22.2 4.2 %collective-permute-start.5 = (f32[112,128]{1,0:T(8,128)S(1)}, f32[112,128]{1,0:T(8,128)S(1)}, u32[]{:S(2)}, u32[]{:S(2)}) collective-permute-start(f32[112,128]{1,0:T(8,128)S(1)} %get-tuple-element.19), channel_id=1, source_target_pairs={{0,4},{1,5},{2,6},{3,7},{4,0},{5,1},{6,2},{7,3},{8,12},{9,13},{10,... | collective-permute-start | bytes 172040 | tf_op jit(solution)/shard_map/ppermute | solution.py:347
  26.4 4.5 %collective-permute-start.7 = (f32[112,128]{1,0:T(8,128)S(1)}, f32[112,128]{1,0:T(8,128)S(1)}, u32[]{:S(2)}, u32[]{:S(2)}) collective-permute-start(f32[112,128]{1,0:T(8,128)S(1)} %fusion.1), channel_id=1, source_target_pairs={{0,8},{8,0},{16,24},{24,16},{1,9},{9,1},{17,25},{25,17},{2,10},{10... | collective-permute-start | bytes 172040 | tf_op jit(solution)/shard_map/ppermute | solution.py:347
  31.0 7.3 %collective-permute-start.8 = (f32[128,128]{1,0:T(8,128)S(1)}, f32[128,128]{1,0:T(8,128)S(1)}, u32[]{:S(2)}, u32[]{:S(2)}) collective-permute-start(f32[128,128]{1,0:T(8,128)S(1)} %pad_maximum_fusion.1), channel_id=1, source_target_pairs={{0,16},{8,24},{16,0},{24,8},{1,17},{9,25},{17,1},{25,9},{2,18},{10... | collective-permute-start | bytes 196616 | tf_op jit(solution)/shard_map/ppermute | solution.py:347
  38.3 8.9 %copy-start.1 = (f32[512,128]{1,0:T(8,128)S(1)}, f32[512,128]{1,0:T(8,128)}, u32[]{:S(2)}) copy-start(f32[512,128]{1,0:T(8,128)} %refs_5_.1) | copy-start | bytes 786436
  38.4 4.5 %collective-permute-start.9 = (f32[160,128]{1,0:T(8,128)S(1)}, f32[160,128]{1,0:T(8,128)S(1)}, u32[]{:S(2)}, u32[]{:S(2)}) collective-permute-start(f32[160,128]{1,0:T(8,128)S(1)} %pad_maximum_fusion.refs_0_), channel_id=1, source_target_pairs={{0,1},{1,0},{2,3},{3,2},{4,5},{5,4},{6,7},{7,6},{8,9},{9,8},{10,11... | collective-permute-start | bytes 245768 | tf_op jit(solution)/shard_map/ppermute | solution.py:347
  40.0 5.5 %collective-permute-start.11 = (f32[160,128]{1,0:T(8,128)S(1)}, f32[160,128]{1,0:T(8,128)S(1)}, u32[]{:S(2)}, u32[]{:S(2)}) collective-permute-start(f32[160,128]{1,0:T(8,128)S(1)} %pad_maximum_fusion.refs_0_), channel_id=1, source_target_pairs={{0,5},{1,4},{2,7},{3,6},{4,1},{5,0},{6,3},{7,2},{8,13},{9,12},{10,... | collective-permute-start | bytes 245768 | tf_op jit(solution)/shard_map/ppermute | solution.py:347
  41.1 4.4 %collective-permute-start.10 = (f32[160,128]{1,0:T(8,128)S(1)}, f32[160,128]{1,0:T(8,128)S(1)}, u32[]{:S(2)}, u32[]{:S(2)}) collective-permute-start(f32[160,128]{1,0:T(8,128)S(1)} %pad_maximum_fusion.refs_0_), channel_id=1, source_target_pairs={{0,4},{1,5},{2,6},{3,7},{4,0},{5,1},{6,2},{7,3},{8,12},{9,13},{10,... | collective-permute-start | bytes 245768 | tf_op jit(solution)/shard_map/ppermute | solution.py:347
  45.5 1.7 %collective-permute-start.12 = (f32[640,128]{1,0:T(8,128)S(1)}, f32[640,128]{1,0:T(8,128)S(1)}, u32[]{:S(2)}, u32[]{:S(2)}) collective-permute-start(f32[640,128]{1,0:T(8,128)S(1)} %constant_dynamic-update-slice_fusion), channel_id=1, source_target_pairs={{0,2},{2,0},{4,6},{6,4},{1,3},{3,1},{5,7},{7,5},{8,10},{10,8},{12,... | collective-permute-start | bytes 983048 | tf_op jit(solution)/shard_map/ppermute | solution.py:347

commit v8 on v7

--- a/solution.py
+++ b/solution.py
@@ -355,9 +355,11 @@
         cuts = [value[d * part : (d + 1) * part] for d in range(1 << len(bits))]
         value = sum([swap(cuts[d], bits, d) for d in range(1, len(cuts))], cuts[0])
     height = value.shape[0] - own
-    for bit in axis_bits("af"):
-        got = swap(value, [bit], 1)
-        value = jnp.concatenate([value[:height] + got[:height], value[height:], got[height:]], axis=0)
+    along = axis_bits("af")
+    for bits in [along[b : b + 2][::-1] for b in range(0, len(along), 2)]:
+        got = [swap(value, bits, d) for d in range(1, 1 << len(bits))]
+        summed = sum([piece[:height] for piece in got], value[:height])
+        value = jnp.concatenate([summed, value[height:]] + [piece[height:] for piece in got], axis=0)
     slots = [value]
     for bits in reversed(groups):
         whole = jnp.concatenate(slots, axis=0) if len(slots) > 1 else slots[0]

time: 65.3 us -> 61.9 us (0.948)
  starting transfers between devices: 19.7 us -> 17.8 us
  waiting for transfers between devices: 23.7 us -> 22.2 us
    ppermute x13 -> x14, starting transfers between devices: 19.7 us -> 17.8 us  [swap(): return lax.ppermute(value, axes, pairs)]
    ppermute x13 -> x14, waiting for transfers between devices: 23.7 us -> 22.2 us  [swap(): return lax.ppermute(value, axes, pairs)]
  transfers between devices with their start and end apart: 13 -> 14, of which waited for: 10 -> 11; matrix products, arithmetic and copies ran while one was open for 0% -> 0% of each run, Pallas kernels for 1% -> 1%
where the time goes in v8:
time: 61.9 us; the launch traced here: 61.8 us
  waiting for transfers between devices  22.2 us (36%)
  Pallas kernels  20.9 us (34%)
  starting transfers between devices  17.8 us (29%)
  between operations  0.76 us (1%)
    ppermute x14, waiting for transfers between devices, swap(): return lax.ppermute(value, axes, pairs)  22.2 us
    pallas_call x1, Pallas kernels, factor(): pl.pallas_call(functools.partial(factor_kernel, chunks, len(pieces)), out...  17.9 us
    ppermute x14, starting transfers between devices, swap(): return lax.ppermute(value, axes, pairs)  17.8 us
    pallas_call x2, Pallas kernels, pick_blocks(): pl.pallas_call(functools.partial(pick_kernel, distances), out_shape=(piec...  2.37 us
  transfers between devices with their start and end apart: 14, of which 11 were waited for; matrix products, arithmetic and copies ran while one was open for 0% of the time, Pallas kernels for 1%

profile of v8, /device:TPU:0, one launch (start us, length us, event | category | flops | bytes accessed | tf_op | source)
XLA Modules:
  0.0 61.8 jit_solution(15039567293338463045)
XLA Ops:
  0.6 0.0 copy-start.2
  0.6 0.0 copy-start
  0.6 1.8 %pick_blocks.2 = bf16[128,512]{1,0:T(8,128)(2,1)} custom-call(s32[1,1,4]{2,1,0:T(1,128)} %owner_ref.3, bf16[128,2048]{1,0:T(8,128)(2,1)} %refs_0_), custom_call_target="tpu_custom_call" | custom-call | tf_op jit(solution)/shard_map/pick_blocks/pallas_call | solution.py:167
  2.4 4.0 %collective-permute-start.1 = (bf16[128,512]{1,0:T(8,128)(2,1)}, bf16[128,512]{1,0:T(8,128)(2,1)S(1)}, u32[]{:S(2)}, u32[]{:S(2)}) collective-permute-start(bf16[128,512]{1,0:T(8,128)(2,1)} %pick_blocks.2), channel_id=1, source_target_pairs={{0,16},{8,24},{16,0},{24,8},{1,17},{9,25},{17,1},{25,9},{2,18},{10... | collective-permute-start | bytes 393224 | tf_op jit(solution)/shard_map/ppermute | solution.py:347
  6.5 0.0 copy-done.2
  6.5 0.0 copy-done
  6.5 0.6 pick_blocks.3
  7.1 1.6 %collective-permute-start = (bf16[128,512]{1,0:T(8,128)(2,1)S(1)}, bf16[128,512]{1,0:T(8,128)(2,1)S(1)}, u32[]{:S(2)}, u32[]{:S(2)}) collective-permute-start(bf16[128,512]{1,0:T(8,128)(2,1)S(1)} %get-tuple-element.11), channel_id=1, source_target_pairs={{0,8},{8,0},{16,24},{24,16},{1,9},{9,1},{17,25},{25,17},{2,10},{10... | collective-permute-start | bytes 393224 | tf_op jit(solution)/shard_map/ppermute | solution.py:347
  8.7 0.0 collective-permute-start.2
  8.7 5.9 %collective-permute-done.1.refs_3_.refs_8_ = bf16[128,512]{1,0:T(8,128)(2,1)S(1)} collective-permute-done((bf16[128,512]{1,0:T(8,128)(2,1)}, bf16[128,512]{1,0:T(8,128)(2,1)S(1)}, u32[]{:S(2)}, u32[]{:S(2)}) %collective-permute-start.1) | collective-permute-done | bytes 131104 | tf_op jit(solution)/shard_map/ppermute | solution.py:347
  14.6 0.0 collective-permute-done.refs_2_.refs_7_
  14.6 2.4 %collective-permute-done.2.refs_4_.refs_9_ = bf16[128,512]{1,0:T(8,128)(2,1)S(1)} collective-permute-done((bf16[128,512]{1,0:T(8,128)(2,1)S(1)}, bf16[128,512]{1,0:T(8,128)(2,1)S(1)}, u32[]{:S(2)}, u32[]{:S(2)}) %collective-permute-start.2) | collective-permute-done | bytes 131104 | tf_op jit(solution)/shard_map/ppermute | solution.py:347
  17.0 0.6 local_gram.1
  17.6 0.1 collective-permute-start.3
  17.7 1.5 %collective-permute-done.3 = f32[448,128]{1,0:T(8,128)S(1)} collective-permute-done((f32[448,128]{1,0:T(8,128)S(1)}, f32[448,128]{1,0:T(8,128)S(1)}, u32[]{:S(2)}, u32[]{:S(2)}) %collective-permute-start.3) | collective-permute-done | bytes 229408 | tf_op jit(solution)/shard_map/ppermute | solution.py:347
  19.2 1.6 %collective-permute-start.4 = (f32[112,128]{1,0:T(8,128)S(1)}, f32[112,128]{1,0:T(8,128)S(1)}, u32[]{:S(2)}, u32[]{:S(2)}) collective-permute-start(f32[112,128]{1,0:T(8,128)S(1)} %get-tuple-element.17), channel_id=1, source_target_pairs={{0,1},{1,0},{2,3},{3,2},{4,5},{5,4},{6,7},{7,6},{8,9},{9,8},{10,11... | collective-permute-start | bytes 172040 | tf_op jit(solution)/shard_map/ppermute | solution.py:347
  20.8 1.4 %collective-permute-start.6 = (f32[112,128]{1,0:T(8,128)S(1)}, f32[112,128]{1,0:T(8,128)S(1)}, u32[]{:S(2)}, u32[]{:S(2)}) collective-permute-start(f32[112,128]{1,0:T(8,128)S(1)} %get-tuple-element.18), channel_id=1, source_target_pairs={{0,5},{1,4},{2,7},{3,6},{4,1},{5,0},{6,3},{7,2},{8,13},{9,12},{10,... | collective-permute-start | bytes 172040 | tf_op jit(solution)/shard_map/ppermute | solution.py:347
  22.2 0.5 collective-permute-start.5
  22.8 0.7 %collective-permute-done.4 = f32[112,128]{1,0:T(8,128)S(1)} collective-permute-done((f32[112,128]{1,0:T(8,128)S(1)}, f32[112,128]{1,0:T(8,128)S(1)}, u32[]{:S(2)}, u32[]{:S(2)}) %collective-permute-start.4) | collective-permute-done | bytes 57376 | tf_op jit(solution)/shard_map/ppermute | solution.py:347
  23.5 2.9 %collective-permute-done.6 = f32[112,128]{1,0:T(8,128)S(1)} collective-permute-done((f32[112,128]{1,0:T(8,128)S(1)}, f32[112,128]{1,0:T(8,128)S(1)}, u32[]{:S(2)}, u32[]{:S(2)}) %collective-permute-start.6) | collective-permute-done | bytes 57376 | tf_op jit(solution)/shard_map/ppermute | solution.py:347
  26.4 0.0 collective-permute-done.5
  26.4 2.5 %collective-permute-start.9 = (f32[112,128]{1,0:T(8,128)S(1)}, f32[112,128]{1,0:T(8,128)S(1)}, u32[]{:S(2)}, u32[]{:S(2)}) collective-permute-start(f32[112,128]{1,0:T(8,128)S(1)} %fusion.1), channel_id=1, source_target_pairs={{0,24},{8,16},{16,8},{24,0},{1,25},{9,17},{17,9},{25,1},{2,26},{10... | collective-permute-start | bytes 172040 | tf_op jit(solution)/shard_map/ppermute | solution.py:347
  28.9 1.9 %collective-permute-start.8 = (f32[112,128]{1,0:T(8,128)S(1)}, f32[112,128]{1,0:T(8,128)S(1)}, u32[]{:S(2)}, u32[]{:S(2)}) collective-permute-start(f32[112,128]{1,0:T(8,128)S(1)} %fusion.1), channel_id=1, source_target_pairs={{0,16},{8,24},{16,0},{24,8},{1,17},{9,25},{17,1},{25,9},{2,18},{10... | collective-permute-start | bytes 172040 | tf_op jit(solution)/shard_map/ppermute | solution.py:347
  30.8 0.5 collective-permute-start.7
  31.3 1.3 %collective-permute-done.9 = f32[112,128]{1,0:T(8,128)S(1)} collective-permute-done((f32[112,128]{1,0:T(8,128)S(1)}, f32[112,128]{1,0:T(8,128)S(1)}, u32[]{:S(2)}, u32[]{:S(2)}) %collective-permute-start.9) | collective-permute-done | bytes 57376 | tf_op jit(solution)/shard_map/ppermute | solution.py:347
  32.6 1.9 %collective-permute-done.8 = f32[112,128]{1,0:T(8,128)S(1)} collective-permute-done((f32[112,128]{1,0:T(8,128)S(1)}, f32[112,128]{1,0:T(8,128)S(1)}, u32[]{:S(2)}, u32[]{:S(2)}) %collective-permute-start.8) | collective-permute-done | bytes 57376 | tf_op jit(solution)/shard_map/ppermute | solution.py:347
  34.5 0.6 collective-permute-done.7
  35.2 0.0 copy-start.1
  35.2 1.5 %collective-permute-start.10 = (f32[160,128]{1,0:T(8,128)S(1)}, f32[160,128]{1,0:T(8,128)S(1)}, u32[]{:S(2)}, u32[]{:S(2)}) collective-permute-start(f32[160,128]{1,0:T(8,128)S(1)} %get-tuple-element.21.refs_0_), channel_id=1, source_target_pairs={{0,1},{1,0},{2,3},{3,2},{4,5},{5,4},{6,7},{7,6},{8,9},{9,8},{10,11... | collective-permute-start | bytes 245768 | tf_op jit(solution)/shard_map/ppermute | solution.py:347
  36.7 1.0 %collective-permute-start.12 = (f32[160,128]{1,0:T(8,128)S(1)}, f32[160,128]{1,0:T(8,128)S(1)}, u32[]{:S(2)}, u32[]{:S(2)}) collective-permute-start(f32[160,128]{1,0:T(8,128)S(1)} %get-tuple-element.21.refs_0_), channel_id=1, source_target_pairs={{0,5},{1,4},{2,7},{3,6},{4,1},{5,0},{6,3},{7,2},{8,13},{9,12},{10,... | collective-permute-start | bytes 245768 | tf_op jit(solution)/shard_map/ppermute | solution.py:347
  37.7 1.1 %collective-permute-start.11 = (f32[160,128]{1,0:T(8,128)S(1)}, f32[160,128]{1,0:T(8,128)S(1)}, u32[]{:S(2)}, u32[]{:S(2)}) collective-permute-start(f32[160,128]{1,0:T(8,128)S(1)} %get-tuple-element.21.refs_0_), channel_id=1, source_target_pairs={{0,4},{1,5},{2,6},{3,7},{4,0},{5,1},{6,2},{7,3},{8,12},{9,13},{10,... | collective-permute-start | bytes 245768 | tf_op jit(solution)/shard_map/ppermute | solution.py:347
  38.8 1.0 %collective-permute-done.10.refs_1_ = f32[160,128]{1,0:T(8,128)S(1)} collective-permute-done((f32[160,128]{1,0:T(8,128)S(1)}, f32[160,128]{1,0:T(8,128)S(1)}, u32[]{:S(2)}, u32[]{:S(2)}) %collective-permute-start.10) | collective-permute-done | bytes 81952 | tf_op jit(solution)/shard_map/ppermute | solution.py:347
  39.7 2.4 %collective-permute-done.11.refs_2_ = f32[160,128]{1,0:T(8,128)S(1)} collective-permute-done((f32[160,128]{1,0:T(8,128)S(1)}, f32[160,128]{1,0:T(8,128)S(1)}, u32[]{:S(2)}, u32[]{:S(2)}) %collective-permute-start.11) | collective-permute-done | bytes 81952 | tf_op jit(solution)/shard_map/ppermute | solution.py:347
  42.1 0.0 collective-permute-done.12.refs_3_
  42.2 0.1 collective-permute-start.13
  42.2 1.6 %collective-permute-done.13.refs_4_ = f32[640,128]{1,0:T(8,128)S(1)} collective-permute-done((f32[640,128]{1,0:T(8,128)S(1)}, f32[640,128]{1,0:T(8,128)S(1)}, u32[]{:S(2)}, u32[]{:S(2)}) %collective-permute-start.13) | collective-permute-done | bytes 327712 | tf_op jit(solution)/shard_map/ppermute | solution.py:347
  43.9 0.0 copy-done.1
  43.9 17.9 %factor.1 = (f32[512,512]{1,0:T(8,128)}, f32[512,128]{1,0:T(8,128)}, bf16[128,512]{1,0:T(8,128)(2,1)}) custom-call(f32[160,128]{1,0:T(8,128)S(1)} %get-tuple-element.21.refs_0_, f32[160,128]{1,0:T(8,128)S(1)} %collective-permute-done.10.refs_1_, f32[160,128]{1,0:T(8,128)S(1)} %collective-permute-done.11.refs_2_, ...), custom_call_target="tpu_custom_call" | custom-call | tf_op jit(solution)/shard_map/factor/pallas_call | solution.py:314
  (12 shorter events, 0.1 us)
Async XLA Ops:
  0.6 5.9 %copy-start.2 = (s32[1,1,4]{2,1,0:T(1,128)S(1)}, s32[1,1,4]{2,1,0:T(1,128)}, u32[]{:S(2)}) copy-start(s32[1,1,4]{2,1,0:T(1,128)} %owner_ref.3) | copy-start | bytes 52
  0.6 5.8 %copy-start = (bf16[128,2048]{1,0:T(8,128)(2,1)S(1)}, bf16[128,2048]{1,0:T(8,128)(2,1)}, u32[]{:S(2)}) copy-start(bf16[128,2048]{1,0:T(8,128)(2,1)} %refs_0_) | copy-start | bytes 1572868
  2.4 12.2 %collective-permute-start.1 = (bf16[128,512]{1,0:T(8,128)(2,1)}, bf16[128,512]{1,0:T(8,128)(2,1)S(1)}, u32[]{:S(2)}, u32[]{:S(2)}) collective-permute-start(bf16[128,512]{1,0:T(8,128)(2,1)} %pick_blocks.2), channel_id=1, source_target_pairs={{0,16},{8,24},{16,0},{24,8},{1,17},{9,25},{17,1},{25,9},{2,18},{10... | collective-permute-start | bytes 393224 | tf_op jit(solution)/shard_map/ppermute | solution.py:347
  7.1 7.6 %collective-permute-start = (bf16[128,512]{1,0:T(8,128)(2,1)S(1)}, bf16[128,512]{1,0:T(8,128)(2,1)S(1)}, u32[]{:S(2)}, u32[]{:S(2)}) collective-permute-start(bf16[128,512]{1,0:T(8,128)(2,1)S(1)} %get-tuple-element.11), channel_id=1, source_target_pairs={{0,8},{8,0},{16,24},{24,16},{1,9},{9,1},{17,25},{25,17},{2,10},{10... | collective-permute-start | bytes 393224 | tf_op jit(solution)/shard_map/ppermute | solution.py:347
  8.7 8.3 %collective-permute-start.2 = (bf16[128,512]{1,0:T(8,128)(2,1)S(1)}, bf16[128,512]{1,0:T(8,128)(2,1)S(1)}, u32[]{:S(2)}, u32[]{:S(2)}) collective-permute-start(bf16[128,512]{1,0:T(8,128)(2,1)S(1)} %get-tuple-element.12), channel_id=1, source_target_pairs={{0,24},{8,16},{16,8},{24,0},{1,25},{9,17},{17,9},{25,1},{2,26},{10... | collective-permute-start | bytes 393224 | tf_op jit(solution)/shard_map/ppermute | solution.py:347
  17.6 1.6 %collective-permute-start.3 = (f32[448,128]{1,0:T(8,128)S(1)}, f32[448,128]{1,0:T(8,128)S(1)}, u32[]{:S(2)}, u32[]{:S(2)}) collective-permute-start(f32[448,128]{1,0:T(8,128)S(1)} %get-tuple-element.14), channel_id=1, source_target_pairs={{0,2},{2,0},{4,6},{6,4},{1,3},{3,1},{5,7},{7,5},{8,10},{10,8},{12,... | collective-permute-start | bytes 688136 | tf_op jit(solution)/shard_map/ppermute | solution.py:347
  19.2 4.2 %collective-permute-start.4 = (f32[112,128]{1,0:T(8,128)S(1)}, f32[112,128]{1,0:T(8,128)S(1)}, u32[]{:S(2)}, u32[]{:S(2)}) collective-permute-start(f32[112,128]{1,0:T(8,128)S(1)} %get-tuple-element.17), channel_id=1, source_target_pairs={{0,1},{1,0},{2,3},{3,2},{4,5},{5,4},{6,7},{7,6},{8,9},{9,8},{10,11... | collective-permute-start | bytes 172040 | tf_op jit(solution)/shard_map/ppermute | solution.py:347
  20.8 5.6 %collective-permute-start.6 = (f32[112,128]{1,0:T(8,128)S(1)}, f32[112,128]{1,0:T(8,128)S(1)}, u32[]{:S(2)}, u32[]{:S(2)}) collective-permute-start(f32[112,128]{1,0:T(8,128)S(1)} %get-tuple-element.18), channel_id=1, source_target_pairs={{0,5},{1,4},{2,7},{3,6},{4,1},{5,0},{6,3},{7,2},{8,13},{9,12},{10,... | collective-permute-start | bytes 172040 | tf_op jit(solution)/shard_map/ppermute | solution.py:347
  22.2 4.2 %collective-permute-start.5 = (f32[112,128]{1,0:T(8,128)S(1)}, f32[112,128]{1,0:T(8,128)S(1)}, u32[]{:S(2)}, u32[]{:S(2)}) collective-permute-start(f32[112,128]{1,0:T(8,128)S(1)} %get-tuple-element.19), channel_id=1, source_target_pairs={{0,4},{1,5},{2,6},{3,7},{4,0},{5,1},{6,2},{7,3},{8,12},{9,13},{10,... | collective-permute-start | bytes 172040 | tf_op jit(solution)/shard_map/ppermute | solution.py:347
  26.4 6.2 %collective-permute-start.9 = (f32[112,128]{1,0:T(8,128)S(1)}, f32[112,128]{1,0:T(8,128)S(1)}, u32[]{:S(2)}, u32[]{:S(2)}) collective-permute-start(f32[112,128]{1,0:T(8,128)S(1)} %fusion.1), channel_id=1, source_target_pairs={{0,24},{8,16},{16,8},{24,0},{1,25},{9,17},{17,9},{25,1},{2,26},{10... | collective-permute-start | bytes 172040 | tf_op jit(solution)/shard_map/ppermute | solution.py:347
  28.9 5.6 %collective-permute-start.8 = (f32[112,128]{1,0:T(8,128)S(1)}, f32[112,128]{1,0:T(8,128)S(1)}, u32[]{:S(2)}, u32[]{:S(2)}) collective-permute-start(f32[112,128]{1,0:T(8,128)S(1)} %fusion.1), channel_id=1, source_target_pairs={{0,16},{8,24},{16,0},{24,8},{1,17},{9,25},{17,1},{25,9},{2,18},{10... | collective-permute-start | bytes 172040 | tf_op jit(solution)/shard_map/ppermute | solution.py:347
  30.8 4.3 %collective-permute-start.7 = (f32[112,128]{1,0:T(8,128)S(1)}, f32[112,128]{1,0:T(8,128)S(1)}, u32[]{:S(2)}, u32[]{:S(2)}) collective-permute-start(f32[112,128]{1,0:T(8,128)S(1)} %fusion.1), channel_id=1, source_target_pairs={{0,8},{8,0},{16,24},{24,16},{1,9},{9,1},{17,25},{25,17},{2,10},{10... | collective-permute-start | bytes 172040 | tf_op jit(solution)/shard_map/ppermute | solution.py:347
  35.2 8.7 %copy-start.1 = (f32[512,128]{1,0:T(8,128)S(1)}, f32[512,128]{1,0:T(8,128)}, u32[]{:S(2)}) copy-start(f32[512,128]{1,0:T(8,128)} %refs_5_.1) | copy-start | bytes 786436
  35.2 4.5 %collective-permute-start.10 = (f32[160,128]{1,0:T(8,128)S(1)}, f32[160,128]{1,0:T(8,128)S(1)}, u32[]{:S(2)}, u32[]{:S(2)}) collective-permute-start(f32[160,128]{1,0:T(8,128)S(1)} %get-tuple-element.21.refs_0_), channel_id=1, source_target_pairs={{0,1},{1,0},{2,3},{3,2},{4,5},{5,4},{6,7},{7,6},{8,9},{9,8},{10,11... | collective-permute-start | bytes 245768 | tf_op jit(solution)/shard_map/ppermute | solution.py:347
  36.7 5.5 %collective-permute-start.12 = (f32[160,128]{1,0:T(8,128)S(1)}, f32[160,128]{1,0:T(8,128)S(1)}, u32[]{:S(2)}, u32[]{:S(2)}) collective-permute-start(f32[160,128]{1,0:T(8,128)S(1)} %get-tuple-element.21.refs_0_), channel_id=1, source_target_pairs={{0,5},{1,4},{2,7},{3,6},{4,1},{5,0},{6,3},{7,2},{8,13},{9,12},{10,... | collective-permute-start | bytes 245768 | tf_op jit(solution)/shard_map/ppermute | solution.py:347
  37.7 4.4 %collective-permute-start.11 = (f32[160,128]{1,0:T(8,128)S(1)}, f32[160,128]{1,0:T(8,128)S(1)}, u32[]{:S(2)}, u32[]{:S(2)}) collective-permute-start(f32[160,128]{1,0:T(8,128)S(1)} %get-tuple-element.21.refs_0_), channel_id=1, source_target_pairs={{0,4},{1,5},{2,6},{3,7},{4,0},{5,1},{6,2},{7,3},{8,12},{9,13},{10,... | collective-permute-start | bytes 245768 | tf_op jit(solution)/shard_map/ppermute | solution.py:347
  42.2 1.7 %collective-permute-start.13 = (f32[640,128]{1,0:T(8,128)S(1)}, f32[640,128]{1,0:T(8,128)S(1)}, u32[]{:S(2)}, u32[]{:S(2)}) collective-permute-start(f32[640,128]{1,0:T(8,128)S(1)} %constant_dynamic-update-slice_fusion.5), channel_id=1, source_target_pairs={{0,2},{2,0},{4,6},{6,4},{1,3},{3,1},{5,7},{7,5},{8,10},{10,8},{12,... | collective-permute-start | bytes 983048 | tf_op jit(solution)/shard_map/ppermute | solution.py:347

commit v9 on v8

--- a/solution.py
+++ b/solution.py
@@ -11,6 +11,7 @@
 ITERS = 2
 GROUP = 32
 BLOCK = 16
+LIMIT = 2500.0
 TILE = 8
 
 
@@ -55,6 +56,12 @@
     return first[:, :n] + (first[:, n:] + second[:, :n] + (second[:, n:] + small))
 
 
+def rows_of(start, size):
+    if isinstance(start, int):
+        return slice(start, start + size)
+    return pl.ds(pl.multiple_of(start, TILE), size)
+
+
 def eliminate(states, start, n):
     shape = (TILE, n)
     tiles = GROUP // TILE
@@ -65,7 +72,7 @@
 
     halves = [
         [
-            [state[start + t * TILE : start + (t + 1) * TILE, side] for t in range(tiles)]
+            [state[rows_of(start + t * TILE, TILE), side] for t in range(tiles)]
             for side in (slice(0, n), slice(n, 2 * n))
         ]
         for state in states
@@ -104,16 +111,20 @@
                     across = spread(side, i)
                     for t in below:
                         side[t] = side[t] - factor[t] * across
-    rows = slice(start, start + GROUP)
-    rest = slice(start + GROUP, n)
+    rows = rows_of(start, GROUP)
+    lane = lax.broadcasted_iota(jnp.int32, (GROUP, n), 1)
     for state, sides, pivot_of in zip(states, halves, pivots):
         scale = jnp.concatenate([lax.rsqrt(p) for p in pivot_of], axis=0)
         left, right = [jnp.concatenate(side, axis=0) * scale for side in sides]
         state[rows, :n] = left
         state[rows, n:] = right
-        if start + GROUP < n:
-            lhs = split3(left)
-            rhs = [jnp.concatenate(pair, axis=1) for pair in zip(lhs, split3(right))]
+        lhs = split3(left)
+        rhs = [jnp.concatenate(pair, axis=1) for pair in zip(lhs, split3(right))]
+        if not isinstance(start, int):
+            lhs = [jnp.where(lane >= start + GROUP, x, jnp.zeros_like(x)) for x in lhs]
+            state[...] = state[...] - deep_dot(lhs, rhs, TN)
+        elif start + GROUP < n:
+            rest = slice(start + GROUP, n)
             state[rest, :] = state[rest, :] - deep_dot(lhs, rhs, TN)[rest, :]
 
 
@@ -227,7 +238,7 @@
     slots, refs = refs[: chunks // 2], refs[chunks // 2 :]
     other_ref, basis_ref, refs = refs[0], refs[1], refs[2:]
     pieces, refs = refs[:fibers], refs[fibers:]
-    tri_ref, out_ref, core_ref, blocks_ref, own_ref, columns, high, middle, lower, work, one, two = refs
+    tri_ref, out_ref, core_ref, blocks_ref, own_ref, columns, high, middle, lower, work, one, two, first = refs
     size = tri_ref.shape[0]
     n = basis_ref.shape[1]
     in_row_order(pieces, columns)
@@ -267,23 +278,21 @@
         lax.broadcasted_iota(jnp.int32, (n, n), 0) == lax.broadcasted_iota(jnp.int32, (n, n), 1)
     ).astype(jnp.float32)
     upper = lax.broadcasted_iota(jnp.int32, (n, n), 0) <= lax.broadcasted_iota(jnp.int32, (n, n), 1)
-    basis = basis_ref[...]
-    for phase in range(max(phases, 2 * ITERS)):
+    whole = (high, middle, lower)
+    value = basis_ref[...]
+    doubtful = jnp.zeros((1, 1), jnp.float32)
+    for phase in range(max(phases, ITERS + 1)):
         if phase < phases:
             at = part[phase]
             one[:, :n] = work[at, at]
             one[:, n:] = eye
-        if phase < 2 * ITERS:
-            if phase % 2 == 0:
-                parts = split3(basis)
-                wide = split3(wide_dot((high[...], middle[...], lower[...]), parts, NN))
-                two[:, :n] = wide_dot(parts, wide, TN)
-            else:
-                wide = split3(wide)
-                two[:, :n] = wide_dot(wide, wide, TN)
+        if phase <= ITERS:
+            pieces = split3(value)
+            wide = split3(wide_dot([ref[...] for ref in whole], pieces, NN)) if phase < ITERS else pieces
+            inner = wide_dot(pieces, wide, TN)
+            two[:, :n] = inner
             two[:, n:] = eye
-
-        states = [one] * (phase < phases) + [two] * (phase < 2 * ITERS)
+        states = [one] * (phase < phases) + [two] * (phase <= ITERS)
         for group in range(n // GROUP):
             eliminate(states, group * GROUP, n)
         if phase < phases:
@@ -299,12 +308,34 @@
                     work[part[i], i * n :] = work[part[i], i * n :] - deep_dot(
                         [x[:, mine] for x in pieces], [x[:, tail] for x in pieces], TN
                     )
-        if phase < 2 * ITERS:
-            wide = short_dot(wide, split3(two[:, n:]), NT)
-            if phase % 2 == 1:
-                basis = wide
-    out_ref[...] = basis
-    core_ref[...] = dot(basis.astype(jnp.bfloat16), columns[...], TN).astype(jnp.bfloat16)
+        if phase <= ITERS:
+            if 0 < phase < ITERS:
+                most = jnp.max(jnp.abs(two[:, n:]), axis=(0, 1), keepdims=True)
+                spread = most * most * jnp.max(inner, axis=(0, 1), keepdims=True)
+                doubtful = jnp.where(spread < LIMIT, doubtful, 1.0)
+            value = short_dot(wide, split3(two[:, n:]), NT)
+            if phase == 0:
+                first[...] = value
+    out_ref[...] = value
+
+    @pl.when(doubtful[0, 0] > 0.0)
+    def _():
+        value = first[...]
+        for half in range(1, 2 * ITERS):
+            pieces = split3(value)
+            wide = split3(wide_dot([ref[...] for ref in whole], pieces, NN)) if half % 2 == 0 else pieces
+            two[:, :n] = wide_dot(pieces, wide, TN)
+            two[:, n:] = eye
+
+            def step(group, carry):
+                eliminate([two], group * GROUP, n)
+                return carry
+
+            lax.fori_loop(0, n // GROUP, step, 0)
+            value = short_dot(wide, split3(two[:, n:]), NT)
+        out_ref[...] = value
+
+    core_ref[...] = dot(out_ref[...].astype(jnp.bfloat16), columns[...], TN).astype(jnp.bfloat16)
 
 
 def factor(slots, other, basis, pieces):
@@ -328,6 +359,7 @@
             pltpu.VMEM((size, size), jnp.float32),
             pltpu.VMEM((n, 2 * n), jnp.float32),
             pltpu.VMEM((n, 2 * n), jnp.float32),
+            pltpu.VMEM((size, n), jnp.float32),
         ],
         compiler_params=pltpu.CompilerParams(vmem_limit_bytes=32 * 1024 * 1024),
         name="factor",

time: 61.9 us -> 60.6 us (0.979)
  Pallas kernels: 20.9 us -> 19.5 us
    pallas_call x1, Pallas kernels: 17.9 us -> 16.6 us  [factor(): pl.pallas_call(functools.partial(factor_kernel, chunks, len(pieces)), out...]
where the time goes in v9:
time: 60.6 us; the launch traced here: 60.4 us
  waiting for transfers between devices  22.2 us (37%)
  Pallas kernels  19.5 us (32%)
  starting transfers between devices  17.8 us (29%)
  between operations  0.76 us (1%)
    ppermute x14, waiting for transfers between devices, swap(): return lax.ppermute(value, axes, pairs)  22.2 us
    ppermute x14, starting transfers between devices, swap(): return lax.ppermute(value, axes, pairs)  17.8 us
    pallas_call x1, Pallas kernels, factor(): pl.pallas_call(functools.partial(factor_kernel, chunks, len(pieces)), out...  16.6 us
    pallas_call x2, Pallas kernels, pick_blocks(): pl.pallas_call(functools.partial(pick_kernel, distances), out_shape=(piec...  2.37 us
  transfers between devices with their start and end apart: 14, of which 11 were waited for; matrix products, arithmetic and copies ran while one was open for 0% of the time, Pallas kernels for 1%

profile of v9, /device:TPU:0, one launch (start us, length us, event | category | flops | bytes accessed | tf_op | source)
XLA Modules:
  0.0 60.4 jit_solution(10860008987073408291)
XLA Ops:
  0.6 0.0 copy-start.2
  0.6 0.0 copy-start
  0.6 1.8 %pick_blocks.2 = bf16[128,512]{1,0:T(8,128)(2,1)} custom-call(s32[1,1,4]{2,1,0:T(1,128)} %owner_ref.3, bf16[128,2048]{1,0:T(8,128)(2,1)} %refs_0_), custom_call_target="tpu_custom_call" | custom-call | tf_op jit(solution)/shard_map/pick_blocks/pallas_call | solution.py:178
  2.4 4.0 %collective-permute-start.1 = (bf16[128,512]{1,0:T(8,128)(2,1)}, bf16[128,512]{1,0:T(8,128)(2,1)S(1)}, u32[]{:S(2)}, u32[]{:S(2)}) collective-permute-start(bf16[128,512]{1,0:T(8,128)(2,1)} %pick_blocks.2), channel_id=1, source_target_pairs={{0,16},{8,24},{16,0},{24,8},{1,17},{9,25},{17,1},{25,9},{2,18},{10... | collective-permute-start | bytes 393224 | tf_op jit(solution)/shard_map/ppermute | solution.py:379
  6.5 0.0 copy-done.2
  6.5 0.0 copy-done
  6.5 0.6 pick_blocks.3
  7.1 1.6 %collective-permute-start = (bf16[128,512]{1,0:T(8,128)(2,1)S(1)}, bf16[128,512]{1,0:T(8,128)(2,1)S(1)}, u32[]{:S(2)}, u32[]{:S(2)}) collective-permute-start(bf16[128,512]{1,0:T(8,128)(2,1)S(1)} %get-tuple-element.11), channel_id=1, source_target_pairs={{0,8},{8,0},{16,24},{24,16},{1,9},{9,1},{17,25},{25,17},{2,10},{10... | collective-permute-start | bytes 393224 | tf_op jit(solution)/shard_map/ppermute | solution.py:379
  8.7 0.0 collective-permute-start.2
  8.7 5.9 %collective-permute-done.1.refs_3_.refs_8_ = bf16[128,512]{1,0:T(8,128)(2,1)S(1)} collective-permute-done((bf16[128,512]{1,0:T(8,128)(2,1)}, bf16[128,512]{1,0:T(8,128)(2,1)S(1)}, u32[]{:S(2)}, u32[]{:S(2)}) %collective-permute-start.1) | collective-permute-done | bytes 131104 | tf_op jit(solution)/shard_map/ppermute | solution.py:379
  14.6 0.0 collective-permute-done.refs_2_.refs_7_
  14.6 2.4 %collective-permute-done.2.refs_4_.refs_9_ = bf16[128,512]{1,0:T(8,128)(2,1)S(1)} collective-permute-done((bf16[128,512]{1,0:T(8,128)(2,1)S(1)}, bf16[128,512]{1,0:T(8,128)(2,1)S(1)}, u32[]{:S(2)}, u32[]{:S(2)}) %collective-permute-start.2) | collective-permute-done | bytes 131104 | tf_op jit(solution)/shard_map/ppermute | solution.py:379
  17.0 0.6 local_gram.1
  17.6 0.1 collective-permute-start.3
  17.7 1.5 %collective-permute-done.3 = f32[448,128]{1,0:T(8,128)S(1)} collective-permute-done((f32[448,128]{1,0:T(8,128)S(1)}, f32[448,128]{1,0:T(8,128)S(1)}, u32[]{:S(2)}, u32[]{:S(2)}) %collective-permute-start.3) | collective-permute-done | bytes 229408 | tf_op jit(solution)/shard_map/ppermute | solution.py:379
  19.2 1.6 %collective-permute-start.4 = (f32[112,128]{1,0:T(8,128)S(1)}, f32[112,128]{1,0:T(8,128)S(1)}, u32[]{:S(2)}, u32[]{:S(2)}) collective-permute-start(f32[112,128]{1,0:T(8,128)S(1)} %get-tuple-element.17), channel_id=1, source_target_pairs={{0,1},{1,0},{2,3},{3,2},{4,5},{5,4},{6,7},{7,6},{8,9},{9,8},{10,11... | collective-permute-start | bytes 172040 | tf_op jit(solution)/shard_map/ppermute | solution.py:379
  20.8 1.4 %collective-permute-start.6 = (f32[112,128]{1,0:T(8,128)S(1)}, f32[112,128]{1,0:T(8,128)S(1)}, u32[]{:S(2)}, u32[]{:S(2)}) collective-permute-start(f32[112,128]{1,0:T(8,128)S(1)} %get-tuple-element.18), channel_id=1, source_target_pairs={{0,5},{1,4},{2,7},{3,6},{4,1},{5,0},{6,3},{7,2},{8,13},{9,12},{10,... | collective-permute-start | bytes 172040 | tf_op jit(solution)/shard_map/ppermute | solution.py:379
  22.2 0.5 collective-permute-start.5
  22.8 0.7 %collective-permute-done.4 = f32[112,128]{1,0:T(8,128)S(1)} collective-permute-done((f32[112,128]{1,0:T(8,128)S(1)}, f32[112,128]{1,0:T(8,128)S(1)}, u32[]{:S(2)}, u32[]{:S(2)}) %collective-permute-start.4) | collective-permute-done | bytes 57376 | tf_op jit(solution)/shard_map/ppermute | solution.py:379
  23.5 2.9 %collective-permute-done.6 = f32[112,128]{1,0:T(8,128)S(1)} collective-permute-done((f32[112,128]{1,0:T(8,128)S(1)}, f32[112,128]{1,0:T(8,128)S(1)}, u32[]{:S(2)}, u32[]{:S(2)}) %collective-permute-start.6) | collective-permute-done | bytes 57376 | tf_op jit(solution)/shard_map/ppermute | solution.py:379
  26.4 0.0 collective-permute-done.5
  26.4 2.5 %collective-permute-start.9 = (f32[112,128]{1,0:T(8,128)S(1)}, f32[112,128]{1,0:T(8,128)S(1)}, u32[]{:S(2)}, u32[]{:S(2)}) collective-permute-start(f32[112,128]{1,0:T(8,128)S(1)} %fusion.1), channel_id=1, source_target_pairs={{0,24},{8,16},{16,8},{24,0},{1,25},{9,17},{17,9},{25,1},{2,26},{10... | collective-permute-start | bytes 172040 | tf_op jit(solution)/shard_map/ppermute | solution.py:379
  28.9 1.9 %collective-permute-start.8 = (f32[112,128]{1,0:T(8,128)S(1)}, f32[112,128]{1,0:T(8,128)S(1)}, u32[]{:S(2)}, u32[]{:S(2)}) collective-permute-start(f32[112,128]{1,0:T(8,128)S(1)} %fusion.1), channel_id=1, source_target_pairs={{0,16},{8,24},{16,0},{24,8},{1,17},{9,25},{17,1},{25,9},{2,18},{10... | collective-permute-start | bytes 172040 | tf_op jit(solution)/shard_map/ppermute | solution.py:379
  30.8 0.5 collective-permute-start.7
  31.3 1.3 %collective-permute-done.9 = f32[112,128]{1,0:T(8,128)S(1)} collective-permute-done((f32[112,128]{1,0:T(8,128)S(1)}, f32[112,128]{1,0:T(8,128)S(1)}, u32[]{:S(2)}, u32[]{:S(2)}) %collective-permute-start.9) | collective-permute-done | bytes 57376 | tf_op jit(solution)/shard_map/ppermute | solution.py:379
  32.6 1.9 %collective-permute-done.8 = f32[112,128]{1,0:T(8,128)S(1)} collective-permute-done((f32[112,128]{1,0:T(8,128)S(1)}, f32[112,128]{1,0:T(8,128)S(1)}, u32[]{:S(2)}, u32[]{:S(2)}) %collective-permute-start.8) | collective-permute-done | bytes 57376 | tf_op jit(solution)/shard_map/ppermute | solution.py:379
  34.5 0.6 collective-permute-done.7
  35.2 0.0 copy-start.1
  35.2 1.5 %collective-permute-start.10 = (f32[160,128]{1,0:T(8,128)S(1)}, f32[160,128]{1,0:T(8,128)S(1)}, u32[]{:S(2)}, u32[]{:S(2)}) collective-permute-start(f32[160,128]{1,0:T(8,128)S(1)} %get-tuple-element.21.refs_0_), channel_id=1, source_target_pairs={{0,1},{1,0},{2,3},{3,2},{4,5},{5,4},{6,7},{7,6},{8,9},{9,8},{10,11... | collective-permute-start | bytes 245768 | tf_op jit(solution)/shard_map/ppermute | solution.py:379
  36.7 1.0 %collective-permute-start.12 = (f32[160,128]{1,0:T(8,128)S(1)}, f32[160,128]{1,0:T(8,128)S(1)}, u32[]{:S(2)}, u32[]{:S(2)}) collective-permute-start(f32[160,128]{1,0:T(8,128)S(1)} %get-tuple-element.21.refs_0_), channel_id=1, source_target_pairs={{0,5},{1,4},{2,7},{3,6},{4,1},{5,0},{6,3},{7,2},{8,13},{9,12},{10,... | collective-permute-start | bytes 245768 | tf_op jit(solution)/shard_map/ppermute | solution.py:379
  37.7 1.1 %collective-permute-start.11 = (f32[160,128]{1,0:T(8,128)S(1)}, f32[160,128]{1,0:T(8,128)S(1)}, u32[]{:S(2)}, u32[]{:S(2)}) collective-permute-start(f32[160,128]{1,0:T(8,128)S(1)} %get-tuple-element.21.refs_0_), channel_id=1, source_target_pairs={{0,4},{1,5},{2,6},{3,7},{4,0},{5,1},{6,2},{7,3},{8,12},{9,13},{10,... | collective-permute-start | bytes 245768 | tf_op jit(solution)/shard_map/ppermute | solution.py:379
  38.8 1.0 %collective-permute-done.10.refs_1_ = f32[160,128]{1,0:T(8,128)S(1)} collective-permute-done((f32[160,128]{1,0:T(8,128)S(1)}, f32[160,128]{1,0:T(8,128)S(1)}, u32[]{:S(2)}, u32[]{:S(2)}) %collective-permute-start.10) | collective-permute-done | bytes 81952 | tf_op jit(solution)/shard_map/ppermute | solution.py:379
  39.7 2.4 %collective-permute-done.11.refs_2_ = f32[160,128]{1,0:T(8,128)S(1)} collective-permute-done((f32[160,128]{1,0:T(8,128)S(1)}, f32[160,128]{1,0:T(8,128)S(1)}, u32[]{:S(2)}, u32[]{:S(2)}) %collective-permute-start.11) | collective-permute-done | bytes 81952 | tf_op jit(solution)/shard_map/ppermute | solution.py:379
  42.1 0.0 collective-permute-done.12.refs_3_
  42.2 0.1 collective-permute-start.13
  42.2 1.6 %collective-permute-done.13.refs_4_ = f32[640,128]{1,0:T(8,128)S(1)} collective-permute-done((f32[640,128]{1,0:T(8,128)S(1)}, f32[640,128]{1,0:T(8,128)S(1)}, u32[]{:S(2)}, u32[]{:S(2)}) %collective-permute-start.13) | collective-permute-done | bytes 327712 | tf_op jit(solution)/shard_map/ppermute | solution.py:379
  43.9 0.0 copy-done.1
  43.9 16.6 %factor.1 = (f32[512,512]{1,0:T(8,128)}, f32[512,128]{1,0:T(8,128)}, bf16[128,512]{1,0:T(8,128)(2,1)}) custom-call(f32[160,128]{1,0:T(8,128)S(1)} %get-tuple-element.21.refs_0_, f32[160,128]{1,0:T(8,128)S(1)} %collective-permute-done.10.refs_1_, f32[160,128]{1,0:T(8,128)S(1)} %collective-permute-done.11.refs_2_, ...), custom_call_target="tpu_custom_call" | custom-call | tf_op jit(solution)/shard_map/factor/pallas_call | solution.py:345
  (12 shorter events, 0.1 us)
Async XLA Ops:
  0.6 5.9 %copy-start.2 = (s32[1,1,4]{2,1,0:T(1,128)S(1)}, s32[1,1,4]{2,1,0:T(1,128)}, u32[]{:S(2)}) copy-start(s32[1,1,4]{2,1,0:T(1,128)} %owner_ref.3) | copy-start | bytes 52
  0.6 5.8 %copy-start = (bf16[128,2048]{1,0:T(8,128)(2,1)S(1)}, bf16[128,2048]{1,0:T(8,128)(2,1)}, u32[]{:S(2)}) copy-start(bf16[128,2048]{1,0:T(8,128)(2,1)} %refs_0_) | copy-start | bytes 1572868
  2.4 12.2 %collective-permute-start.1 = (bf16[128,512]{1,0:T(8,128)(2,1)}, bf16[128,512]{1,0:T(8,128)(2,1)S(1)}, u32[]{:S(2)}, u32[]{:S(2)}) collective-permute-start(bf16[128,512]{1,0:T(8,128)(2,1)} %pick_blocks.2), channel_id=1, source_target_pairs={{0,16},{8,24},{16,0},{24,8},{1,17},{9,25},{17,1},{25,9},{2,18},{10... | collective-permute-start | bytes 393224 | tf_op jit(solution)/shard_map/ppermute | solution.py:379
  7.1 7.6 %collective-permute-start = (bf16[128,512]{1,0:T(8,128)(2,1)S(1)}, bf16[128,512]{1,0:T(8,128)(2,1)S(1)}, u32[]{:S(2)}, u32[]{:S(2)}) collective-permute-start(bf16[128,512]{1,0:T(8,128)(2,1)S(1)} %get-tuple-element.11), channel_id=1, source_target_pairs={{0,8},{8,0},{16,24},{24,16},{1,9},{9,1},{17,25},{25,17},{2,10},{10... | collective-permute-start | bytes 393224 | tf_op jit(solution)/shard_map/ppermute | solution.py:379
  8.7 8.3 %collective-permute-start.2 = (bf16[128,512]{1,0:T(8,128)(2,1)S(1)}, bf16[128,512]{1,0:T(8,128)(2,1)S(1)}, u32[]{:S(2)}, u32[]{:S(2)}) collective-permute-start(bf16[128,512]{1,0:T(8,128)(2,1)S(1)} %get-tuple-element.12), channel_id=1, source_target_pairs={{0,24},{8,16},{16,8},{24,0},{1,25},{9,17},{17,9},{25,1},{2,26},{10... | collective-permute-start | bytes 393224 | tf_op jit(solution)/shard_map/ppermute | solution.py:379
  17.6 1.6 %collective-permute-start.3 = (f32[448,128]{1,0:T(8,128)S(1)}, f32[448,128]{1,0:T(8,128)S(1)}, u32[]{:S(2)}, u32[]{:S(2)}) collective-permute-start(f32[448,128]{1,0:T(8,128)S(1)} %get-tuple-element.14), channel_id=1, source_target_pairs={{0,2},{2,0},{4,6},{6,4},{1,3},{3,1},{5,7},{7,5},{8,10},{10,8},{12,... | collective-permute-start | bytes 688136 | tf_op jit(solution)/shard_map/ppermute | solution.py:379
  19.2 4.2 %collective-permute-start.4 = (f32[112,128]{1,0:T(8,128)S(1)}, f32[112,128]{1,0:T(8,128)S(1)}, u32[]{:S(2)}, u32[]{:S(2)}) collective-permute-start(f32[112,128]{1,0:T(8,128)S(1)} %get-tuple-element.17), channel_id=1, source_target_pairs={{0,1},{1,0},{2,3},{3,2},{4,5},{5,4},{6,7},{7,6},{8,9},{9,8},{10,11... | collective-permute-start | bytes 172040 | tf_op jit(solution)/shard_map/ppermute | solution.py:379
  20.8 5.6 %collective-permute-start.6 = (f32[112,128]{1,0:T(8,128)S(1)}, f32[112,128]{1,0:T(8,128)S(1)}, u32[]{:S(2)}, u32[]{:S(2)}) collective-permute-start(f32[112,128]{1,0:T(8,128)S(1)} %get-tuple-element.18), channel_id=1, source_target_pairs={{0,5},{1,4},{2,7},{3,6},{4,1},{5,0},{6,3},{7,2},{8,13},{9,12},{10,... | collective-permute-start | bytes 172040 | tf_op jit(solution)/shard_map/ppermute | solution.py:379
  22.2 4.2 %collective-permute-start.5 = (f32[112,128]{1,0:T(8,128)S(1)}, f32[112,128]{1,0:T(8,128)S(1)}, u32[]{:S(2)}, u32[]{:S(2)}) collective-permute-start(f32[112,128]{1,0:T(8,128)S(1)} %get-tuple-element.19), channel_id=1, source_target_pairs={{0,4},{1,5},{2,6},{3,7},{4,0},{5,1},{6,2},{7,3},{8,12},{9,13},{10,... | collective-permute-start | bytes 172040 | tf_op jit(solution)/shard_map/ppermute | solution.py:379
  26.4 6.2 %collective-permute-start.9 = (f32[112,128]{1,0:T(8,128)S(1)}, f32[112,128]{1,0:T(8,128)S(1)}, u32[]{:S(2)}, u32[]{:S(2)}) collective-permute-start(f32[112,128]{1,0:T(8,128)S(1)} %fusion.1), channel_id=1, source_target_pairs={{0,24},{8,16},{16,8},{24,0},{1,25},{9,17},{17,9},{25,1},{2,26},{10... | collective-permute-start | bytes 172040 | tf_op jit(solution)/shard_map/ppermute | solution.py:379
  28.9 5.6 %collective-permute-start.8 = (f32[112,128]{1,0:T(8,128)S(1)}, f32[112,128]{1,0:T(8,128)S(1)}, u32[]{:S(2)}, u32[]{:S(2)}) collective-permute-start(f32[112,128]{1,0:T(8,128)S(1)} %fusion.1), channel_id=1, source_target_pairs={{0,16},{8,24},{16,0},{24,8},{1,17},{9,25},{17,1},{25,9},{2,18},{10... | collective-permute-start | bytes 172040 | tf_op jit(solution)/shard_map/ppermute | solution.py:379
  30.8 4.3 %collective-permute-start.7 = (f32[112,128]{1,0:T(8,128)S(1)}, f32[112,128]{1,0:T(8,128)S(1)}, u32[]{:S(2)}, u32[]{:S(2)}) collective-permute-start(f32[112,128]{1,0:T(8,128)S(1)} %fusion.1), channel_id=1, source_target_pairs={{0,8},{8,0},{16,24},{24,16},{1,9},{9,1},{17,25},{25,17},{2,10},{10... | collective-permute-start | bytes 172040 | tf_op jit(solution)/shard_map/ppermute | solution.py:379
  35.2 8.7 %copy-start.1 = (f32[512,128]{1,0:T(8,128)S(1)}, f32[512,128]{1,0:T(8,128)}, u32[]{:S(2)}) copy-start(f32[512,128]{1,0:T(8,128)} %refs_5_.1) | copy-start | bytes 786436
  35.2 4.5 %collective-permute-start.10 = (f32[160,128]{1,0:T(8,128)S(1)}, f32[160,128]{1,0:T(8,128)S(1)}, u32[]{:S(2)}, u32[]{:S(2)}) collective-permute-start(f32[160,128]{1,0:T(8,128)S(1)} %get-tuple-element.21.refs_0_), channel_id=1, source_target_pairs={{0,1},{1,0},{2,3},{3,2},{4,5},{5,4},{6,7},{7,6},{8,9},{9,8},{10,11... | collective-permute-start | bytes 245768 | tf_op jit(solution)/shard_map/ppermute | solution.py:379
  36.7 5.5 %collective-permute-start.12 = (f32[160,128]{1,0:T(8,128)S(1)}, f32[160,128]{1,0:T(8,128)S(1)}, u32[]{:S(2)}, u32[]{:S(2)}) collective-permute-start(f32[160,128]{1,0:T(8,128)S(1)} %get-tuple-element.21.refs_0_), channel_id=1, source_target_pairs={{0,5},{1,4},{2,7},{3,6},{4,1},{5,0},{6,3},{7,2},{8,13},{9,12},{10,... | collective-permute-start | bytes 245768 | tf_op jit(solution)/shard_map/ppermute | solution.py:379
  37.7 4.4 %collective-permute-start.11 = (f32[160,128]{1,0:T(8,128)S(1)}, f32[160,128]{1,0:T(8,128)S(1)}, u32[]{:S(2)}, u32[]{:S(2)}) collective-permute-start(f32[160,128]{1,0:T(8,128)S(1)} %get-tuple-element.21.refs_0_), channel_id=1, source_target_pairs={{0,4},{1,5},{2,6},{3,7},{4,0},{5,1},{6,2},{7,3},{8,12},{9,13},{10,... | collective-permute-start | bytes 245768 | tf_op jit(solution)/shard_map/ppermute | solution.py:379
  42.2 1.7 %collective-permute-start.13 = (f32[640,128]{1,0:T(8,128)S(1)}, f32[640,128]{1,0:T(8,128)S(1)}, u32[]{:S(2)}, u32[]{:S(2)}) collective-permute-start(f32[640,128]{1,0:T(8,128)S(1)} %constant_dynamic-update-slice_fusion.5), channel_id=1, source_target_pairs={{0,2},{2,0},{4,6},{6,4},{1,3},{3,1},{5,7},{7,5},{8,10},{10,8},{12,... | collective-permute-start | bytes 983048 | tf_op jit(solution)/shard_map/ppermute | solution.py:379

commit v10 on v9

--- a/solution.py
+++ b/solution.py
@@ -280,6 +280,11 @@
     upper = lax.broadcasted_iota(jnp.int32, (n, n), 0) <= lax.broadcasted_iota(jnp.int32, (n, n), 1)
     whole = (high, middle, lower)
     value = basis_ref[...]
+
+    def finish(basis):
+        out_ref[...] = basis
+        core_ref[...] = dot(basis.astype(jnp.bfloat16), columns[...], TN).astype(jnp.bfloat16)
+
     doubtful = jnp.zeros((1, 1), jnp.float32)
     for phase in range(max(phases, ITERS + 1)):
         if phase < phases:
@@ -316,7 +321,8 @@
             value = short_dot(wide, split3(two[:, n:]), NT)
             if phase == 0:
                 first[...] = value
-    out_ref[...] = value
+            if phase == ITERS:
+                finish(value)
 
     @pl.when(doubtful[0, 0] > 0.0)
     def _():
@@ -333,9 +339,7 @@
 
             lax.fori_loop(0, n // GROUP, step, 0)
             value = short_dot(wide, split3(two[:, n:]), NT)
-        out_ref[...] = value
-
-    core_ref[...] = dot(out_ref[...].astype(jnp.bfloat16), columns[...], TN).astype(jnp.bfloat16)
+        finish(value)
 
 
 def factor(slots, other, basis, pieces):

time: 60.6 us -> 60.5 us (level)
  no operation moved by 1% of the time
where the time goes in v10:
time: 60.5 us; the launch traced here: 60.3 us
  waiting for transfers between devices  22.2 us (37%)
  Pallas kernels  19.4 us (32%)
  starting transfers between devices  17.8 us (29%)
  between operations  0.76 us (1%)
    ppermute x14, waiting for transfers between devices, swap(): return lax.ppermute(value, axes, pairs)  22.2 us
    ppermute x14, starting transfers between devices, swap(): return lax.ppermute(value, axes, pairs)  17.8 us
    pallas_call x1, Pallas kernels, factor(): pl.pallas_call(functools.partial(factor_kernel, chunks, len(pieces)), out...  16.5 us
    pallas_call x2, Pallas kernels, pick_blocks(): pl.pallas_call(functools.partial(pick_kernel, distances), out_shape=(piec...  2.37 us
  transfers between devices with their start and end apart: 14, of which 11 were waited for; matrix products, arithmetic and copies ran while one was open for 0% of the time, Pallas kernels for 1%

profile of v10, /device:TPU:0, one launch (start us, length us, event | category | flops | bytes accessed | tf_op | source)
XLA Modules:
  0.0 60.3 jit_solution(7074421718593244776)
XLA Ops:
  0.6 0.0 copy-start.2
  0.6 0.0 copy-start
  0.6 1.8 %pick_blocks.2 = bf16[128,512]{1,0:T(8,128)(2,1)} custom-call(s32[1,1,4]{2,1,0:T(1,128)} %owner_ref.3, bf16[128,2048]{1,0:T(8,128)(2,1)} %refs_0_), custom_call_target="tpu_custom_call" | custom-call | tf_op jit(solution)/shard_map/pick_blocks/pallas_call | solution.py:178
  2.4 4.0 %collective-permute-start.1 = (bf16[128,512]{1,0:T(8,128)(2,1)}, bf16[128,512]{1,0:T(8,128)(2,1)S(1)}, u32[]{:S(2)}, u32[]{:S(2)}) collective-permute-start(bf16[128,512]{1,0:T(8,128)(2,1)} %pick_blocks.2), channel_id=1, source_target_pairs={{0,16},{8,24},{16,0},{24,8},{1,17},{9,25},{17,1},{25,9},{2,18},{10... | collective-permute-start | bytes 393224 | tf_op jit(solution)/shard_map/ppermute | solution.py:383
  6.5 0.0 copy-done.2
  6.5 0.0 copy-done
  6.5 0.6 pick_blocks.3
  7.1 1.6 %collective-permute-start = (bf16[128,512]{1,0:T(8,128)(2,1)S(1)}, bf16[128,512]{1,0:T(8,128)(2,1)S(1)}, u32[]{:S(2)}, u32[]{:S(2)}) collective-permute-start(bf16[128,512]{1,0:T(8,128)(2,1)S(1)} %get-tuple-element.11), channel_id=1, source_target_pairs={{0,8},{8,0},{16,24},{24,16},{1,9},{9,1},{17,25},{25,17},{2,10},{10... | collective-permute-start | bytes 393224 | tf_op jit(solution)/shard_map/ppermute | solution.py:383
  8.7 0.0 collective-permute-start.2
  8.7 5.9 %collective-permute-done.1.refs_3_.refs_8_ = bf16[128,512]{1,0:T(8,128)(2,1)S(1)} collective-permute-done((bf16[128,512]{1,0:T(8,128)(2,1)}, bf16[128,512]{1,0:T(8,128)(2,1)S(1)}, u32[]{:S(2)}, u32[]{:S(2)}) %collective-permute-start.1) | collective-permute-done | bytes 131104 | tf_op jit(solution)/shard_map/ppermute | solution.py:383
  14.6 0.0 collective-permute-done.refs_2_.refs_7_
  14.6 2.4 %collective-permute-done.2.refs_4_.refs_9_ = bf16[128,512]{1,0:T(8,128)(2,1)S(1)} collective-permute-done((bf16[128,512]{1,0:T(8,128)(2,1)S(1)}, bf16[128,512]{1,0:T(8,128)(2,1)S(1)}, u32[]{:S(2)}, u32[]{:S(2)}) %collective-permute-start.2) | collective-permute-done | bytes 131104 | tf_op jit(solution)/shard_map/ppermute | solution.py:383
  17.0 0.6 local_gram.1
  17.6 0.1 collective-permute-start.3
  17.7 1.5 %collective-permute-done.3 = f32[448,128]{1,0:T(8,128)S(1)} collective-permute-done((f32[448,128]{1,0:T(8,128)S(1)}, f32[448,128]{1,0:T(8,128)S(1)}, u32[]{:S(2)}, u32[]{:S(2)}) %collective-permute-start.3) | collective-permute-done | bytes 229408 | tf_op jit(solution)/shard_map/ppermute | solution.py:383
  19.2 1.6 %collective-permute-start.4 = (f32[112,128]{1,0:T(8,128)S(1)}, f32[112,128]{1,0:T(8,128)S(1)}, u32[]{:S(2)}, u32[]{:S(2)}) collective-permute-start(f32[112,128]{1,0:T(8,128)S(1)} %get-tuple-element.17), channel_id=1, source_target_pairs={{0,1},{1,0},{2,3},{3,2},{4,5},{5,4},{6,7},{7,6},{8,9},{9,8},{10,11... | collective-permute-start | bytes 172040 | tf_op jit(solution)/shard_map/ppermute | solution.py:383
  20.8 1.4 %collective-permute-start.6 = (f32[112,128]{1,0:T(8,128)S(1)}, f32[112,128]{1,0:T(8,128)S(1)}, u32[]{:S(2)}, u32[]{:S(2)}) collective-permute-start(f32[112,128]{1,0:T(8,128)S(1)} %get-tuple-element.18), channel_id=1, source_target_pairs={{0,5},{1,4},{2,7},{3,6},{4,1},{5,0},{6,3},{7,2},{8,13},{9,12},{10,... | collective-permute-start | bytes 172040 | tf_op jit(solution)/shard_map/ppermute | solution.py:383
  22.2 0.5 collective-permute-start.5
  22.8 0.7 %collective-permute-done.4 = f32[112,128]{1,0:T(8,128)S(1)} collective-permute-done((f32[112,128]{1,0:T(8,128)S(1)}, f32[112,128]{1,0:T(8,128)S(1)}, u32[]{:S(2)}, u32[]{:S(2)}) %collective-permute-start.4) | collective-permute-done | bytes 57376 | tf_op jit(solution)/shard_map/ppermute | solution.py:383
  23.5 2.9 %collective-permute-done.6 = f32[112,128]{1,0:T(8,128)S(1)} collective-permute-done((f32[112,128]{1,0:T(8,128)S(1)}, f32[112,128]{1,0:T(8,128)S(1)}, u32[]{:S(2)}, u32[]{:S(2)}) %collective-permute-start.6) | collective-permute-done | bytes 57376 | tf_op jit(solution)/shard_map/ppermute | solution.py:383
  26.4 0.0 collective-permute-done.5
  26.4 2.5 %collective-permute-start.9 = (f32[112,128]{1,0:T(8,128)S(1)}, f32[112,128]{1,0:T(8,128)S(1)}, u32[]{:S(2)}, u32[]{:S(2)}) collective-permute-start(f32[112,128]{1,0:T(8,128)S(1)} %fusion.1), channel_id=1, source_target_pairs={{0,24},{8,16},{16,8},{24,0},{1,25},{9,17},{17,9},{25,1},{2,26},{10... | collective-permute-start | bytes 172040 | tf_op jit(solution)/shard_map/ppermute | solution.py:383
  28.9 1.9 %collective-permute-start.8 = (f32[112,128]{1,0:T(8,128)S(1)}, f32[112,128]{1,0:T(8,128)S(1)}, u32[]{:S(2)}, u32[]{:S(2)}) collective-permute-start(f32[112,128]{1,0:T(8,128)S(1)} %fusion.1), channel_id=1, source_target_pairs={{0,16},{8,24},{16,0},{24,8},{1,17},{9,25},{17,1},{25,9},{2,18},{10... | collective-permute-start | bytes 172040 | tf_op jit(solution)/shard_map/ppermute | solution.py:383
  30.8 0.5 collective-permute-start.7
  31.3 1.3 %collective-permute-done.9 = f32[112,128]{1,0:T(8,128)S(1)} collective-permute-done((f32[112,128]{1,0:T(8,128)S(1)}, f32[112,128]{1,0:T(8,128)S(1)}, u32[]{:S(2)}, u32[]{:S(2)}) %collective-permute-start.9) | collective-permute-done | bytes 57376 | tf_op jit(solution)/shard_map/ppermute | solution.py:383
  32.6 1.9 %collective-permute-done.8 = f32[112,128]{1,0:T(8,128)S(1)} collective-permute-done((f32[112,128]{1,0:T(8,128)S(1)}, f32[112,128]{1,0:T(8,128)S(1)}, u32[]{:S(2)}, u32[]{:S(2)}) %collective-permute-start.8) | collective-permute-done | bytes 57376 | tf_op jit(solution)/shard_map/ppermute | solution.py:383
  34.5 0.6 collective-permute-done.7
  35.2 0.0 copy-start.1
  35.2 1.5 %collective-permute-start.10 = (f32[160,128]{1,0:T(8,128)S(1)}, f32[160,128]{1,0:T(8,128)S(1)}, u32[]{:S(2)}, u32[]{:S(2)}) collective-permute-start(f32[160,128]{1,0:T(8,128)S(1)} %get-tuple-element.21.refs_0_), channel_id=1, source_target_pairs={{0,1},{1,0},{2,3},{3,2},{4,5},{5,4},{6,7},{7,6},{8,9},{9,8},{10,11... | collective-permute-start | bytes 245768 | tf_op jit(solution)/shard_map/ppermute | solution.py:383
  36.7 1.0 %collective-permute-start.12 = (f32[160,128]{1,0:T(8,128)S(1)}, f32[160,128]{1,0:T(8,128)S(1)}, u32[]{:S(2)}, u32[]{:S(2)}) collective-permute-start(f32[160,128]{1,0:T(8,128)S(1)} %get-tuple-element.21.refs_0_), channel_id=1, source_target_pairs={{0,5},{1,4},{2,7},{3,6},{4,1},{5,0},{6,3},{7,2},{8,13},{9,12},{10,... | collective-permute-start | bytes 245768 | tf_op jit(solution)/shard_map/ppermute | solution.py:383
  37.7 1.1 %collective-permute-start.11 = (f32[160,128]{1,0:T(8,128)S(1)}, f32[160,128]{1,0:T(8,128)S(1)}, u32[]{:S(2)}, u32[]{:S(2)}) collective-permute-start(f32[160,128]{1,0:T(8,128)S(1)} %get-tuple-element.21.refs_0_), channel_id=1, source_target_pairs={{0,4},{1,5},{2,6},{3,7},{4,0},{5,1},{6,2},{7,3},{8,12},{9,13},{10,... | collective-permute-start | bytes 245768 | tf_op jit(solution)/shard_map/ppermute | solution.py:383
  38.8 1.0 %collective-permute-done.10.refs_1_ = f32[160,128]{1,0:T(8,128)S(1)} collective-permute-done((f32[160,128]{1,0:T(8,128)S(1)}, f32[160,128]{1,0:T(8,128)S(1)}, u32[]{:S(2)}, u32[]{:S(2)}) %collective-permute-start.10) | collective-permute-done | bytes 81952 | tf_op jit(solution)/shard_map/ppermute | solution.py:383
  39.7 2.4 %collective-permute-done.11.refs_2_ = f32[160,128]{1,0:T(8,128)S(1)} collective-permute-done((f32[160,128]{1,0:T(8,128)S(1)}, f32[160,128]{1,0:T(8,128)S(1)}, u32[]{:S(2)}, u32[]{:S(2)}) %collective-permute-start.11) | collective-permute-done | bytes 81952 | tf_op jit(solution)/shard_map/ppermute | solution.py:383
  42.1 0.0 collective-permute-done.12.refs_3_
  42.2 0.1 collective-permute-start.13
  42.2 1.6 %collective-permute-done.13.refs_4_ = f32[640,128]{1,0:T(8,128)S(1)} collective-permute-done((f32[640,128]{1,0:T(8,128)S(1)}, f32[640,128]{1,0:T(8,128)S(1)}, u32[]{:S(2)}, u32[]{:S(2)}) %collective-permute-start.13) | collective-permute-done | bytes 327712 | tf_op jit(solution)/shard_map/ppermute | solution.py:383
  43.9 0.0 copy-done.1
  43.9 16.5 %factor.1 = (f32[512,512]{1,0:T(8,128)}, f32[512,128]{1,0:T(8,128)}, bf16[128,512]{1,0:T(8,128)(2,1)}) custom-call(f32[160,128]{1,0:T(8,128)S(1)} %get-tuple-element.21.refs_0_, f32[160,128]{1,0:T(8,128)S(1)} %collective-permute-done.10.refs_1_, f32[160,128]{1,0:T(8,128)S(1)} %collective-permute-done.11.refs_2_, ...), custom_call_target="tpu_custom_call" | custom-call | tf_op jit(solution)/shard_map/factor/pallas_call | solution.py:349
  (12 shorter events, 0.1 us)
Async XLA Ops:
  0.6 5.9 %copy-start.2 = (s32[1,1,4]{2,1,0:T(1,128)S(1)}, s32[1,1,4]{2,1,0:T(1,128)}, u32[]{:S(2)}) copy-start(s32[1,1,4]{2,1,0:T(1,128)} %owner_ref.3) | copy-start | bytes 52
  0.6 5.8 %copy-start = (bf16[128,2048]{1,0:T(8,128)(2,1)S(1)}, bf16[128,2048]{1,0:T(8,128)(2,1)}, u32[]{:S(2)}) copy-start(bf16[128,2048]{1,0:T(8,128)(2,1)} %refs_0_) | copy-start | bytes 1572868
  2.4 12.2 %collective-permute-start.1 = (bf16[128,512]{1,0:T(8,128)(2,1)}, bf16[128,512]{1,0:T(8,128)(2,1)S(1)}, u32[]{:S(2)}, u32[]{:S(2)}) collective-permute-start(bf16[128,512]{1,0:T(8,128)(2,1)} %pick_blocks.2), channel_id=1, source_target_pairs={{0,16},{8,24},{16,0},{24,8},{1,17},{9,25},{17,1},{25,9},{2,18},{10... | collective-permute-start | bytes 393224 | tf_op jit(solution)/shard_map/ppermute | solution.py:383
  7.1 7.6 %collective-permute-start = (bf16[128,512]{1,0:T(8,128)(2,1)S(1)}, bf16[128,512]{1,0:T(8,128)(2,1)S(1)}, u32[]{:S(2)}, u32[]{:S(2)}) collective-permute-start(bf16[128,512]{1,0:T(8,128)(2,1)S(1)} %get-tuple-element.11), channel_id=1, source_target_pairs={{0,8},{8,0},{16,24},{24,16},{1,9},{9,1},{17,25},{25,17},{2,10},{10... | collective-permute-start | bytes 393224 | tf_op jit(solution)/shard_map/ppermute | solution.py:383
  8.7 8.3 %collective-permute-start.2 = (bf16[128,512]{1,0:T(8,128)(2,1)S(1)}, bf16[128,512]{1,0:T(8,128)(2,1)S(1)}, u32[]{:S(2)}, u32[]{:S(2)}) collective-permute-start(bf16[128,512]{1,0:T(8,128)(2,1)S(1)} %get-tuple-element.12), channel_id=1, source_target_pairs={{0,24},{8,16},{16,8},{24,0},{1,25},{9,17},{17,9},{25,1},{2,26},{10... | collective-permute-start | bytes 393224 | tf_op jit(solution)/shard_map/ppermute | solution.py:383
  17.6 1.6 %collective-permute-start.3 = (f32[448,128]{1,0:T(8,128)S(1)}, f32[448,128]{1,0:T(8,128)S(1)}, u32[]{:S(2)}, u32[]{:S(2)}) collective-permute-start(f32[448,128]{1,0:T(8,128)S(1)} %get-tuple-element.14), channel_id=1, source_target_pairs={{0,2},{2,0},{4,6},{6,4},{1,3},{3,1},{5,7},{7,5},{8,10},{10,8},{12,... | collective-permute-start | bytes 688136 | tf_op jit(solution)/shard_map/ppermute | solution.py:383
  19.2 4.2 %collective-permute-start.4 = (f32[112,128]{1,0:T(8,128)S(1)}, f32[112,128]{1,0:T(8,128)S(1)}, u32[]{:S(2)}, u32[]{:S(2)}) collective-permute-start(f32[112,128]{1,0:T(8,128)S(1)} %get-tuple-element.17), channel_id=1, source_target_pairs={{0,1},{1,0},{2,3},{3,2},{4,5},{5,4},{6,7},{7,6},{8,9},{9,8},{10,11... | collective-permute-start | bytes 172040 | tf_op jit(solution)/shard_map/ppermute | solution.py:383
  20.8 5.6 %collective-permute-start.6 = (f32[112,128]{1,0:T(8,128)S(1)}, f32[112,128]{1,0:T(8,128)S(1)}, u32[]{:S(2)}, u32[]{:S(2)}) collective-permute-start(f32[112,128]{1,0:T(8,128)S(1)} %get-tuple-element.18), channel_id=1, source_target_pairs={{0,5},{1,4},{2,7},{3,6},{4,1},{5,0},{6,3},{7,2},{8,13},{9,12},{10,... | collective-permute-start | bytes 172040 | tf_op jit(solution)/shard_map/ppermute | solution.py:383
  22.2 4.2 %collective-permute-start.5 = (f32[112,128]{1,0:T(8,128)S(1)}, f32[112,128]{1,0:T(8,128)S(1)}, u32[]{:S(2)}, u32[]{:S(2)}) collective-permute-start(f32[112,128]{1,0:T(8,128)S(1)} %get-tuple-element.19), channel_id=1, source_target_pairs={{0,4},{1,5},{2,6},{3,7},{4,0},{5,1},{6,2},{7,3},{8,12},{9,13},{10,... | collective-permute-start | bytes 172040 | tf_op jit(solution)/shard_map/ppermute | solution.py:383
  26.4 6.2 %collective-permute-start.9 = (f32[112,128]{1,0:T(8,128)S(1)}, f32[112,128]{1,0:T(8,128)S(1)}, u32[]{:S(2)}, u32[]{:S(2)}) collective-permute-start(f32[112,128]{1,0:T(8,128)S(1)} %fusion.1), channel_id=1, source_target_pairs={{0,24},{8,16},{16,8},{24,0},{1,25},{9,17},{17,9},{25,1},{2,26},{10... | collective-permute-start | bytes 172040 | tf_op jit(solution)/shard_map/ppermute | solution.py:383
  28.9 5.6 %collective-permute-start.8 = (f32[112,128]{1,0:T(8,128)S(1)}, f32[112,128]{1,0:T(8,128)S(1)}, u32[]{:S(2)}, u32[]{:S(2)}) collective-permute-start(f32[112,128]{1,0:T(8,128)S(1)} %fusion.1), channel_id=1, source_target_pairs={{0,16},{8,24},{16,0},{24,8},{1,17},{9,25},{17,1},{25,9},{2,18},{10... | collective-permute-start | bytes 172040 | tf_op jit(solution)/shard_map/ppermute | solution.py:383
  30.8 4.3 %collective-permute-start.7 = (f32[112,128]{1,0:T(8,128)S(1)}, f32[112,128]{1,0:T(8,128)S(1)}, u32[]{:S(2)}, u32[]{:S(2)}) collective-permute-start(f32[112,128]{1,0:T(8,128)S(1)} %fusion.1), channel_id=1, source_target_pairs={{0,8},{8,0},{16,24},{24,16},{1,9},{9,1},{17,25},{25,17},{2,10},{10... | collective-permute-start | bytes 172040 | tf_op jit(solution)/shard_map/ppermute | solution.py:383
  35.2 8.7 %copy-start.1 = (f32[512,128]{1,0:T(8,128)S(1)}, f32[512,128]{1,0:T(8,128)}, u32[]{:S(2)}) copy-start(f32[512,128]{1,0:T(8,128)} %refs_5_.1) | copy-start | bytes 786436
  35.2 4.5 %collective-permute-start.10 = (f32[160,128]{1,0:T(8,128)S(1)}, f32[160,128]{1,0:T(8,128)S(1)}, u32[]{:S(2)}, u32[]{:S(2)}) collective-permute-start(f32[160,128]{1,0:T(8,128)S(1)} %get-tuple-element.21.refs_0_), channel_id=1, source_target_pairs={{0,1},{1,0},{2,3},{3,2},{4,5},{5,4},{6,7},{7,6},{8,9},{9,8},{10,11... | collective-permute-start | bytes 245768 | tf_op jit(solution)/shard_map/ppermute | solution.py:383
  36.7 5.5 %collective-permute-start.12 = (f32[160,128]{1,0:T(8,128)S(1)}, f32[160,128]{1,0:T(8,128)S(1)}, u32[]{:S(2)}, u32[]{:S(2)}) collective-permute-start(f32[160,128]{1,0:T(8,128)S(1)} %get-tuple-element.21.refs_0_), channel_id=1, source_target_pairs={{0,5},{1,4},{2,7},{3,6},{4,1},{5,0},{6,3},{7,2},{8,13},{9,12},{10,... | collective-permute-start | bytes 245768 | tf_op jit(solution)/shard_map/ppermute | solution.py:383
  37.7 4.4 %collective-permute-start.11 = (f32[160,128]{1,0:T(8,128)S(1)}, f32[160,128]{1,0:T(8,128)S(1)}, u32[]{:S(2)}, u32[]{:S(2)}) collective-permute-start(f32[160,128]{1,0:T(8,128)S(1)} %get-tuple-element.21.refs_0_), channel_id=1, source_target_pairs={{0,4},{1,5},{2,6},{3,7},{4,0},{5,1},{6,2},{7,3},{8,12},{9,13},{10,... | collective-permute-start | bytes 245768 | tf_op jit(solution)/shard_map/ppermute | solution.py:383
  42.2 1.7 %collective-permute-start.13 = (f32[640,128]{1,0:T(8,128)S(1)}, f32[640,128]{1,0:T(8,128)S(1)}, u32[]{:S(2)}, u32[]{:S(2)}) collective-permute-start(f32[640,128]{1,0:T(8,128)S(1)} %constant_dynamic-update-slice_fusion.5), channel_id=1, source_target_pairs={{0,2},{2,0},{4,6},{6,4},{1,3},{3,1},{5,7},{7,5},{8,10},{10,8},{12,... | collective-permute-start | bytes 983048 | tf_op jit(solution)/shard_map/ppermute | solution.py:383
